TPU v7x, 32 devices: a whole 2x2x4 slice. The times are simulated.
32 devices in a mesh: grp: 2 (over y), kz: 4 (over z), coil: 2 (over x), kx: 2 (over core).
Axes of the slice: x: 2, y: 2, z: 4, core: 2. Of those that a mesh axis runs over, the one named last changes fastest.
Arguments:
- measured: float32 [2, 64, 32, 32, 32], P(None, ('grp', 'coil'), 'kx', 'kz'), parts along dimension 1, may hold values from -6 to 6
- mask: int32 [64, 32, 32], P(('grp', 'kx'), 'kz'), parts along dimension 0, may hold values 0 or 1
- kernel: float32 [27, 2, 32, 64], P(None, None, 'coil'), may hold values from -0.109375 to 0.109375
Outputs:
- restored: float32 [2, 64, 32, 32, 32], P(None, ('grp', 'coil'), 'kx', 'kz'), parts along dimension 1
There are 2 independent parts, one for each index of `grp`. A program takes and returns all parts, laid end to end along the dimension named above; an argument that names none is the same for every part. Nothing has to cross between parts.
All inputs are finite; a program needn't handle non-finite values. No bound on the sum of `mask` on one device may be relied on, other than what follows from the above.
Results may differ from a plain program's by a relative error of at most 0.0001.
Values sent between devices are 32-bit elements; how exact they have to be, the bound alone decides.
No kernel may reach another device: no remote copies, remote signals or barrier semaphores. Data moves between devices by JAX's collectives and lax.ppermute only.
A program may use at most 128 MiB of HBM per device.

v0:
```python
import jax
import jax.numpy as jnp
from jax import lax
from jax.sharding import PartitionSpec as P

ITERS = 2


def partner(array, axis, apart):
    return lax.ppermute(array, axis, [(i, i ^ 1 << apart) for i in range(lax.axis_size(axis))])


def padded_2(array, sides, width):
    for axis, dim in sides:
        peers, length = (lax.axis_size(axis), array.shape[dim])
        up = [(i, (i + 1) % peers) for i in range(peers - 1)]
        down = [(j, i) for i, j in up]
        last = lax.slice_in_dim(array, length - width, length, axis=dim)
        first = lax.slice_in_dim(array, 0, width, axis=dim)
        before = lax.ppermute(last, axis, up)
        after = lax.ppermute(first, axis, down)
        array = jnp.concatenate([before, array, after], axis=dim)
    return array


def build_weights(kernel_part):
    real_k = kernel_part[:, 0]
    imag_k = kernel_part[:, 1]
    return jnp.concatenate(
        [jnp.concatenate([real_k, -imag_k], 2), jnp.concatenate([imag_k, real_k], 2)], 1
    )


def convolve(padded, weights, rows, depth, width):
    padded = jnp.pad(padded, ((0, 0), (0, 0), (0, 0), (0, 0), (1, 1)))
    shape = padded.shape
    line = width + 2
    plane = (depth + 2) * line
    extra = 2 * line + 2
    flat = padded.reshape(shape[0] * shape[1], -1)
    flat = jnp.pad(flat, ((0, 0), (0, extra)))
    out_rows = weights.shape[1]
    length = rows * plane
    result = jnp.zeros((out_rows, length), jnp.float32)
    for first in range(3):
        window = flat[:, first * plane : first * plane + length + extra]
        group = weights[9 * first : 9 * first + 9].reshape(9 * out_rows, -1)
        products = jnp.dot(group, window, precision=lax.Precision.HIGHEST)
        products = products.reshape(9, out_rows, length + extra)
        for second in range(3):
            for third in range(3):
                offset = third * line + second
                result = result + products[3 * second + third, :, offset : offset + length]
    result = result.reshape(2, out_rows // 2, rows, depth + 2, line)
    return result[:, :, :, :depth, :width]


def on_device(measured, mask, kernel):
    sampled = (mask == 1)[None, None]
    state = jnp.where(sampled, measured, jnp.zeros_like(measured))
    weights = build_weights(kernel)
    sign = jnp.array([1.0, -1.0], jnp.float32).reshape(2, 1, 1, 1, 1)
    kz_bits = lax.axis_size("kz").bit_length() - 1
    rows = measured.shape[2]
    depth = measured.shape[3]
    width = measured.shape[4]
    for step in range(ITERS):
        mirrored = state
        for bit in range(kz_bits):
            mirrored = partner(mirrored, "kz", bit)
        bit = 0
        mirrored = partner(mirrored, "kx", bit)
        own_virtual = jnp.flip(mirrored, (2, 3, 4)) * sign
        physical, virtual = (
            lax.all_gather(state, "coil", axis=1, tiled=True),
            lax.all_gather(own_virtual, "coil", axis=1, tiled=True),
        )
        stacked = jnp.concatenate([physical, virtual], 1)
        padded = padded_2(stacked, (("kz", 3), ("kx", 2)), 1)
        result = convolve(padded, weights, rows, depth, width)
        state = jnp.where(sampled, measured, result)
    return state


def solution(mesh):
    placed = (
        P(None, ("grp", "coil"), "kx", "kz", None),
        P(("grp", "kx"), "kz", None),
        P(None, None, "coil", None),
    )
    return jax.shard_map(
        on_device,
        mesh=mesh,
        in_specs=placed,
        out_specs=P(None, ("grp", "coil"), "kx", "kz", None),
        check_vma=False,
    )
```

profile of v0, /device:TPU:9, one launch (start us, length us, event | category | flops | bytes accessed | tf_op | source)
XLA Modules:
  0.0 727.1 jit_solution(10788578500702772405)
XLA Ops:
  9.2 46.6 %collective-permute-done = f32[2,16,16,8,32]{4,3,2,1,0:T(8,128)} collective-permute-done((f32[2,16,16,8,32]{4,3,2,1,0:T(8,128)S(1)}, f32[2,16,16,8,32]{4,3,2,1,0:T(8,128)}, u32[]{:S(2)}, u32[]{:S(2)}) %collective-permute-start) | collective-permute-done | bytes 524320 | tf_op jit(solution)/shard_map/ppermute | solution.py:10
  58.2 90.4 %collective-permute-done.1 = f32[2,16,16,8,32]{4,3,2,1,0:T(8,128)} collective-permute-done((f32[2,16,16,8,32]{4,3,2,1,0:T(8,128)}, f32[2,16,16,8,32]{4,3,2,1,0:T(8,128)}, u32[]{:S(2)}, u32[]{:S(2)}) %collective-permute-start.1) | collective-permute-done | bytes 524320 | tf_op jit(solution)/shard_map/ppermute | solution.py:10
  149.1 4.1 collective-permute-done.2
  157.8 4.7 constant_dynamic-update-slice_fusion.1
  162.5 53.8 %all-gather.7.cloned.1.call-done = f32[2,32,16,8,32]{4,3,2,1,0:T(8,128)} async-done(((f32[2,16,16,8,32]{4,3,2,1,0:T(8,128)}), f32[2,32,16,8,32]{4,3,2,1,0:T(8,128)}) %all-gather.7.cloned.1.call-update) | async-done | bytes 1048592 | tf_op jit(solution)/shard_map/all_gather | solution.py:76
  216.3 4.7 constant_dynamic-update-slice_fusion
  221.0 8.2 %fusion.16 = (f32[2,64,16,1,32]{4,3,2,1,0:T(1,128)S(1)}, f32[2,64,16,1,32]{4,3,2,1,0:T(1,128)S(1)}) fusion(f32[2,64,16,8,32]{4,3,2,1,0:T(8,128)} %constant_dynamic-update-slice_fusion), kind=kLoop, calls=%fused_computation.85 | loop fusion | bytes 1048576 | tf_op jit(solution)/shard_map/slice | solution.py:18
  229.8 3.1 collective-permute-start.3
  235.7 7.8 %copy.17 = f32[2,64,16,8,32]{1,4,3,2,0:T(8,128)} copy(f32[2,64,16,8,32]{4,3,2,1,0:T(8,128)} %constant_dynamic-update-slice_fusion) | data formatting | bytes 4194304 | tf_op jit(solution)/shard_map/concatenate | solution.py:78
  244.4 3.4 collective-permute-done.4
  250.3 4.0 collective-permute-start.6
  256.0 8.4 %copy.25 = f32[2,64,18,10,32]{1,0,4,3,2:T(2,128)} copy(f32[2,64,18,10,32]{1,4,3,2,0:T(8,128)S(1)} %pad_maximum_fusion) | data formatting | bytes 5898240
  264.4 7.4 %pad.14.clone = f32[2,64,18,10,34]{1,0,4,3,2:T(2,128)} pad(f32[2,64,18,10,32]{1,0,4,3,2:T(2,128)} %copy.25, f32[]{:T(128)} %constant.2.clone.1), padding=0_0x0_0x0_0x0_0x1_1 | pad | bytes 6082564 | tf_op jit(solution)/shard_map/jit(_pad)/pad | solution.py:35
  271.8 6.2 reshape.97
  278.1 6.2 fusion.8
  284.3 5.2 fusion.9
  289.5 7.3 %fusion.1 = f32[9,32,5510]{2,1,0:T(8,128)} fusion(f32[27,32,128]{2,1,0:T(8,128)S(1)} %copy-done.7, f32[128,6120]{0,1:T(8,128)S(1)} %reshape.97), kind=kOutput, calls=%fused_computation.7 | convolution fusion | flops 2437447680 | bytes 9923328 | tf_op jit(solution)/shard_map/dot_general | solution.py:48
  296.9 3.0 fusion.19
  299.8 3.3 reshape.121
  303.2 3.4 squeeze.162
  306.5 5.9 fusion.20
  312.4 4.3 squeeze.163
  316.7 4.2 squeeze.164
  320.9 4.6 squeeze.165
  325.5 4.3 squeeze.166
  329.8 3.3 squeeze.167
  333.1 3.3 squeeze.168
  336.4 3.3 squeeze.169
  339.6 3.2 squeeze.170
  342.9 3.4 squeeze.171
  346.2 11.6 %add_add_fusion.1 = f32[2,16,16,10,34]{4,3,2,1,0:T(8,128)} fusion(f32[2,16,16,10,34]{4,3,2,1,0:T(8,128)} %squeeze.165, f32[2,16,16,10,34]{4,3,2,1,0:T(8,128)} %squeeze.164, f32[2,16,16,10,34]{4,3,2,1,0:T(8,128)} %squeeze.163, f32[2,16,16,10,34]{4,3,2,1,0:T(8,128)} %reshape.121, f32[2,16,16,10,34]{4,3,2,1,0:T(8,128)} %squeeze.162), kind=kLoop, calls=%fused_computation.3 | loop fusion | flops 696320 | bytes 4177920 | tf_op jit(solution)/shard_map/add | solution.py:53
  357.9 7.8 %fusion.11 = f32[2,16,16,8,32]{4,3,2,1,0:T(8,128)} fusion(f32[2,16,16,8,32]{4,3,2,1,0:T(8,128)S(1)} %copy-done.2, f32[2,16,16,10,34]{4,3,2,1,0:T(8,128)} %squeeze.171, f32[2,16,16,10,34]{4,3,2,1,0:T(8,128)} %squeeze.170, f32[2,16,16,10,34]{4,3,2,1,0:T(8,128)} %squeeze.169, f32[2,16,16,10,34]{4,3,2,1,0:T(8,128)} %squeeze.168, ...), kind=kLoop, calls=%fused_computation.26 | loop fusion | flops 917504 | bytes 4722688 | tf_op jit(solution)/shard_map/jit(_where)/select_n | solution.py:81
  365.9 46.9 %collective-permute-done.7 = f32[2,16,16,8,32]{4,3,2,1,0:T(8,128)} collective-permute-done((f32[2,16,16,8,32]{4,3,2,1,0:T(8,128)}, f32[2,16,16,8,32]{4,3,2,1,0:T(8,128)}, u32[]{:S(2)}, u32[]{:S(2)}) %collective-permute-start.7) | collective-permute-done | bytes 524320 | tf_op jit(solution)/shard_map/ppermute | solution.py:10
  414.1 89.6 %collective-permute-done.8 = f32[2,16,16,8,32]{4,3,2,1,0:T(8,128)S(1)} collective-permute-done((f32[2,16,16,8,32]{4,3,2,1,0:T(8,128)}, f32[2,16,16,8,32]{4,3,2,1,0:T(8,128)S(1)}, u32[]{:S(2)}, u32[]{:S(2)}) %collective-permute-start.8) | collective-permute-done | bytes 524320 | tf_op jit(solution)/shard_map/ppermute | solution.py:10
  505.1 3.9 collective-permute-done.9
  513.6 4.7 constant_dynamic-update-slice_fusion.3
  518.3 52.8 %all-gather.11.cloned.1.call-done = f32[2,32,16,8,32]{4,3,2,1,0:T(8,128)} async-done(((f32[2,16,16,8,32]{4,3,2,1,0:T(8,128)}), f32[2,32,16,8,32]{4,3,2,1,0:T(8,128)}) %all-gather.11.cloned.1.call-update) | async-done | bytes 1048592 | tf_op jit(solution)/shard_map/all_gather | solution.py:76
  571.1 4.8 constant_dynamic-update-slice_fusion.2
  575.9 8.3 %fusion.15 = (f32[2,64,16,1,32]{4,3,2,1,0:T(1,128)S(1)}, f32[2,64,16,1,32]{4,3,2,1,0:T(1,128)S(1)}) fusion(f32[2,64,16,8,32]{4,3,2,1,0:T(8,128)} %constant_dynamic-update-slice_fusion.2), kind=kLoop, calls=%fused_computation.84 | loop fusion | bytes 1048576 | tf_op jit(solution)/shard_map/slice | solution.py:18
  584.8 3.1 collective-permute-start.10
  590.7 7.9 %copy.21 = f32[2,64,16,8,32]{1,4,3,2,0:T(8,128)} copy(f32[2,64,16,8,32]{4,3,2,1,0:T(8,128)} %constant_dynamic-update-slice_fusion.2) | data formatting | bytes 4194304 | tf_op jit(solution)/shard_map/concatenate | solution.py:78
  599.5 3.4 collective-permute-done.11
  605.3 3.8 collective-permute-start.13
  611.0 8.4 %copy.26 = f32[2,64,18,10,32]{1,0,4,3,2:T(2,128)} copy(f32[2,64,18,10,32]{1,4,3,2,0:T(8,128)S(1)} %pad_maximum_fusion.1) | data formatting | bytes 5898240
  619.4 7.4 %pad.16.clone = f32[2,64,18,10,34]{1,0,4,3,2:T(2,128)} pad(f32[2,64,18,10,32]{1,0,4,3,2:T(2,128)} %copy.26, f32[]{:T(128)} %constant.2.clone.1), padding=0_0x0_0x0_0x0_0x1_1 | pad | bytes 6082564 | tf_op jit(solution)/shard_map/jit(_pad)/pad | solution.py:35
  626.8 6.2 reshape.98
  633.1 6.2 fusion.6
  639.3 5.2 fusion.7
  644.5 7.3 %fusion.4 = f32[9,32,5510]{2,1,0:T(8,128)} fusion(f32[27,32,128]{2,1,0:T(8,128)S(1)} %copy-done.8, f32[128,6120]{0,1:T(8,128)S(1)} %reshape.98), kind=kOutput, calls=%fused_computation.9 | convolution fusion | flops 2437447680 | bytes 9923328 | tf_op jit(solution)/shard_map/dot_general | solution.py:48
  651.8 3.0 fusion.17
  654.8 3.3 reshape.122
  658.1 3.3 squeeze.184
  661.4 5.9 fusion.18
  667.3 4.2 squeeze.185
  671.6 4.2 squeeze.186
  675.8 4.4 squeeze.187
  680.2 4.3 squeeze.188
  684.5 3.3 squeeze.189
  687.8 3.3 squeeze.190
  691.1 3.3 squeeze.191
  694.4 3.3 squeeze.192
  697.6 3.3 squeeze.193
  701.0 11.6 %add_add_fusion = f32[2,16,16,10,34]{4,3,2,1,0:T(8,128)} fusion(f32[2,16,16,10,34]{4,3,2,1,0:T(8,128)} %squeeze.187, f32[2,16,16,10,34]{4,3,2,1,0:T(8,128)} %squeeze.186, f32[2,16,16,10,34]{4,3,2,1,0:T(8,128)} %squeeze.185, f32[2,16,16,10,34]{4,3,2,1,0:T(8,128)} %reshape.122, f32[2,16,16,10,34]{4,3,2,1,0:T(8,128)} %squeeze.184), kind=kLoop, calls=%fused_computation.2 | loop fusion | flops 696320 | bytes 4177920 | tf_op jit(solution)/shard_map/add | solution.py:53
  712.6 7.8 %fusion.10 = f32[2,16,16,8,32]{4,3,2,1,0:T(8,128)} fusion(f32[2,16,16,8,32]{4,3,2,1,0:T(8,128)S(1)} %copy-done.3, f32[2,16,16,10,34]{4,3,2,1,0:T(8,128)} %squeeze.193, f32[2,16,16,10,34]{4,3,2,1,0:T(8,128)} %squeeze.192, f32[2,16,16,10,34]{4,3,2,1,0:T(8,128)} %squeeze.191, f32[2,16,16,10,34]{4,3,2,1,0:T(8,128)} %squeeze.190, ...), kind=kLoop, calls=%fused_computation.19 | loop fusion | flops 917504 | bytes 4722688 | tf_op jit(solution)/shard_map/jit(_where)/select_n | solution.py:81
  (65 shorter events, 34.6 us)
Async XLA Ops:
  6.5 151.3 %all-gather.5.cloned.1.call-start = ((), (), s32[]{:S(2)}) async-start(), calls=%async_computation | async-start | bytes 6291456 | tf_op jit(solution)/shard_map/all_gather | solution.py:75
  9.1 49.0 %copy-start.6 = (f32[2,16,16,8,32]{4,3,2,1,0:T(8,128)}, f32[2,16,16,8,32]{4,3,2,1,0:T(8,128)S(1)}, u32[]{:S(2)}) copy-start(f32[2,16,16,8,32]{4,3,2,1,0:T(8,128)S(1)} %broadcast_select_fusion) | copy-start | bytes 1572868
  9.2 146.9 %copy-start.10 = (f32[2]{0:T(128)S(1)}, f32[2]{0:T(128)}, u32[]{:S(2)}) copy-start(f32[2]{0:T(128)} %constant.8.clone) | copy-start | bytes 28
  9.2 46.7 %collective-permute-start = (f32[2,16,16,8,32]{4,3,2,1,0:T(8,128)S(1)}, f32[2,16,16,8,32]{4,3,2,1,0:T(8,128)}, u32[]{:S(2)}, u32[]{:S(2)}) collective-permute-start(f32[2,16,16,8,32]{4,3,2,1,0:T(8,128)S(1)} %broadcast_select_fusion), channel_id=1, source_target_pairs={{0,4},{4,0},{8,12},{12,8},{1,5},{5,1},{9,13},{13,9},{2,6},{6,2},{1... | collective-permute-start | bytes 1572872 | tf_op jit(solution)/shard_map/ppermute | solution.py:10
  55.8 92.8 %collective-permute-start.1 = (f32[2,16,16,8,32]{4,3,2,1,0:T(8,128)}, f32[2,16,16,8,32]{4,3,2,1,0:T(8,128)}, u32[]{:S(2)}, u32[]{:S(2)}) collective-permute-start(f32[2,16,16,8,32]{4,3,2,1,0:T(8,128)} %collective-permute-done), channel_id=1, source_target_pairs={{0,8},{4,12},{8,0},{12,4},{1,9},{5,13},{9,1},{13,5},{2,10},{6,14},... | collective-permute-start | bytes 1572872 | tf_op jit(solution)/shard_map/ppermute | solution.py:10
  58.2 158.1 %all-gather.7.cloned.1.call-start = ((), (), s32[]{:S(2)}) async-start(), calls=%async_computation.1 | async-start | bytes 6291456 | tf_op jit(solution)/shard_map/all_gather | solution.py:76
  148.6 4.6 collective-permute-start.2
  157.7 355.9 %all-gather.9.cloned.1.call-start = ((), (), s32[]{:S(2)}) async-start(), calls=%async_computation.2 | async-start | bytes 6291456 | tf_op jit(solution)/shard_map/all_gather | solution.py:75
  221.0 14.7 %copy-start.9 = (f32[27,2,16,64]{3,2,1,0:T(8,128)S(1)}, f32[27,2,16,64]{3,2,1,0:T(8,128)}, u32[]{:S(2)}) copy-start(f32[27,2,16,64]{3,2,1,0:T(8,128)} %param.6) | copy-start | bytes 663556
  229.8 14.7 %collective-permute-start.3 = (f32[2,64,16,1,32]{1,4,3,2,0:T(8,128)S(1)}, f32[2,64,16,1,32]{1,4,3,2,0:T(8,128)S(1)}, u32[]{:S(2)}, u32[]{:S(2)}) collective-permute-start(f32[2,64,16,1,32]{1,4,3,2,0:T(8,128)S(1)} %copy.15), channel_id=1, source_target_pairs={{0,4},{4,8},{8,12},{1,5},{5,9},{9,13},{2,6},{6,10},{10,14},{3,7},{... | collective-permute-start | bytes 786440 | tf_op jit(solution)/shard_map/ppermute | solution.py:20
  233.5 14.4 %collective-permute-start.4 = (f32[2,64,16,1,32]{1,4,3,2,0:T(8,128)S(1)}, f32[2,64,16,1,32]{1,4,3,2,0:T(8,128)S(1)}, u32[]{:S(2)}, u32[]{:S(2)}) collective-permute-start(f32[2,64,16,1,32]{1,4,3,2,0:T(8,128)S(1)} %copy.16), channel_id=1, source_target_pairs={{4,0},{8,4},{12,8},{5,1},{9,5},{13,9},{6,2},{10,6},{14,10},{7,3},{... | collective-permute-start | bytes 786440 | tf_op jit(solution)/shard_map/ppermute | solution.py:21
  243.5 11.7 %copy-start = (f32[2,64,16,8,32]{1,4,3,2,0:T(8,128)S(1)}, f32[2,64,16,8,32]{1,4,3,2,0:T(8,128)}, u32[]{:S(2)}) copy-start(f32[2,64,16,8,32]{1,4,3,2,0:T(8,128)} %copy.17) | copy-start | bytes 6291460
  249.0 6.3 collective-permute-start.5
  250.3 5.0 collective-permute-start.6
  278.1 6.2 copy-start.7
  346.2 11.6 %copy-start.2 = (f32[2,16,16,8,32]{4,3,2,1,0:T(8,128)S(1)}, f32[2,16,16,8,32]{4,3,2,1,0:T(8,128)}, u32[]{:S(2)}) copy-start(f32[2,16,16,8,32]{4,3,2,1,0:T(8,128)} %param.4) | copy-start | bytes 1572868
  346.2 11.6 %copy-start.5 = (f32[2,16,16,10,34]{4,3,2,1,0:T(8,128)S(1)}, f32[2,16,16,10,34]{4,3,2,1,0:T(8,128)}, u32[]{:S(2)}) copy-start(f32[2,16,16,10,34]{4,3,2,1,0:T(8,128)} %squeeze.166) | copy-start | bytes 2088964
  365.6 47.2 %collective-permute-start.7 = (f32[2,16,16,8,32]{4,3,2,1,0:T(8,128)}, f32[2,16,16,8,32]{4,3,2,1,0:T(8,128)}, u32[]{:S(2)}, u32[]{:S(2)}) collective-permute-start(f32[2,16,16,8,32]{4,3,2,1,0:T(8,128)} %fusion.11), channel_id=1, source_target_pairs={{0,4},{4,0},{8,12},{12,8},{1,5},{5,1},{9,13},{13,9},{2,6},{6,2},{1... | collective-permute-start | bytes 1572872 | tf_op jit(solution)/shard_map/ppermute | solution.py:10
  412.8 90.9 %collective-permute-start.8 = (f32[2,16,16,8,32]{4,3,2,1,0:T(8,128)}, f32[2,16,16,8,32]{4,3,2,1,0:T(8,128)S(1)}, u32[]{:S(2)}, u32[]{:S(2)}) collective-permute-start(f32[2,16,16,8,32]{4,3,2,1,0:T(8,128)} %collective-permute-done.7), channel_id=1, source_target_pairs={{0,8},{4,12},{8,0},{12,4},{1,9},{5,13},{9,1},{13,5},{2,10},{6,14},... | collective-permute-start | bytes 1572872 | tf_op jit(solution)/shard_map/ppermute | solution.py:10
  414.0 157.0 %all-gather.11.cloned.1.call-start = ((), (), s32[]{:S(2)}) async-start(), calls=%async_computation.3 | async-start | bytes 6291456 | tf_op jit(solution)/shard_map/all_gather | solution.py:76
  503.7 5.3 collective-permute-start.9
  584.8 14.7 %collective-permute-start.10 = (f32[2,64,16,1,32]{1,4,3,2,0:T(8,128)S(1)}, f32[2,64,16,1,32]{1,4,3,2,0:T(8,128)S(1)}, u32[]{:S(2)}, u32[]{:S(2)}) collective-permute-start(f32[2,64,16,1,32]{1,4,3,2,0:T(8,128)S(1)} %copy.19), channel_id=1, source_target_pairs={{0,4},{4,8},{8,12},{1,5},{5,9},{9,13},{2,6},{6,10},{10,14},{3,7},{... | collective-permute-start | bytes 786440 | tf_op jit(solution)/shard_map/ppermute | solution.py:20
  588.5 14.4 %collective-permute-start.11 = (f32[2,64,16,1,32]{1,4,3,2,0:T(8,128)S(1)}, f32[2,64,16,1,32]{1,4,3,2,0:T(8,128)S(1)}, u32[]{:S(2)}, u32[]{:S(2)}) collective-permute-start(f32[2,64,16,1,32]{1,4,3,2,0:T(8,128)S(1)} %copy.20), channel_id=1, source_target_pairs={{4,0},{8,4},{12,8},{5,1},{9,5},{13,9},{6,2},{10,6},{14,10},{7,3},{... | collective-permute-start | bytes 786440 | tf_op jit(solution)/shard_map/ppermute | solution.py:21
  598.6 11.7 %copy-start.1 = (f32[2,64,16,8,32]{1,4,3,2,0:T(8,128)S(1)}, f32[2,64,16,8,32]{1,4,3,2,0:T(8,128)}, u32[]{:S(2)}) copy-start(f32[2,64,16,8,32]{1,4,3,2,0:T(8,128)} %copy.21) | copy-start | bytes 6291460
  604.0 5.1 collective-permute-start.12
  605.3 5.0 collective-permute-start.13
  633.1 6.2 copy-start.8
  700.9 11.6 %copy-start.3 = (f32[2,16,16,8,32]{4,3,2,1,0:T(8,128)S(1)}, f32[2,16,16,8,32]{4,3,2,1,0:T(8,128)}, u32[]{:S(2)}) copy-start(f32[2,16,16,8,32]{4,3,2,1,0:T(8,128)} %param.4) | copy-start | bytes 1572868
  701.0 11.6 %copy-start.4 = (f32[2,16,16,10,34]{4,3,2,1,0:T(8,128)S(1)}, f32[2,16,16,10,34]{4,3,2,1,0:T(8,128)}, u32[]{:S(2)}) copy-start(f32[2,16,16,10,34]{4,3,2,1,0:T(8,128)} %squeeze.188) | copy-start | bytes 2088964
Sparse Core Ops, SparseCore 0:
  58.3 57.0 all-gather.4
  157.8 58.3 all-gather.6
  414.2 56.5 all-gather.8
  513.7 57.2 all-gather.10
where the time goes:
time: 734 us; the launch traced here: 727 us
  waiting for transfers between devices  398 us (54%)
  local copies, waits for them, and re-layouts  196 us (27%)
  other arithmetic  55.1 us (8%)
  matrix products  37.5 us (5%)
  starting transfers between devices  27 us (4%)
  between operations  13.7 us (2%)
    ppermute x6, waiting for transfers between devices, partner(): lax.ppermute(array, axis, [(i, i ^ 1 << apart) for i in range(lax.axis_si...  282 us
    all_gather x2, waiting for transfers between devices, on_device(): lax.all_gather(own_virtual, 'coil', axis=1, tiled=True)  107 us
    squeeze x20, local copies, waits for them, and re-layouts, convolve(): result = result + products[3 * second + third, :, offset:offset + length]  74.1 us
    dot_general x6, matrix products, convolve(): products = jnp.dot(group, window, precision=lax.Precision.HIGHEST)  37.5 us
    unnamed x26, local copies, waits for them, and re-layouts  26.3 us
    concatenate x4, local copies, waits for them, and re-layouts, on_device(): stacked = jnp.concatenate([physical, virtual], 1)  25.1 us
    add x2, other arithmetic, convolve(): result = result + products[3 * second + third, :, offset:offset + length]  23.2 us
    slice x4, local copies, waits for them, and re-layouts, padded_2(): last = lax.slice_in_dim(array, length - width, length, axis=dim)  17.7 us
  transfers between devices with their start and end apart: 18, of which 13 were waited for; matrix products, arithmetic and copies ran while one was open for 5% of the time, Pallas kernels for 0%

commit v1 on v0

v1 whole, which is shorter than its diff:
```python
import functools

import jax
import jax.numpy as jnp
from jax import lax
from jax.experimental import pallas as pl
from jax.experimental.pallas import tpu as pltpu
from jax.sharding import PartitionSpec as P

ITERS = 2
F32 = jnp.float32
BF16 = jnp.bfloat16
PARAMS = pltpu.CompilerParams(vmem_limit_bytes=48 << 20)
SMEM = pl.BlockSpec(memory_space=pltpu.SMEM)
VMEM = pl.BlockSpec(memory_space=pltpu.VMEM)


def split(x):
    hi = x.astype(BF16)
    return hi, (x - hi.astype(F32)).astype(BF16)


def reversal(n):
    row = lax.broadcasted_iota(jnp.int32, (n, n), 0)
    column = lax.broadcasted_iota(jnp.int32, (n, n), 1)
    return jnp.where(row + column == n - 1, 1.0, 0.0).astype(BF16)


def dot(a, b):
    return jnp.dot(a, b, preferred_element_type=F32)


def reversed_rows(x):
    hi, lo = split(x)
    flip = reversal(x.shape[0])
    return dot(flip, hi) + dot(flip, lo)


def pack_kernel(C, R, c_ref, measured, mask, *outs):
    c = c_ref[0]
    ch, _, D, W = measured.shape
    for d in range(C):
        for side in range(2):
            piece = lax.bitwise_xor(c, d)
            if side:
                piece = 2 * C - 1 - piece
            rows, marks = [], []
            for j in range(R):
                mark = mask[piece * R + j] == 1
                marks.append(jnp.where(mark, 1.0, 0.0))
                rows.append(jnp.where(mark[None], measured[:, piece * R + j], 0.0))
            out = outs[2 * d + side]
            out[: ch * D] = jnp.concatenate(rows, -1).reshape(ch * D, R * W)
            if d == 0:
                out[ch * D :] = jnp.concatenate(marks, -1)


def pack(c, measured, mask, C, R):
    ch, _, D, W = measured.shape
    shapes = []
    for d in range(C):
        shapes += [jax.ShapeDtypeStruct((ch * D + (D if d == 0 else 0), R * W), F32)] * 2
    return pl.pallas_call(
        functools.partial(pack_kernel, C, R),
        out_shape=shapes,
        in_specs=[SMEM, VMEM, VMEM],
        out_specs=[VMEM] * len(shapes),
        compiler_params=PARAMS,
        name="pack",
    )(c, measured, mask)


def weights_kernel(coils, kernel, w_hi, w_lo):
    taps = kernel.shape[0]

    def step(t, carry):
        def parts(tap):
            re, im = kernel[tap, 0], kernel[tap, 1]
            return re[:, :coils], im[:, :coils], re[:, coils:], im[:, coils:]

        pr, pi, vr, vi = parts(t)
        qr, qi, ur, ui = parts(taps - 1 - t)
        block = jnp.concatenate(
            [
                jnp.concatenate([pr, -pi, vr, vi], 1),
                jnp.concatenate([pi, pr, vi, -vr], 1),
                jnp.concatenate([ur, ui, qr, -qi], 1),
                jnp.concatenate([ui, -ur, qi, qr], 1),
            ],
            0,
        ).T
        hi, lo = split(block)
        first, second, third = t // 9, (t // 3) % 3, t % 3
        w_hi[second, first * 3 + third] = hi
        w_lo[second, first * 3 + third] = lo
        return carry

    lax.fori_loop(0, taps, step, 0)


def build_weights(kernel):
    taps, _, coils, _ = kernel.shape
    shape = jax.ShapeDtypeStruct((3, taps // 3, 4 * coils, 4 * coils), BF16)
    return pl.pallas_call(
        functools.partial(weights_kernel, coils),
        out_shape=[shape, shape],
        in_specs=[VMEM],
        out_specs=[VMEM, VMEM],
        compiler_params=PARAMS,
        name="weights",
    )(kernel)


def points_kernel(C, R, D, W, half, c_ref, *refs):
    msgs, (x, marks, stage) = refs[: 2 * C], refs[2 * C :]
    c = c_ref[0]
    size = msgs[1 if C > 1 else 0].shape[0]
    ch = 2 * (half // (2 * C))
    part = (ch // 2) * D
    for d in range(C):
        for side in range(2):
            for ri in range(2):
                start = ((side * 2 + ri) * C + lax.bitwise_xor(c, d)) * part
                start = pl.multiple_of(start, part)
                stage[pl.ds(start, part)] = msgs[2 * d + side][ri * part : (ri + 1) * part]
    L = R * W
    lane = lax.broadcasted_iota(jnp.int32, (L, 2 * half), 1)
    own_marks = msgs[0][ch * D :]
    other_marks = msgs[1][ch * D :]
    pad = jnp.zeros((2 * half - D, L), F32)
    own_marks = jnp.concatenate([own_marks, pad], 0).T
    other_marks = reversed_rows(jnp.concatenate([other_marks, pad], 0).T)
    for k in range(D):
        mine = stage[pl.ds(k, half, stride=D)]
        other = stage[pl.ds(half * D + D - 1 - k, half, stride=D)]
        both = jnp.concatenate([mine, other], 0).T
        both = jnp.where(lane < half, both, reversed_rows(both))
        mark = jnp.where(lane < half, own_marks[:, k : k + 1], other_marks[:, D - 1 - k : D - k])
        for i in range(R):
            x[i, k * W : (k + 1) * W] = both[i * W : (i + 1) * W]
            marks[i, k * W : (k + 1) * W] = mark[i * W : (i + 1) * W]


def points(c, msgs, C, R, D, W, half):
    shape = jax.ShapeDtypeStruct((R, D * W, 2 * half), F32)
    return pl.pallas_call(
        functools.partial(points_kernel, C, R, D, W, half),
        out_shape=[shape, shape],
        in_specs=[SMEM] + [VMEM] * len(msgs),
        out_specs=[VMEM, VMEM],
        scratch_shapes=[pltpu.VMEM((2 * half * D, R * W), F32)],
        compiler_params=PARAMS,
        name="points",
    )(c, *msgs)


def convolve(C, R, D, W, c, x, before, after, natural, mirrored, w_hi, w_lo, hi, lo):
    half = x.shape[-1] // 2

    def put(i, rows, value):
        h, l = split(value)
        hi[i, rows] = h
        lo[i, rows] = l

    inner, low, high = slice(W, (D + 1) * W), slice(0, W), slice((D + 1) * W, (D + 2) * W)
    for i in range(R):
        put(i + 1, low, before[i * W : (i + 1) * W])
        put(i + 1, inner, x[i])
        put(i + 1, high, after[i * W : (i + 1) * W])
    odd = lax.rem(c, 2)
    put((1 - odd) * (R + 1), slice(None), natural[...])
    face = mirrored[...]
    flipped = pltpu.roll(reversed_rows(face), half, 1)
    if C > 2:
        flipped = jnp.where(jnp.logical_or(c == 0, c == C - 1), flipped, face)
    put(odd * (R + 1), slice(None), flipped)

    def window(ref):
        return jnp.concatenate(
            [
                jnp.concatenate([ref[i + a, e * W : (e + D) * W] for i in range(R)], 0)
                for a in range(3)
                for e in range(3)
            ],
            1,
        )

    wide = jnp.concatenate([window(hi), window(lo), window(hi)], 1)
    rows = lax.broadcasted_iota(jnp.int32, (R * D * W, 2 * half), 0) % W
    total = None
    for b in range(3):
        own_hi = w_hi[b].reshape(-1, 2 * half)
        own_lo = w_lo[b].reshape(-1, 2 * half)
        y = dot(wide, jnp.concatenate([own_hi, own_hi, own_lo], 0))
        if b == 0:
            y = jnp.where(rows == 0, 0.0, pltpu.roll(y, 1, 0))
        if b == 2:
            y = jnp.where(rows == W - 1, 0.0, pltpu.roll(y, R * D * W - 1, 0))
        total = y if total is None else total + y
    return total.reshape(R, D * W, 2 * half)


def middle_kernel(C, R, D, W, c_ref, x, marks, before, after, natural, mirrored, w_hi, w_lo, out, hi, lo):
    y = convolve(C, R, D, W, c_ref[0], x, before, after, natural, mirrored, w_hi, w_lo, hi, lo)
    out[...] = jnp.where(marks[...] > 0.5, x[...], y)


def last_kernel(C, R, D, W, c_ref, x, before, after, natural, mirrored, w_hi, w_lo, *rest):
    outs, (hi, lo, stage) = rest[: 2 * C], rest[2 * C :]
    c = c_ref[0]
    y = convolve(C, R, D, W, c, x, before, after, natural, mirrored, w_hi, w_lo, hi, lo)
    half = x.shape[-1] // 2
    flip = reversal(R * W)
    for k in range(D):
        rows = jnp.concatenate([y[i, k * W : (k + 1) * W] for i in range(R)], 0).T
        stage[pl.ds(k, half, stride=D)] = rows[:half]
        h, l = split(rows[half:])
        stage[pl.ds(half * D + D - 1 - k, half, stride=D)] = dot(h, flip) + dot(l, flip)
    part = (half // (2 * C)) * D
    for d in range(C):
        for side in range(2):
            for ri in range(2):
                start = ((side * 2 + ri) * C + lax.bitwise_xor(c, d)) * part
                start = pl.multiple_of(start, part)
                outs[2 * d + side][ri * part : (ri + 1) * part] = stage[pl.ds(start, part)]


def iterate(last, c, x, marks, halos, weights, C, R, D, W):
    channels = x.shape[-1]
    scratch = [pltpu.VMEM((R + 2, (D + 2) * W, channels), BF16)] * 2
    if last:
        message = jax.ShapeDtypeStruct((channels // (2 * C) * D, R * W), F32)
        shapes = [message] * (2 * C)
        scratch.append(pltpu.VMEM((channels * D, R * W), F32))
        body, args = last_kernel, (c, x, *halos, *weights)
    else:
        shapes = [jax.ShapeDtypeStruct(x.shape, F32)]
        body, args = middle_kernel, (c, x, marks, *halos, *weights)
    return pl.pallas_call(
        functools.partial(body, C, R, D, W),
        out_shape=shapes,
        in_specs=[SMEM] + [VMEM] * (len(args) - 1),
        out_specs=[VMEM] * len(shapes),
        scratch_shapes=scratch,
        compiler_params=PARAMS,
        name="last" if last else "middle",
    )(*args)


def unpack_kernel(C, R, c_ref, measured, mask, *refs):
    msgs, out = refs[: 2 * C], refs[2 * C]
    c = c_ref[0]
    ch, _, D, W = measured.shape
    for d in range(C):
        for side in range(2):
            piece = lax.bitwise_xor(c, d)
            if side:
                piece = 2 * C - 1 - piece
            msg = msgs[2 * d + side][...].reshape(ch, D, R * W)
            for j in range(R):
                row = piece * R + j
                out[:, row] = jnp.where((mask[row] == 1)[None], measured[:, row], msg[:, :, j * W : (j + 1) * W])


def unpack(c, measured, mask, msgs, C, R):
    return pl.pallas_call(
        functools.partial(unpack_kernel, C, R),
        out_shape=jax.ShapeDtypeStruct(measured.shape, F32),
        in_specs=[SMEM] + [VMEM] * (2 + len(msgs)),
        out_specs=VMEM,
        compiler_params=PARAMS,
        name="unpack",
    )(c, measured, mask, *msgs)


def on_device(measured, mask, kernel):
    Z, C, X = lax.axis_size("kz"), lax.axis_size("coil"), lax.axis_size("kx")
    axes = ("kz", "coil", "kx")
    every = [(z, c, x) for z in range(Z) for c in range(C) for x in range(X)]

    def index(z, c, x):
        return (z * C + c) * X + x

    def send(array, target):
        pairs = [(index(*p), index(*target(*p))) for p in every if target(*p) is not None]
        return lax.ppermute(array, axes, pairs)

    def exchange(msgs):
        got = list(msgs)
        for d in reversed(range(C)):
            got[2 * d + 1] = send(msgs[2 * d + 1], lambda z, c, x: (Z - 1 - z, c ^ d, X - 1 - x))
        for d in range(1, C):
            got[2 * d] = send(msgs[2 * d], lambda z, c, x: (z, c ^ d, x))
        return got

    def across(z, c, x):
        if c % 2:
            return (z, c + 1, x) if c + 1 < C else (Z - 1 - z, c, X - 1 - x)
        if c:
            return (z, c - 1, x)
        return (Z - 1 - z, c, X - x) if x else None

    parts, coils, rows, D, W = measured.shape
    R = rows // (2 * C)
    half = parts * coils * C
    coil = lax.axis_index("coil")
    c = coil.astype(jnp.int32).reshape(1)
    odd = coil % 2 == 1
    flat = measured.reshape(parts * coils, rows, D, W)

    msgs = exchange(pack(c, flat, mask, C, R))
    weights = build_weights(lax.all_gather(kernel, "coil", axis=2, tiled=True))
    x, marks = points(c, msgs, C, R, D, W, half)
    for step in range(ITERS):
        first = x[:, :W].reshape(R * W, 2 * half)
        final = x[:, (D - 1) * W :].reshape(R * W, 2 * half)
        before = send(final, lambda z, c, x: (z + 1, c, x) if z + 1 < Z else None)
        after = send(first, lambda z, c, x: (z - 1, c, x) if z else None)

        def face(i):
            return jnp.concatenate([before[i * W : (i + 1) * W], x[i], after[i * W : (i + 1) * W]], 0)

        lower, upper = face(0), face(R - 1)
        natural = send(jnp.where(odd, lower, upper), lambda z, c, x: (z, c ^ 1, x))
        mirrored = send(jnp.where(odd, upper, lower), across)
        out = iterate(step == ITERS - 1, c, x, marks, (before, after, natural, mirrored), weights, C, R, D, W)
        if step < ITERS - 1:
            x = out[0]
    return unpack(c, flat, mask, exchange(out), C, R).reshape(measured.shape)


def solution(mesh):
    placed = (
        P(None, ("grp", "coil"), "kx", "kz", None),
        P(("grp", "kx"), "kz", None),
        P(None, None, "coil", None),
    )
    return jax.shard_map(
        on_device,
        mesh=mesh,
        in_specs=placed,
        out_specs=P(None, ("grp", "coil"), "kx", "kz", None),
        check_vma=False,
    )
```

time: 734 us -> 98.9 us (0.13)
  waiting for transfers between devices: 398 us -> 33.2 us
  local copies, waits for them, and re-layouts: 196 us -> 2.52 us
  other arithmetic: 55.1 us -> 0.05 us
  matrix products: 37.5 us -> 0 us
  Pallas kernels: 0 us -> 20.1 us
  between operations: 13.7 us -> 0.2 us
  blocking collectives: 0 us -> 13.4 us
    ppermute x14, waiting for transfers between devices: 291 us -> 33.2 us  [send(): return lax.ppermute(array, axes, pairs)]
    all_gather x4 -> x0, waiting for transfers between devices: 107 us -> none  [the longest x2 107 us: on_device(): lax.all_gather(own_virtual, 'coil', axis=1, tiled=True)]
    squeeze x21 -> x2, local copies, waits for them, and re-layouts: 74.1 us -> 0.04 us  [face(): x[i]]
    dot_general x6 -> x0, matrix products: 37.5 us -> none  [convolve(): products = jnp.dot(group, window, precision=lax.Precision.HIGHEST)]
    slice x8 -> x6, local copies, waits for them, and re-layouts: 30.7 us -> 0.04 us  [the longest x2 0.02 us: on_device(): first = x[:, :W].reshape(R * W, 2 * half)]
    concatenate x4 -> x0, local copies, waits for them, and re-layouts: 25.1 us -> none  [on_device(): stacked = jnp.concatenate([physical, virtual], 1)]
    unnamed x26 -> x10, local copies, waits for them, and re-layouts: 26.3 us -> 2.45 us
    add x2 -> x0, other arithmetic: 23.2 us -> none  [convolve(): result = result + products[3 * second + third, :, offset:offset + length]]
  transfers between devices with their start and end apart: 18 -> 14, of which waited for: 13 -> 8; matrix products, arithmetic and copies ran while one was open for 5% -> 0% of each run, Pallas kernels for 0% -> 5%
where the time goes in v1:
time: 98.9 us; the launch traced here: 98.5 us
  waiting for transfers between devices  33.2 us (34%)
  starting transfers between devices  29 us (29%)
  Pallas kernels  20.1 us (20%)
  blocking collectives  13.4 us (14%)
  local copies, waits for them, and re-layouts  2.52 us (3%)
    ppermute x14, waiting for transfers between devices, send(): return lax.ppermute(array, axes, pairs)  33.2 us
    ppermute x14, starting transfers between devices, send(): return lax.ppermute(array, axes, pairs)  29 us
    all_gather x1, blocking collectives, on_device(): weights = build_weights(lax.all_gather(kernel, 'coil', axis=2, tiled=True))  13.4 us
    pallas_call x2, Pallas kernels, iterate(): pl.pallas_call(functools.partial(body, C, R, D, W), out_shape=shapes, in_...  12.3 us
    pallas_call x1, Pallas kernels, build_weights(): pl.pallas_call(functools.partial(weights_kernel, coils), out_shape=[shape...  4.93 us
    unnamed x10, local copies, waits for them, and re-layouts  2.45 us
  transfers between devices with their start and end apart: 14, of which 8 were waited for; matrix products, arithmetic and copies ran while one was open for 0% of the time, Pallas kernels for 5%

profile of v1, /device:TPU:9, one launch (start us, length us, event | category | flops | bytes accessed | tf_op | source)
XLA Modules:
  0.0 98.5 jit_solution(3688364923253703097)
XLA Ops:
  0.0 0.0 copy-start
  0.0 1.6 %copy-done = f32[2,16,16,8,32]{4,3,2,1,0:T(8,128)S(1)} copy-done((f32[2,16,16,8,32]{4,3,2,1,0:T(8,128)S(1)}, f32[2,16,16,8,32]{4,3,2,1,0:T(8,128)}, u32[]{:S(2)}) %copy-start) | copy-done | bytes 524312
  1.6 0.0 copy-start.2
  1.6 0.8 copy-done.2
  2.4 0.0 copy-start.4
  2.4 0.5 pack.1
  2.9 1.9 %collective-permute-start = (f32[264,128]{1,0:T(8,128)S(1)}, f32[264,128]{1,0:T(8,128)S(1)}, u32[]{:S(2)}, u32[]{:S(2)}) collective-permute-start(f32[264,128]{1,0:T(8,128)S(1)} %get-tuple-element.18), channel_id=1, source_target_pairs={{0,13},{1,12},{2,15},{3,14},{4,9},{5,8},{6,11},{7,10},{8,5},{9,4},... | collective-permute-start | bytes 405512 | tf_op jit(solution)/shard_map/ppermute | solution.py:286
  4.9 1.2 %collective-permute-start.1 = (f32[256,128]{1,0:T(8,128)S(1)}, f32[256,128]{1,0:T(8,128)S(1)}, u32[]{:S(2)}, u32[]{:S(2)}) collective-permute-start(f32[256,128]{1,0:T(8,128)S(1)} %get-tuple-element.19), channel_id=1, source_target_pairs={{0,2},{1,3},{2,0},{3,1},{4,6},{5,7},{6,4},{7,5},{8,10},{9,11},{10,... | collective-permute-start | bytes 393224 | tf_op jit(solution)/shard_map/ppermute | solution.py:286
  6.1 0.3 collective-permute-start.2
  6.4 3.7 %collective-permute-done.1.refs_2_ = f32[256,128]{1,0:T(8,128)S(1)} collective-permute-done((f32[256,128]{1,0:T(8,128)S(1)}, f32[256,128]{1,0:T(8,128)S(1)}, u32[]{:S(2)}, u32[]{:S(2)}) %collective-permute-start.1) | collective-permute-done | bytes 131104 | tf_op jit(solution)/shard_map/ppermute | solution.py:286
  10.1 8.4 %collective-permute-done.2.refs_3_ = f32[256,128]{1,0:T(8,128)S(1)} collective-permute-done((f32[256,128]{1,0:T(8,128)S(1)}, f32[256,128]{1,0:T(8,128)S(1)}, u32[]{:S(2)}, u32[]{:S(2)}) %collective-permute-start.2) | collective-permute-done | bytes 131104 | tf_op jit(solution)/shard_map/ppermute | solution.py:286
  18.5 0.0 collective-permute-done.refs_1_
  18.5 0.6 points.1
  19.1 3.3 %collective-permute-start.3 = (f32[128,128]{1,0:T(8,128)S(1)}, f32[128,128]{1,0:T(8,128)S(1)}, u32[]{:S(2)}, u32[]{:S(2)}) collective-permute-start(f32[128,128]{1,0:T(8,128)S(1)} %bitcast.19), channel_id=1, source_target_pairs={{0,4},{1,5},{2,6},{3,7},{4,8},{5,9},{6,10},{7,11},{8,12},{9,13},{1... | collective-permute-start | bytes 196616 | tf_op jit(solution)/shard_map/ppermute | solution.py:286
  22.5 2.0 %collective-permute-start.4 = (f32[128,128]{1,0:T(8,128)S(1)}, f32[128,128]{1,0:T(8,128)S(1)}, u32[]{:S(2)}, u32[]{:S(2)}) collective-permute-start(f32[128,128]{1,0:T(8,128)S(1)} %bitcast.17), channel_id=1, source_target_pairs={{4,0},{5,1},{6,2},{7,3},{8,4},{9,5},{10,6},{11,7},{12,8},{13,9},{1... | collective-permute-start | bytes 196616 | tf_op jit(solution)/shard_map/ppermute | solution.py:286
  24.5 0.0 collective-permute-done.3.before
  24.5 3.0 %collective-permute-done.4.after = f32[128,128]{1,0:T(8,128)S(1)} collective-permute-done((f32[128,128]{1,0:T(8,128)S(1)}, f32[128,128]{1,0:T(8,128)S(1)}, u32[]{:S(2)}, u32[]{:S(2)}) %collective-permute-start.4) | collective-permute-done | bytes 65568 | tf_op jit(solution)/shard_map/ppermute | solution.py:286
  27.5 1.9 %collective-permute-start.6 = (f32[320,128]{1,0:T(8,128)S(1)}, f32[320,128]{1,0:T(8,128)S(1)}, u32[]{:S(2)}, u32[]{:S(2)}) collective-permute-start(f32[320,128]{1,0:T(8,128)S(1)} %get-tuple-element.39), channel_id=1, source_target_pairs={{1,13},{2,15},{3,14},{5,9},{6,11},{7,10},{9,5},{10,7},{11,6},{13,1... | collective-permute-start | bytes 491528 | tf_op jit(solution)/shard_map/ppermute | solution.py:286
  29.5 1.7 %collective-permute-start.5 = (f32[320,128]{1,0:T(8,128)S(1)}, f32[320,128]{1,0:T(8,128)S(1)}, u32[]{:S(2)}, u32[]{:S(2)}) collective-permute-start(f32[320,128]{1,0:T(8,128)S(1)} %get-tuple-element.40), channel_id=1, source_target_pairs={{0,2},{1,3},{2,0},{3,1},{4,6},{5,7},{6,4},{7,5},{8,10},{9,11},{10,... | collective-permute-start | bytes 491528 | tf_op jit(solution)/shard_map/ppermute | solution.py:286
  31.2 0.0 copy-done.4
  31.2 13.4 %all_gather.3.kernel = f32[27,2,32,64]{3,2,1,0:T(8,128)S(1)} all-gather(f32[27,2,16,64]{3,2,1,0:T(8,128)S(1)} %copy-done.4), channel_id=1, replica_groups=mesh['grp'=2,'kz'=4,'coil'=2,'kx'=2] {'coil'}, dimensions={2}, use_global_device_ids=true | all-gather | bytes 663552 | tf_op jit(solution)/shard_map/all_gather | solution.py:312
  44.7 4.9 %weights.1 = (bf16[3,9,128,128]{3,2,1,0:T(8,128)(2,1)S(1)}, bf16[3,9,128,128]{3,2,1,0:T(8,128)(2,1)S(1)}) custom-call(f32[27,2,32,64]{3,2,1,0:T(8,128)S(1)} %all_gather.3.kernel), custom_call_target="tpu_custom_call" | custom-call | tf_op jit(solution)/shard_map/weights/pallas_call | solution.py:104
  49.6 0.0 collective-permute-done.6.mirrored
  49.6 0.0 collective-permute-done.5.natural
  49.6 5.9 %middle.1.x = f32[4,256,128]{2,1,0:T(8,128)S(1)} custom-call(s32[1]{0:T(128)} %bitcast.c_ref, f32[4,256,128]{2,1,0:T(8,128)S(1)} %get-tuple-element.21.x, f32[4,256,128]{2,1,0:T(8,128)S(1)} %get-tuple-element.22.marks, f32[128,128]{1,0:T(8,128)S(1)} %collective-permute-done.3.before, f32[128,128]{1,0:T(8,128)S(1)} %collective-permute-done.4.after, ...), custom_call_target="tpu_custom_call" | custom-call | tf_op jit(solution)/shard_map/middle/pallas_call | solution.py:239
  55.6 0.0 copy-start.1
  55.6 0.0 copy-start.3
  55.6 3.1 %collective-permute-start.7 = (f32[128,128]{1,0:T(8,128)S(1)}, f32[128,128]{1,0:T(8,128)S(1)}, u32[]{:S(2)}, u32[]{:S(2)}) collective-permute-start(f32[128,128]{1,0:T(8,128)S(1)} %bitcast.20), channel_id=1, source_target_pairs={{0,4},{1,5},{2,6},{3,7},{4,8},{5,9},{6,10},{7,11},{8,12},{9,13},{1... | collective-permute-start | bytes 196616 | tf_op jit(solution)/shard_map/ppermute | solution.py:286
  58.8 2.3 %collective-permute-start.8 = (f32[128,128]{1,0:T(8,128)S(1)}, f32[128,128]{1,0:T(8,128)S(1)}, u32[]{:S(2)}, u32[]{:S(2)}) collective-permute-start(f32[128,128]{1,0:T(8,128)S(1)} %bitcast.18), channel_id=1, source_target_pairs={{4,0},{5,1},{6,2},{7,3},{8,4},{9,5},{10,6},{11,7},{12,8},{13,9},{1... | collective-permute-start | bytes 196616 | tf_op jit(solution)/shard_map/ppermute | solution.py:286
  61.0 0.0 collective-permute-done.7.before
  61.1 3.1 %collective-permute-done.8.after = f32[128,128]{1,0:T(8,128)S(1)} collective-permute-done((f32[128,128]{1,0:T(8,128)S(1)}, f32[128,128]{1,0:T(8,128)S(1)}, u32[]{:S(2)}, u32[]{:S(2)}) %collective-permute-start.8) | collective-permute-done | bytes 65568 | tf_op jit(solution)/shard_map/ppermute | solution.py:286
  64.2 2.9 %collective-permute-start.10 = (f32[320,128]{1,0:T(8,128)S(1)}, f32[320,128]{1,0:T(8,128)S(1)}, u32[]{:S(2)}, u32[]{:S(2)}) collective-permute-start(f32[320,128]{1,0:T(8,128)S(1)} %get-tuple-element.37), channel_id=1, source_target_pairs={{1,13},{2,15},{3,14},{5,9},{6,11},{7,10},{9,5},{10,7},{11,6},{13,1... | collective-permute-start | bytes 491528 | tf_op jit(solution)/shard_map/ppermute | solution.py:286
  67.1 2.7 %collective-permute-start.9 = (f32[320,128]{1,0:T(8,128)S(1)}, f32[320,128]{1,0:T(8,128)S(1)}, u32[]{:S(2)}, u32[]{:S(2)}) collective-permute-start(f32[320,128]{1,0:T(8,128)S(1)} %get-tuple-element.38), channel_id=1, source_target_pairs={{0,2},{1,3},{2,0},{3,1},{4,6},{5,7},{6,4},{7,5},{8,10},{9,11},{10,... | collective-permute-start | bytes 491528 | tf_op jit(solution)/shard_map/ppermute | solution.py:286
  69.8 2.5 %collective-permute-done.10.mirrored = f32[320,128]{1,0:T(8,128)S(1)} collective-permute-done((f32[320,128]{1,0:T(8,128)S(1)}, f32[320,128]{1,0:T(8,128)S(1)}, u32[]{:S(2)}, u32[]{:S(2)}) %collective-permute-start.10) | collective-permute-done | bytes 163872 | tf_op jit(solution)/shard_map/ppermute | solution.py:286
  72.3 1.7 %collective-permute-done.9.natural = f32[320,128]{1,0:T(8,128)S(1)} collective-permute-done((f32[320,128]{1,0:T(8,128)S(1)}, f32[320,128]{1,0:T(8,128)S(1)}, u32[]{:S(2)}, u32[]{:S(2)}) %collective-permute-start.9) | collective-permute-done | bytes 163872 | tf_op jit(solution)/shard_map/ppermute | solution.py:286
  74.0 6.3 %last.1 = (f32[256,128]{1,0:T(8,128)S(1)}, f32[256,128]{1,0:T(8,128)S(1)}, f32[256,128]{1,0:T(8,128)S(1)}, f32[256,128]{1,0:T(8,128)S(1)}) custom-call(s32[1]{0:T(128)} %bitcast.c_ref, f32[4,256,128]{2,1,0:T(8,128)S(1)} %middle.1.x, f32[128,128]{1,0:T(8,128)S(1)} %collective-permute-done.7.before, f32[128,128]{1,0:T(8,128)S(1)} %collective-permute-done.8.after, ...), custom_call_target="tpu_custom_call" | custom-call | tf_op jit(solution)/shard_map/last/pallas_call | solution.py:239
  80.3 1.0 collective-permute-start.11
  81.3 4.5 %collective-permute-start.12 = (f32[256,128]{1,0:T(8,128)S(1)}, f32[256,128]{1,0:T(8,128)S(1)}, u32[]{:S(2)}, u32[]{:S(2)}) collective-permute-start(f32[256,128]{1,0:T(8,128)S(1)} %get-tuple-element.27), channel_id=1, source_target_pairs={{0,2},{1,3},{2,0},{3,1},{4,6},{5,7},{6,4},{7,5},{8,10},{9,11},{10,... | collective-permute-start | bytes 393224 | tf_op jit(solution)/shard_map/ppermute | solution.py:286
  85.8 0.1 collective-permute-start.13
  85.9 5.9 %collective-permute-done.11.refs_1_ = f32[256,128]{1,0:T(8,128)S(1)} collective-permute-done((f32[256,128]{1,0:T(8,128)S(1)}, f32[256,128]{1,0:T(8,128)S(1)}, u32[]{:S(2)}, u32[]{:S(2)}) %collective-permute-start.11) | collective-permute-done | bytes 131104 | tf_op jit(solution)/shard_map/ppermute | solution.py:286
  91.8 0.0 collective-permute-done.12.refs_2_
  91.8 4.9 %collective-permute-done.13.refs_3_ = f32[256,128]{1,0:T(8,128)S(1)} collective-permute-done((f32[256,128]{1,0:T(8,128)S(1)}, f32[256,128]{1,0:T(8,128)S(1)}, u32[]{:S(2)}, u32[]{:S(2)}) %collective-permute-start.13) | collective-permute-done | bytes 131104 | tf_op jit(solution)/shard_map/ppermute | solution.py:286
  96.7 0.0 copy-done.1
  96.7 0.0 copy-done.3
  96.7 1.8 %unpack.1 = f32[32,16,8,32]{3,2,1,0:T(8,128)} custom-call(s32[1]{0:T(128)} %bitcast.c_ref, f32[32,16,8,32]{3,2,1,0:T(8,128)S(1)} %bitcast.16, s32[16,8,32]{2,1,0:T(8,128)S(1)} %copy-done.3, f32[256,128]{1,0:T(8,128)S(1)} %get-tuple-element.25.refs_0_, f32[256,128]{1,0:T(8,128)S(1)} %collective-permute-done.11.refs_1_, ...), custom_call_target="tpu_custom_call" | custom-call | tf_op jit(solution)/shard_map/unpack/pallas_call | solution.py:266
  (10 shorter events, 0.1 us)
Async XLA Ops:
  0.0 1.6 %copy-start = (f32[2,16,16,8,32]{4,3,2,1,0:T(8,128)S(1)}, f32[2,16,16,8,32]{4,3,2,1,0:T(8,128)}, u32[]{:S(2)}) copy-start(f32[2,16,16,8,32]{4,3,2,1,0:T(8,128)} %param.3) | copy-start | bytes 1572868
  1.6 0.8 copy-start.2
  2.4 28.8 %copy-start.4 = (f32[27,2,16,64]{3,2,1,0:T(8,128)S(1)}, f32[27,2,16,64]{3,2,1,0:T(8,128)}, u32[]{:S(2)}) copy-start(f32[27,2,16,64]{3,2,1,0:T(8,128)} %param.5) | copy-start | bytes 663556
  2.9 15.5 %collective-permute-start = (f32[264,128]{1,0:T(8,128)S(1)}, f32[264,128]{1,0:T(8,128)S(1)}, u32[]{:S(2)}, u32[]{:S(2)}) collective-permute-start(f32[264,128]{1,0:T(8,128)S(1)} %get-tuple-element.18), channel_id=1, source_target_pairs={{0,13},{1,12},{2,15},{3,14},{4,9},{5,8},{6,11},{7,10},{8,5},{9,4},... | collective-permute-start | bytes 405512 | tf_op jit(solution)/shard_map/ppermute | solution.py:286
  4.9 5.2 %collective-permute-start.1 = (f32[256,128]{1,0:T(8,128)S(1)}, f32[256,128]{1,0:T(8,128)S(1)}, u32[]{:S(2)}, u32[]{:S(2)}) collective-permute-start(f32[256,128]{1,0:T(8,128)S(1)} %get-tuple-element.19), channel_id=1, source_target_pairs={{0,2},{1,3},{2,0},{3,1},{4,6},{5,7},{6,4},{7,5},{8,10},{9,11},{10,... | collective-permute-start | bytes 393224 | tf_op jit(solution)/shard_map/ppermute | solution.py:286
  6.1 12.4 %collective-permute-start.2 = (f32[256,128]{1,0:T(8,128)S(1)}, f32[256,128]{1,0:T(8,128)S(1)}, u32[]{:S(2)}, u32[]{:S(2)}) collective-permute-start(f32[256,128]{1,0:T(8,128)S(1)} %get-tuple-element.20), channel_id=1, source_target_pairs={{0,15},{1,14},{2,13},{3,12},{4,11},{5,10},{6,9},{7,8},{8,7},{9,6},... | collective-permute-start | bytes 393224 | tf_op jit(solution)/shard_map/ppermute | solution.py:286
  19.1 5.3 %collective-permute-start.3 = (f32[128,128]{1,0:T(8,128)S(1)}, f32[128,128]{1,0:T(8,128)S(1)}, u32[]{:S(2)}, u32[]{:S(2)}) collective-permute-start(f32[128,128]{1,0:T(8,128)S(1)} %bitcast.19), channel_id=1, source_target_pairs={{0,4},{1,5},{2,6},{3,7},{4,8},{5,9},{6,10},{7,11},{8,12},{9,13},{1... | collective-permute-start | bytes 196616 | tf_op jit(solution)/shard_map/ppermute | solution.py:286
  22.5 5.0 %collective-permute-start.4 = (f32[128,128]{1,0:T(8,128)S(1)}, f32[128,128]{1,0:T(8,128)S(1)}, u32[]{:S(2)}, u32[]{:S(2)}) collective-permute-start(f32[128,128]{1,0:T(8,128)S(1)} %bitcast.17), channel_id=1, source_target_pairs={{4,0},{5,1},{6,2},{7,3},{8,4},{9,5},{10,6},{11,7},{12,8},{13,9},{1... | collective-permute-start | bytes 196616 | tf_op jit(solution)/shard_map/ppermute | solution.py:286
  27.5 22.1 %collective-permute-start.6 = (f32[320,128]{1,0:T(8,128)S(1)}, f32[320,128]{1,0:T(8,128)S(1)}, u32[]{:S(2)}, u32[]{:S(2)}) collective-permute-start(f32[320,128]{1,0:T(8,128)S(1)} %get-tuple-element.39), channel_id=1, source_target_pairs={{1,13},{2,15},{3,14},{5,9},{6,11},{7,10},{9,5},{10,7},{11,6},{13,1... | collective-permute-start | bytes 491528 | tf_op jit(solution)/shard_map/ppermute | solution.py:286
  29.5 20.1 %collective-permute-start.5 = (f32[320,128]{1,0:T(8,128)S(1)}, f32[320,128]{1,0:T(8,128)S(1)}, u32[]{:S(2)}, u32[]{:S(2)}) collective-permute-start(f32[320,128]{1,0:T(8,128)S(1)} %get-tuple-element.40), channel_id=1, source_target_pairs={{0,2},{1,3},{2,0},{3,1},{4,6},{5,7},{6,4},{7,5},{8,10},{9,11},{10,... | collective-permute-start | bytes 491528 | tf_op jit(solution)/shard_map/ppermute | solution.py:286
  55.6 41.1 %copy-start.1 = (f32[2,16,16,8,32]{4,3,2,1,0:T(8,128)S(1)}, f32[2,16,16,8,32]{4,3,2,1,0:T(8,128)}, u32[]{:S(2)}) copy-start(f32[2,16,16,8,32]{4,3,2,1,0:T(8,128)} %param.3) | copy-start | bytes 1572868
  55.6 41.1 %copy-start.3 = (s32[16,8,32]{2,1,0:T(8,128)S(1)}, s32[16,8,32]{2,1,0:T(8,128)}, u32[]{:S(2)}) copy-start(s32[16,8,32]{2,1,0:T(8,128)} %mask.3) | copy-start | bytes 49156
  55.6 5.5 %collective-permute-start.7 = (f32[128,128]{1,0:T(8,128)S(1)}, f32[128,128]{1,0:T(8,128)S(1)}, u32[]{:S(2)}, u32[]{:S(2)}) collective-permute-start(f32[128,128]{1,0:T(8,128)S(1)} %bitcast.20), channel_id=1, source_target_pairs={{0,4},{1,5},{2,6},{3,7},{4,8},{5,9},{6,10},{7,11},{8,12},{9,13},{1... | collective-permute-start | bytes 196616 | tf_op jit(solution)/shard_map/ppermute | solution.py:286
  58.8 5.4 %collective-permute-start.8 = (f32[128,128]{1,0:T(8,128)S(1)}, f32[128,128]{1,0:T(8,128)S(1)}, u32[]{:S(2)}, u32[]{:S(2)}) collective-permute-start(f32[128,128]{1,0:T(8,128)S(1)} %bitcast.18), channel_id=1, source_target_pairs={{4,0},{5,1},{6,2},{7,3},{8,4},{9,5},{10,6},{11,7},{12,8},{13,9},{1... | collective-permute-start | bytes 196616 | tf_op jit(solution)/shard_map/ppermute | solution.py:286
  64.2 8.1 %collective-permute-start.10 = (f32[320,128]{1,0:T(8,128)S(1)}, f32[320,128]{1,0:T(8,128)S(1)}, u32[]{:S(2)}, u32[]{:S(2)}) collective-permute-start(f32[320,128]{1,0:T(8,128)S(1)} %get-tuple-element.37), channel_id=1, source_target_pairs={{1,13},{2,15},{3,14},{5,9},{6,11},{7,10},{9,5},{10,7},{11,6},{13,1... | collective-permute-start | bytes 491528 | tf_op jit(solution)/shard_map/ppermute | solution.py:286
  67.1 6.9 %collective-permute-start.9 = (f32[320,128]{1,0:T(8,128)S(1)}, f32[320,128]{1,0:T(8,128)S(1)}, u32[]{:S(2)}, u32[]{:S(2)}) collective-permute-start(f32[320,128]{1,0:T(8,128)S(1)} %get-tuple-element.38), channel_id=1, source_target_pairs={{0,2},{1,3},{2,0},{3,1},{4,6},{5,7},{6,4},{7,5},{8,10},{9,11},{10,... | collective-permute-start | bytes 491528 | tf_op jit(solution)/shard_map/ppermute | solution.py:286
  80.3 11.5 %collective-permute-start.11 = (f32[256,128]{1,0:T(8,128)S(1)}, f32[256,128]{1,0:T(8,128)S(1)}, u32[]{:S(2)}, u32[]{:S(2)}) collective-permute-start(f32[256,128]{1,0:T(8,128)S(1)} %get-tuple-element.26), channel_id=1, source_target_pairs={{0,13},{1,12},{2,15},{3,14},{4,9},{5,8},{6,11},{7,10},{8,5},{9,4},... | collective-permute-start | bytes 393224 | tf_op jit(solution)/shard_map/ppermute | solution.py:286
  81.3 10.5 %collective-permute-start.12 = (f32[256,128]{1,0:T(8,128)S(1)}, f32[256,128]{1,0:T(8,128)S(1)}, u32[]{:S(2)}, u32[]{:S(2)}) collective-permute-start(f32[256,128]{1,0:T(8,128)S(1)} %get-tuple-element.27), channel_id=1, source_target_pairs={{0,2},{1,3},{2,0},{3,1},{4,6},{5,7},{6,4},{7,5},{8,10},{9,11},{10,... | collective-permute-start | bytes 393224 | tf_op jit(solution)/shard_map/ppermute | solution.py:286
  85.8 10.9 %collective-permute-start.13 = (f32[256,128]{1,0:T(8,128)S(1)}, f32[256,128]{1,0:T(8,128)S(1)}, u32[]{:S(2)}, u32[]{:S(2)}) collective-permute-start(f32[256,128]{1,0:T(8,128)S(1)} %get-tuple-element.28), channel_id=1, source_target_pairs={{0,15},{1,14},{2,13},{3,12},{4,11},{5,10},{6,9},{7,8},{8,7},{9,6},... | collective-permute-start | bytes 393224 | tf_op jit(solution)/shard_map/ppermute | solution.py:286

commit v2 on v0

v2 whole, which is shorter than its diff:
```python
import functools

import jax
import jax.numpy as jnp
from jax import lax
from jax.experimental import pallas as pl
from jax.experimental.pallas import tpu as pltpu
from jax.sharding import PartitionSpec as P

ITERS = 2
AXES = ("kz", "coil", "kx")
F32 = jnp.float32
BF16 = jnp.bfloat16
PARAMS = pltpu.CompilerParams(vmem_limit_bytes=48 << 20)
ANY = pl.BlockSpec(memory_space=pl.ANY)
HBM = pl.BlockSpec(memory_space=pltpu.HBM)
VMEM = pl.BlockSpec(memory_space=pltpu.VMEM)


def call(body, name, args, shapes, scratch=(), far=(), space=ANY, out=VMEM, **options):
    return pl.pallas_call(
        body,
        out_shape=shapes,
        in_specs=[space if i in far else VMEM for i in range(len(args))],
        out_specs=[out] * len(shapes),
        scratch_shapes=list(scratch),
        compiler_params=PARAMS,
        name=name,
        **options,
    )(*args)


def split(x):
    hi = x.astype(BF16)
    return hi, (x - hi.astype(F32)).astype(BF16)


def reversal(n):
    row = lax.broadcasted_iota(jnp.int32, (n, n), 0)
    column = lax.broadcasted_iota(jnp.int32, (n, n), 1)
    return jnp.where(row + column == n - 1, 1.0, 0.0).astype(BF16)


def dot(a, b):
    return jnp.dot(a, b, preferred_element_type=F32)


def reversed_rows(x):
    hi, lo = split(x)
    flip = reversal(x.shape[0])
    return dot(flip, hi) + dot(flip, lo)


def is_upper(z, x, Z):
    return (x == 0) != (z >= Z // 2)


def place():
    return tuple(lax.axis_index(axis) for axis in AXES)


def piece_of(C, d, side):
    z, c, x = place()
    upper = jnp.where(is_upper(z, x, lax.axis_size("kz")), C, 0)
    piece = lax.bitwise_xor(c, d) + upper
    return 2 * C - 1 - piece if side else piece


def pack_kernel(C, R, measured, mask, *refs):
    outs, (rows, marks, sems) = refs[: 2 * C], refs[2 * C :]
    ch, _, D, W = measured.shape
    copies = [pltpu.make_async_copy(mask, marks, sems.at[2 * C])]
    order = [(side, d) for side in (1, 0) for d in range(C)]
    for slot, (side, d) in enumerate(order):
        start = piece_of(C, d, side) * R
        copies.append(pltpu.make_async_copy(measured.at[:, pl.ds(start, R)], rows.at[slot], sems.at[slot]))
    for copy in copies:
        copy.start()
    copies[0].wait()
    for slot, (side, d) in enumerate(order):
        copies[slot + 1].wait()
        start = piece_of(C, d, side) * R
        sampled = [marks[start + j] == 1 for j in range(R)]
        kept = [jnp.where(sampled[j][None], rows[slot, :, j], 0.0) for j in range(R)]
        out = outs[2 * d + side]
        out[: ch * D] = jnp.concatenate(kept, -1).reshape(ch * D, R * W)
        if d == 0:
            out[ch * D :] = jnp.concatenate([jnp.where(s, 1.0, 0.0) for s in sampled], -1)


def pack(measured, mask, C, R):
    ch, _, D, W = measured.shape
    shapes = []
    for d in range(C):
        shapes += [jax.ShapeDtypeStruct((ch * D + (D if d == 0 else 0), R * W), F32)] * 2
    scratch = [
        pltpu.VMEM((2 * C, ch, R, D, W), F32),
        pltpu.VMEM(mask.shape, jnp.int32),
        pltpu.SemaphoreType.DMA((2 * C + 1,)),
    ]
    return call(functools.partial(pack_kernel, C, R), "pack", (measured, mask), shapes, scratch, far=(0, 1), space=HBM)


def fold_kernel(kernel, out):
    half = kernel.shape[2] // 2
    out[...] = jnp.concatenate([kernel[:, :, :half], kernel[:, :, half:]], -1)


def weights_kernel(C, *refs):
    folded, (single, double, kernel) = refs[:C], refs[C:]
    taps, _, coils, inputs = kernel.shape
    half = folded[0].shape[2]
    for d in range(C):
        start = pl.multiple_of(lax.bitwise_xor(lax.axis_index("coil"), d) * 2 * half, 2 * half)
        kernel[:, :, pl.ds(start, half)] = folded[d][..., :inputs]
        kernel[:, :, pl.ds(start + half, half)] = folded[d][..., inputs:]

    def parts(tap):
        re, im = kernel[tap, 0], kernel[tap, 1]
        return re[:, :coils], im[:, :coils], re[:, coils:], im[:, coils:]

    N = 4 * coils
    for t in range(taps):
        pr, pi, vr, vi = parts(t)
        qr, qi, ur, ui = parts(taps - 1 - t)
        block = jnp.concatenate(
            [
                jnp.concatenate([pr, -pi, vr, vi], 1),
                jnp.concatenate([pi, pr, vi, -vr], 1),
                jnp.concatenate([ur, ui, qr, -qi], 1),
                jnp.concatenate([ui, -ur, qi, qr], 1),
            ],
            0,
        ).T
        hi, lo = split(block)
        b, tap = (t // 3) % 3, t // 9 * 3 + t % 3
        single[tap, :, b * N : (b + 1) * N] = hi
        double[tap, :, 2 * b * N : (2 * b + 1) * N] = hi
        double[tap, :, (2 * b + 1) * N : (2 * b + 2) * N] = lo


def build_weights(C, folded, coils):
    taps, parts, _, inputs = folded[0].shape
    N = 4 * coils
    shapes = [jax.ShapeDtypeStruct((9, N, 3 * N), BF16), jax.ShapeDtypeStruct((9, N, 6 * N), BF16)]
    scratch = [pltpu.VMEM((taps, parts, coils, inputs // 2), F32)]
    return call(functools.partial(weights_kernel, C), "weights", folded, shapes, scratch)


def plane_faces(x, face_a, face_b):
    R, rows, channels = x.shape
    W = face_a.shape[0] // R
    z, Z = lax.axis_index("kz"), lax.axis_size("kz")
    first = x[:, :W].reshape(R * W, channels)
    final = x[:, rows - W :].reshape(R * W, channels)
    odd = lax.rem(z, 2) == 1
    face_a[...] = jnp.where(odd, first, final)
    face = jnp.where(odd, final, first)
    flipped = pltpu.roll(reversed_rows(face), channels // 2, 1)
    face_b[...] = jnp.where(jnp.logical_or(z == Z // 2 - 1, z == Z // 2), flipped, face)


def points_kernel(C, R, D, W, half, ready, *refs):
    msgs, (x, marks, face_a, face_b, stage) = refs[: 2 * C], refs[2 * C :]
    c = lax.axis_index("coil")
    ch = half // C
    part = (ch // 2) * D
    for d in range(C):
        for side in range(2):
            for ri in range(2):
                start = ((side * 2 + ri) * C + lax.bitwise_xor(c, d)) * part
                start = pl.multiple_of(start, part)
                stage[pl.ds(start, part)] = msgs[2 * d + side][ri * part : (ri + 1) * part]
    L = R * W
    lane = lax.broadcasted_iota(jnp.int32, (L, 2 * half), 1)
    pad = jnp.zeros((2 * half - D, L), F32)
    own_marks = jnp.concatenate([msgs[0][ch * D :], pad], 0).T
    other_marks = reversed_rows(jnp.concatenate([msgs[1][ch * D :], pad], 0).T)
    for k in range(D):
        mine = stage[pl.ds(k, half, stride=D)]
        other = stage[pl.ds(half * D + D - 1 - k, half, stride=D)]
        both = jnp.concatenate([mine, other], 0).T
        both = jnp.where(lane < half, both, reversed_rows(both))
        mark = jnp.where(lane < half, own_marks[:, k : k + 1], other_marks[:, D - 1 - k : D - k])
        for i in range(R):
            x[i, k * W : (k + 1) * W] = both[i * W : (i + 1) * W]
            marks[i, k * W : (k + 1) * W] = mark[i * W : (i + 1) * W]
    plane_faces(x, face_a, face_b)


def points(ready, msgs, C, R, D, W, half):
    shape = jax.ShapeDtypeStruct((R, D * W, 2 * half), F32)
    face = jax.ShapeDtypeStruct((R * W, 2 * half), F32)
    return call(
        functools.partial(points_kernel, C, R, D, W, half),
        "points",
        (ready, *msgs),
        [shape, shape, face, face],
        [pltpu.VMEM((2 * half * D, R * W), F32)],
        far=(0,),
    )


def multiply(hi, lo, single, double, W):
    M, N = hi.shape[0], single.shape[-1] // 3
    y, z = dot(hi, double), dot(lo, single)
    y = [
        y[:, 2 * b * N : (2 * b + 1) * N] + y[:, (2 * b + 1) * N : (2 * b + 2) * N] + z[:, b * N : (b + 1) * N]
        for b in range(3)
    ]
    rows = lax.broadcasted_iota(jnp.int32, (M, N), 0) % W
    right = jnp.where(rows == 0, 0.0, pltpu.roll(y[0], 1, 0))
    left = jnp.where(rows == W - 1, 0.0, pltpu.roll(y[2], M - 1, 0))
    return y[1] + right + left


def taps_of(weights, a, e):
    return [jnp.concatenate([w[3 * i + j] for i in a for j in e], 0) for w in weights]


def own_part(R, D, W, start, count, x, weights, hi, lo):
    channels = x.shape[-1]
    edge = jnp.zeros((W, channels), BF16)
    for j in range(count + 2):
        row = start + j - 1
        if 0 <= row < R:
            hi[j, W : (D + 1) * W], lo[j, W : (D + 1) * W] = split(x[row])
            for ref in (hi, lo):
                ref[j, :W] = edge
                ref[j, (D + 1) * W :] = edge
        else:
            hi[j] = lo[j] = jnp.zeros(((D + 2) * W, channels), BF16)

    def window(ref):
        return jnp.concatenate(
            [
                jnp.concatenate([ref[i + a, e * W : (e + D) * W] for i in range(count)], 0)
                for a in range(3)
                for e in range(3)
            ],
            1,
        )

    y = multiply(window(hi), window(lo), *taps_of(weights, range(3), range(3)), W)
    return y.reshape(count, D * W, channels)


def upper_kernel(R, D, W, x, single, double, out, hi, lo):
    out[...] = own_part(R, D, W, 0, out.shape[0], x, (single, double), hi, lo)


def lower_kernel(R, D, W, x, upper, before, after, single, double, out, hi, lo):
    weights = (single, double)
    count = upper.shape[0]
    out[:count] = upper[...]
    out[count:] = own_part(R, D, W, count, R - count, x, weights, hi, lo)
    edge = jnp.zeros((W, x.shape[-1]), BF16)
    for plane, e, k in ((before, 0, 0), (after, 2, D - 1)):
        wide = [
            jnp.concatenate(
                [jnp.concatenate([edge, part[:-W]], 0), part, jnp.concatenate([part[W:], edge], 0)], 1
            )
            for part in split(plane[...])
        ]
        y = multiply(*wide, *taps_of(weights, range(3), [e]), W)
        for i in range(R):
            out[i, k * W : (k + 1) * W] += y[i * W : (i + 1) * W]


def finish(D, W, main, near, far, weights):
    R, _, channels = main.shape
    z, c, x = place()
    C = lax.axis_size("coil")
    upper = is_upper(z, x, lax.axis_size("kz"))
    mirrored = jnp.where(upper, c == 0, c == C - 1)
    edge = jnp.where(upper, (c == C - 1) & (x == 1), (c == 0) & (x == 0))
    near, far = near[...], far[...]
    far = jnp.where(mirrored, pltpu.roll(reversed_rows(far), channels // 2, 1), far)
    far = jnp.where(edge, 0.0, far)
    odd = lax.rem(c, 2) == 1
    below = jnp.where(odd, near, far)
    above = jnp.where(odd, far, near)
    rows = [main[i] for i in range(R)]
    for plane, a, row in ((below, 0, 0), (above, 2, R - 1)):
        wide = [jnp.concatenate([p[e * W : (e + D) * W] for e in range(3)], 1) for p in split(plane)]
        rows[row] += multiply(*wide, *taps_of(weights, [a], range(3)), W)
    return rows


def middle_kernel(D, W, x, marks, main, near, far, single, double, out, face_a, face_b):
    for i, row in enumerate(finish(D, W, main, near, far, (single, double))):
        out[i] = jnp.where(marks[i] > 0.5, x[i], row)
    plane_faces(out, face_a, face_b)


def last_kernel(C, D, W, main, near, far, single, double, *rest):
    outs, stage = rest[: 2 * C], rest[2 * C]
    y = finish(D, W, main, near, far, (single, double))
    half = main.shape[-1] // 2
    flip = reversal(len(y) * W)
    for k in range(D):
        rows = jnp.concatenate([row[k * W : (k + 1) * W] for row in y], 0).T
        stage[pl.ds(k, half, stride=D)] = rows[:half]
        h, l = split(rows[half:])
        stage[pl.ds(half * D + D - 1 - k, half, stride=D)] = dot(h, flip) + dot(l, flip)
    part = (half // (2 * C)) * D
    for d in range(C):
        for side in range(2):
            for ri in range(2):
                start = ((side * 2 + ri) * C + lax.bitwise_xor(lax.axis_index("coil"), d)) * part
                start = pl.multiple_of(start, part)
                outs[2 * d + side][ri * part : (ri + 1) * part] = stage[pl.ds(start, part)]


def unpack_kernel(C, R, side, measured, mask, *refs):
    msgs, (out, rows, sems) = refs[:C], refs[-3:]
    ch, _, D, W = measured.shape
    copies = []
    for d in range(C):
        start = piece_of(C, d, side) * R
        msg = msgs[d][...].reshape(ch, D, R * W)
        for j in range(R):
            sampled = (mask[start + j] == 1)[None]
            rows[d, :, j] = jnp.where(sampled, measured[:, start + j], msg[:, :, j * W : (j + 1) * W])
        copies.append(pltpu.make_async_copy(rows.at[d], out.at[:, pl.ds(start, R)], sems.at[d]))
        copies[-1].start()
    for copy in copies:
        copy.wait()


def unpack(side, measured, mask, msgs, C, R, into=None):
    ch, _, D, W = measured.shape
    args = (measured, mask, *msgs) + (() if into is None else (into,))
    (out,) = call(
        functools.partial(unpack_kernel, C, R, side),
        "unpack_mirrored" if side else "unpack_own",
        args,
        [jax.ShapeDtypeStruct(measured.shape, F32)],
        [pltpu.VMEM((C, ch, R, D, W), F32), pltpu.SemaphoreType.DMA((C,))],
        far=() if into is None else (len(args) - 1,),
        out=ANY,
        input_output_aliases={} if into is None else {len(args) - 1: 0},
    )
    return out


def on_device(measured, mask, kernel):
    Z, C, X = (lax.axis_size(axis) for axis in AXES)
    every = [(z, c, x) for z in range(Z) for c in range(C) for x in range(X)]

    def index(z, c, x):
        return (z * C + c) * X + x

    def send(array, target):
        pairs = [(index(*p), index(*target(*p))) for p in every if target(*p) is not None]
        return lax.ppermute(array, AXES, pairs)

    def exchange(msgs):
        got = list(msgs)
        for d in range(C):
            got[2 * d + 1] = send(msgs[2 * d + 1], lambda z, c, x: (Z - 1 - z, c ^ d, X - 1 - x))
        for d in range(1, C):
            got[2 * d] = send(msgs[2 * d], lambda z, c, x: (z, c ^ d, x))
        return got

    def plane_a(z, c, x):
        return (z ^ 1, c, x)

    def plane_b(z, c, x):
        other = z + 1 if z % 2 else z - 1
        if {z, other} == {Z // 2 - 1, Z // 2}:
            return (z, C - 1 - c, X - 1 - x)
        return (other, c, x) if 0 <= other < Z else (z, c, X - 1 - x)

    def row_a(z, c, x):
        return (z, c ^ 1, x)

    def row_b(z, c, x):
        other = c + 1 if c % 2 else c - 1
        if 0 <= other < C:
            return (z, other, x)
        if is_upper(z, x, Z) == (other < 0):
            return (Z - 1 - z, c, X - 1 - x)
        return (z, C - 1 - c, X - 1 - x)

    parts, coils, rows, D, W = measured.shape
    R = rows // (2 * C)
    half = parts * coils * C
    flat = measured.reshape(parts * coils, rows, D, W)
    z, c, _ = place()
    z_odd, c_odd = z % 2 == 1, c % 2 == 1

    taps, _, _, inputs = kernel.shape
    (folded,) = call(
        fold_kernel, "fold", (kernel,), [jax.ShapeDtypeStruct((taps, parts, coils // 2, 2 * inputs), F32)]
    )
    msgs = pack(flat, mask, C, R)
    folded, *msgs = lax.optimization_barrier((folded, *msgs))
    msgs = exchange(msgs)
    folded = [folded] + [send(folded, lambda z, c, x: (z, c ^ d, x)) for d in range(1, C)]
    weights = build_weights(C, folded, coils * C)
    state, marks, face_a, face_b = points(weights[0], msgs, C, R, D, W, half)
    full = jax.ShapeDtypeStruct(state.shape, F32)
    face = jax.ShapeDtypeStruct(face_a.shape, F32)
    early = max(R // 4, 1)
    sizes = (R, D, W)

    def padded(count):
        return [pltpu.VMEM((count + 2, (D + 2) * W, 2 * half), BF16)] * 2

    for step in range(ITERS):
        got_a, got_b = send(face_a, plane_a), send(face_b, plane_b)
        part = jax.ShapeDtypeStruct((early, D * W, 2 * half), F32)
        (top,) = call(functools.partial(upper_kernel, *sizes), "upper", (state, *weights), [part], padded(early))
        got_a, got_b, top = lax.optimization_barrier((got_a, got_b, top))
        got_b = jnp.where((z == 0) | (z == Z - 1), 0.0, got_b)
        before, after = jnp.where(z_odd, got_a, got_b), jnp.where(z_odd, got_b, got_a)

        def row(i):
            return jnp.concatenate([before[i * W : (i + 1) * W], state[i], after[i * W : (i + 1) * W]], 0)

        first, final = row(0), row(R - 1)
        near = send(jnp.where(c_odd, first, final), row_a)
        far = send(jnp.where(c_odd, final, first), row_b)
        (main,) = call(
            functools.partial(lower_kernel, *sizes),
            "lower",
            (state, top, before, after, *weights),
            [full],
            padded(R - early),
        )
        if step < ITERS - 1:
            state, face_a, face_b = call(
                functools.partial(middle_kernel, D, W),
                "middle",
                (state, marks, main, near, far, *weights),
                [full, face, face],
            )
    message = jax.ShapeDtypeStruct((2 * half // (2 * C) * D, R * W), F32)
    msgs = call(
        functools.partial(last_kernel, C, D, W),
        "last",
        (main, near, far, *weights),
        [message] * (2 * C),
        [pltpu.VMEM((2 * half * D, R * W), F32)],
    )
    msgs = exchange(msgs)
    out = unpack(0, flat, mask, msgs[0::2], C, R)
    return unpack(1, flat, mask, msgs[1::2], C, R, out).reshape(measured.shape)


def solution(mesh):
    placed = (
        P(None, ("grp", "coil"), "kx", "kz", None),
        P(("grp", "kx"), "kz", None),
        P(None, None, "coil", None),
    )
    return jax.shard_map(
        on_device,
        mesh=mesh,
        in_specs=placed,
        out_specs=P(None, ("grp", "coil"), "kx", "kz", None),
        check_vma=False,
    )
```

time: 734 us -> 66.1 us (0.09)
  waiting for transfers between devices: 398 us -> 27.9 us
  local copies, waits for them, and re-layouts: 196 us -> 3.5 us
  other arithmetic: 55.1 us -> 0.08 us
  matrix products: 37.5 us -> 0 us
  Pallas kernels: 0 us -> 17 us
  between operations: 13.7 us -> 0.19 us
  starting transfers between devices: 27 us -> 16.7 us
    ppermute x14 -> x15, waiting for transfers between devices: 291 us -> 27.9 us  [send(): return lax.ppermute(array, AXES, pairs)]
    all_gather x4 -> x0, waiting for transfers between devices: 107 us -> none  [the longest x2 107 us: on_device(): lax.all_gather(own_virtual, 'coil', axis=1, tiled=True)]
    squeeze x21 -> x2, local copies, waits for them, and re-layouts: 74.1 us -> 0.04 us  [row(): state[i]]
    dot_general x6 -> x0, matrix products: 37.5 us -> none  [convolve(): products = jnp.dot(group, window, precision=lax.Precision.HIGHEST)]
    slice x8 -> x3, local copies, waits for them, and re-layouts: 30.7 us -> 0.02 us  [the longest x2 0.01 us: row(): before[i * W:(i + 1) * W]]
    concatenate x4 -> x0, local copies, waits for them, and re-layouts: 25.1 us -> none  [on_device(): stacked = jnp.concatenate([physical, virtual], 1)]
    add x2 -> x0, other arithmetic: 23.2 us -> none  [convolve(): result = result + products[3 * second + third, :, offset:offset + length]]
    unnamed x26 -> x10, local copies, waits for them, and re-layouts: 26.3 us -> 3.45 us
  transfers between devices with their start and end apart: 18 -> 15, of which waited for: 13 -> 12; matrix products, arithmetic and copies ran while one was open for 5% -> 0% of each run, Pallas kernels for 0% -> 17%
where the time goes in v2:
time: 66.1 us; the launch traced here: 65.4 us
  waiting for transfers between devices  27.9 us (42%)
  Pallas kernels  17 us (26%)
  starting transfers between devices  16.7 us (25%)
  local copies, waits for them, and re-layouts  3.5 us (5%)
    ppermute x15, waiting for transfers between devices, send(): return lax.ppermute(array, AXES, pairs)  27.9 us
    pallas_call x12, Pallas kernels, call(): pl.pallas_call(body, out_shape=shapes, in_specs=[space if i in far else V...  17 us
    ppermute x15, starting transfers between devices, send(): return lax.ppermute(array, AXES, pairs)  16.7 us
    unnamed x10, local copies, waits for them, and re-layouts  3.45 us
  transfers between devices with their start and end apart: 15, of which 12 were waited for; matrix products, arithmetic and copies ran while one was open for 0% of the time, Pallas kernels for 17%

profile of v2, /device:TPU:9, one launch (start us, length us, event | category | flops | bytes accessed | tf_op | source)
XLA Modules:
  0.0 65.4 jit_solution(4867066132776008574)
XLA Ops:
  0.0 0.0 copy-start.4
  0.0 1.0 %copy-done.4 = f32[27,2,16,64]{3,2,1,0:T(8,128)S(1)} copy-done((f32[27,2,16,64]{3,2,1,0:T(8,128)S(1)}, f32[27,2,16,64]{3,2,1,0:T(8,128)}, u32[]{:S(2)}) %copy-start.4) | copy-done | bytes 221208
  1.0 0.1 fold.1.refs_0_
  1.1 0.0 copy-start
  1.2 1.6 %copy-done = f32[2,16,16,8,32]{4,3,2,1,0:T(8,128)S(1)} copy-done((f32[2,16,16,8,32]{4,3,2,1,0:T(8,128)S(1)}, f32[2,16,16,8,32]{4,3,2,1,0:T(8,128)}, u32[]{:S(2)}) %copy-start) | copy-done | bytes 524312
  2.7 0.0 copy-start.2
  2.7 0.8 %copy-done.2 = s32[16,8,32]{2,1,0:T(8,128)S(1)} copy-done((s32[16,8,32]{2,1,0:T(8,128)S(1)}, s32[16,8,32]{2,1,0:T(8,128)}, u32[]{:S(2)}) %copy-start.2) | copy-done | bytes 16408
  3.6 1.0 %pack.1 = (f32[264,128]{1,0:T(8,128)S(1)}, f32[264,128]{1,0:T(8,128)S(1)}, f32[256,128]{1,0:T(8,128)S(1)}, f32[256,128]{1,0:T(8,128)S(1)}) custom-call(f32[32,16,8,32]{3,2,1,0:T(8,128)S(1)} %bitcast.10, s32[16,8,32]{2,1,0:T(8,128)S(1)} %copy-done.2), custom_call_target="tpu_custom_call" | custom-call | tf_op jit(solution)/shard_map/pack/pallas_call | solution.py:21
  4.6 1.3 %collective-permute-start = (f32[27,2,8,128]{3,2,1,0:T(8,128)S(1)}, f32[27,2,8,128]{3,2,1,0:T(8,128)S(1)}, u32[]{:S(2)}, u32[]{:S(2)}) collective-permute-start(f32[27,2,8,128]{3,2,1,0:T(8,128)S(1)} %fold.1.refs_0_), channel_id=1, source_target_pairs={{0,2},{1,3},{2,0},{3,1},{4,6},{5,7},{6,4},{7,5},{8,10},{9,11},{10,... | collective-permute-start | bytes 663560 | tf_op jit(solution)/shard_map/ppermute | solution.py:356
  5.8 2.1 %collective-permute-start.1 = (f32[264,128]{1,0:T(8,128)S(1)}, f32[264,128]{1,0:T(8,128)S(1)}, u32[]{:S(2)}, u32[]{:S(2)}) collective-permute-start(f32[264,128]{1,0:T(8,128)S(1)} %get-tuple-element.40), channel_id=1, source_target_pairs={{0,13},{1,12},{2,15},{3,14},{4,9},{5,8},{6,11},{7,10},{8,5},{9,4},... | collective-permute-start | bytes 405512 | tf_op jit(solution)/shard_map/ppermute | solution.py:356
  8.0 0.3 collective-permute-start.2
  8.2 1.2 %collective-permute-start.3 = (f32[256,128]{1,0:T(8,128)S(1)}, f32[256,128]{1,0:T(8,128)S(1)}, u32[]{:S(2)}, u32[]{:S(2)}) collective-permute-start(f32[256,128]{1,0:T(8,128)S(1)} %get-tuple-element.42), channel_id=1, source_target_pairs={{0,15},{1,14},{2,13},{3,12},{4,11},{5,10},{6,9},{7,8},{8,7},{9,6},... | collective-permute-start | bytes 393224 | tf_op jit(solution)/shard_map/ppermute | solution.py:356
  9.4 1.5 %collective-permute-done.refs_1_ = f32[27,2,8,128]{3,2,1,0:T(8,128)S(1)} collective-permute-done((f32[27,2,8,128]{3,2,1,0:T(8,128)S(1)}, f32[27,2,8,128]{3,2,1,0:T(8,128)S(1)}, u32[]{:S(2)}, u32[]{:S(2)}) %collective-permute-start) | collective-permute-done | bytes 221216 | tf_op jit(solution)/shard_map/ppermute | solution.py:356
  10.9 2.0 %weights.1 = (bf16[9,128,384]{2,1,0:T(8,128)(2,1)S(1)}, bf16[9,128,768]{2,1,0:T(8,128)(2,1)S(1)}) custom-call(f32[27,2,8,128]{3,2,1,0:T(8,128)S(1)} %fold.1.refs_0_, f32[27,2,8,128]{3,2,1,0:T(8,128)S(1)} %collective-permute-done.refs_1_), custom_call_target="tpu_custom_call" | custom-call | tf_op jit(solution)/shard_map/weights/pallas_call | solution.py:21
  12.9 0.8 %collective-permute-done.2.refs_2_ = f32[256,128]{1,0:T(8,128)S(1)} collective-permute-done((f32[256,128]{1,0:T(8,128)S(1)}, f32[256,128]{1,0:T(8,128)S(1)}, u32[]{:S(2)}, u32[]{:S(2)}) %collective-permute-start.2) | collective-permute-done | bytes 131104 | tf_op jit(solution)/shard_map/ppermute | solution.py:356
  13.7 6.9 %collective-permute-done.3.refs_3_ = f32[256,128]{1,0:T(8,128)S(1)} collective-permute-done((f32[256,128]{1,0:T(8,128)S(1)}, f32[256,128]{1,0:T(8,128)S(1)}, u32[]{:S(2)}, u32[]{:S(2)}) %collective-permute-start.3) | collective-permute-done | bytes 131104 | tf_op jit(solution)/shard_map/ppermute | solution.py:356
  20.6 0.0 collective-permute-done.1.refs_1_
  20.6 0.7 %points.1 = (f32[4,256,128]{2,1,0:T(8,128)S(1)}, f32[4,256,128]{2,1,0:T(8,128)S(1)}, f32[128,128]{1,0:T(8,128)S(1)}, f32[128,128]{1,0:T(8,128)S(1)}) custom-call(bf16[9,128,384]{2,1,0:T(8,128)(2,1)S(1)} %get-tuple-element.38.ready.single, f32[264,128]{1,0:T(8,128)S(1)} %get-tuple-element.39.refs_0_, f32[264,128]{1,0:T(8,128)S(1)} %collective-permute-done.1.refs_1_, ...), custom_call_target="tpu_custom_call" | custom-call | tf_op jit(solution)/shard_map/points/pallas_call | solution.py:21
  21.4 0.1 collective-permute-start.4
  21.4 1.6 %collective-permute-start.5 = (f32[128,128]{1,0:T(8,128)S(1)}, f32[128,128]{1,0:T(8,128)S(1)}, u32[]{:S(2)}, u32[]{:S(2)}) collective-permute-start(f32[128,128]{1,0:T(8,128)S(1)} %get-tuple-element.46), channel_id=1, source_target_pairs={{0,1},{1,0},{2,3},{3,2},{4,7},{5,6},{6,5},{7,4},{8,11},{9,10},{10,... | collective-permute-start | bytes 196616 | tf_op jit(solution)/shard_map/ppermute | solution.py:356
  23.0 1.0 %upper.2 = f32[1,256,128]{2,1,0:T(8,128)S(1)} custom-call(f32[4,256,128]{2,1,0:T(8,128)S(1)} %get-tuple-element.43.x, bf16[9,128,384]{2,1,0:T(8,128)(2,1)S(1)} %get-tuple-element.38.ready.single, bf16[9,128,768]{2,1,0:T(8,128)(2,1)S(1)} %get-tuple-element.47.double), custom_call_target="tpu_custom_call" | custom-call | tf_op jit(solution)/shard_map/upper/pallas_call | solution.py:21
  24.1 0.8 %collective-permute-done.4 = f32[128,128]{1,0:T(8,128)S(1)} collective-permute-done((f32[128,128]{1,0:T(8,128)S(1)}, f32[128,128]{1,0:T(8,128)S(1)}, u32[]{:S(2)}, u32[]{:S(2)}) %collective-permute-start.4) | collective-permute-done | bytes 65568 | tf_op jit(solution)/shard_map/ppermute | solution.py:356
  24.8 0.9 %collective-permute-done.5 = f32[128,128]{1,0:T(8,128)S(1)} collective-permute-done((f32[128,128]{1,0:T(8,128)S(1)}, f32[128,128]{1,0:T(8,128)S(1)}, u32[]{:S(2)}, u32[]{:S(2)}) %collective-permute-start.5) | collective-permute-done | bytes 65568 | tf_op jit(solution)/shard_map/ppermute | solution.py:356
  25.8 1.6 %collective-permute-start.7 = (f32[320,128]{1,0:T(8,128)S(1)}, f32[320,128]{1,0:T(8,128)S(1)}, u32[]{:S(2)}, u32[]{:S(2)}) collective-permute-start(f32[320,128]{1,0:T(8,128)S(1)} %get-tuple-element.67), channel_id=1, source_target_pairs={{0,13},{1,2},{2,1},{3,14},{4,9},{5,6},{6,5},{7,10},{8,11},{9,4},{1... | collective-permute-start | bytes 491528 | tf_op jit(solution)/shard_map/ppermute | solution.py:356
  27.3 1.3 %collective-permute-start.6 = (f32[320,128]{1,0:T(8,128)S(1)}, f32[320,128]{1,0:T(8,128)S(1)}, u32[]{:S(2)}, u32[]{:S(2)}) collective-permute-start(f32[320,128]{1,0:T(8,128)S(1)} %get-tuple-element.68), channel_id=1, source_target_pairs={{0,2},{1,3},{2,0},{3,1},{4,6},{5,7},{6,4},{7,5},{8,10},{9,11},{10,... | collective-permute-start | bytes 491528 | tf_op jit(solution)/shard_map/ppermute | solution.py:356
  28.7 3.0 %lower.2.main = f32[4,256,128]{2,1,0:T(8,128)S(1)} custom-call(f32[4,256,128]{2,1,0:T(8,128)S(1)} %get-tuple-element.43.x, f32[1,256,128]{2,1,0:T(8,128)S(1)} %upper.2, f32[128,128]{1,0:T(8,128)S(1)} %get-tuple-element.72.before, f32[128,128]{1,0:T(8,128)S(1)} %get-tuple-element.71.after, bf16[9,128,384]{2,1,0:T(8,128)(2,1)S(1)} %get-tuple-element.38.ready.single, ...), custom_call_target="tpu_custom_call" | custom-call | tf_op jit(solution)/shard_map/lower/pallas_call | solution.py:21
  31.7 0.0 collective-permute-done.7.far
  31.7 1.8 %collective-permute-done.6.near = f32[320,128]{1,0:T(8,128)S(1)} collective-permute-done((f32[320,128]{1,0:T(8,128)S(1)}, f32[320,128]{1,0:T(8,128)S(1)}, u32[]{:S(2)}, u32[]{:S(2)}) %collective-permute-start.6) | collective-permute-done | bytes 163872 | tf_op jit(solution)/shard_map/ppermute | solution.py:356
  33.5 1.4 %middle.1 = (f32[4,256,128]{2,1,0:T(8,128)S(1)}, f32[128,128]{1,0:T(8,128)S(1)}, f32[128,128]{1,0:T(8,128)S(1)}) custom-call(f32[4,256,128]{2,1,0:T(8,128)S(1)} %get-tuple-element.43.x, f32[4,256,128]{2,1,0:T(8,128)S(1)} %get-tuple-element.44.marks, f32[4,256,128]{2,1,0:T(8,128)S(1)} %lower.2.main, f32[320,128]{1,0:T(8,128)S(1)} %collective-permute-done.6.near, ...), custom_call_target="tpu_custom_call" | custom-call | tf_op jit(solution)/shard_map/middle/pallas_call | solution.py:21
  34.9 0.5 collective-permute-start.8
  35.4 0.8 %collective-permute-start.9 = (f32[128,128]{1,0:T(8,128)S(1)}, f32[128,128]{1,0:T(8,128)S(1)}, u32[]{:S(2)}, u32[]{:S(2)}) collective-permute-start(f32[128,128]{1,0:T(8,128)S(1)} %get-tuple-element.53), channel_id=1, source_target_pairs={{0,1},{1,0},{2,3},{3,2},{4,7},{5,6},{6,5},{7,4},{8,11},{9,10},{10,... | collective-permute-start | bytes 196616 | tf_op jit(solution)/shard_map/ppermute | solution.py:356
  36.2 1.0 %upper.3 = f32[1,256,128]{2,1,0:T(8,128)S(1)} custom-call(f32[4,256,128]{2,1,0:T(8,128)S(1)} %get-tuple-element.51.x, bf16[9,128,384]{2,1,0:T(8,128)(2,1)S(1)} %get-tuple-element.38.ready.single, bf16[9,128,768]{2,1,0:T(8,128)(2,1)S(1)} %get-tuple-element.47.double), custom_call_target="tpu_custom_call" | custom-call | tf_op jit(solution)/shard_map/upper/pallas_call | solution.py:21
  37.2 0.9 %collective-permute-done.8 = f32[128,128]{1,0:T(8,128)S(1)} collective-permute-done((f32[128,128]{1,0:T(8,128)S(1)}, f32[128,128]{1,0:T(8,128)S(1)}, u32[]{:S(2)}, u32[]{:S(2)}) %collective-permute-start.8) | collective-permute-done | bytes 65568 | tf_op jit(solution)/shard_map/ppermute | solution.py:356
  38.1 1.7 %collective-permute-done.9 = f32[128,128]{1,0:T(8,128)S(1)} collective-permute-done((f32[128,128]{1,0:T(8,128)S(1)}, f32[128,128]{1,0:T(8,128)S(1)}, u32[]{:S(2)}, u32[]{:S(2)}) %collective-permute-start.9) | collective-permute-done | bytes 65568 | tf_op jit(solution)/shard_map/ppermute | solution.py:356
  39.9 1.1 %collective-permute-start.11 = (f32[320,128]{1,0:T(8,128)S(1)}, f32[320,128]{1,0:T(8,128)S(1)}, u32[]{:S(2)}, u32[]{:S(2)}) collective-permute-start(f32[320,128]{1,0:T(8,128)S(1)} %get-tuple-element.65), channel_id=1, source_target_pairs={{0,13},{1,2},{2,1},{3,14},{4,9},{5,6},{6,5},{7,10},{8,11},{9,4},{1... | collective-permute-start | bytes 491528 | tf_op jit(solution)/shard_map/ppermute | solution.py:356
  41.0 2.0 %collective-permute-start.10 = (f32[320,128]{1,0:T(8,128)S(1)}, f32[320,128]{1,0:T(8,128)S(1)}, u32[]{:S(2)}, u32[]{:S(2)}) collective-permute-start(f32[320,128]{1,0:T(8,128)S(1)} %get-tuple-element.66), channel_id=1, source_target_pairs={{0,2},{1,3},{2,0},{3,1},{4,6},{5,7},{6,4},{7,5},{8,10},{9,11},{10,... | collective-permute-start | bytes 491528 | tf_op jit(solution)/shard_map/ppermute | solution.py:356
  43.0 3.0 %lower.3.main = f32[4,256,128]{2,1,0:T(8,128)S(1)} custom-call(f32[4,256,128]{2,1,0:T(8,128)S(1)} %get-tuple-element.51.x, f32[1,256,128]{2,1,0:T(8,128)S(1)} %upper.3, f32[128,128]{1,0:T(8,128)S(1)} %get-tuple-element.70.before, f32[128,128]{1,0:T(8,128)S(1)} %get-tuple-element.69.after, bf16[9,128,384]{2,1,0:T(8,128)(2,1)S(1)} %get-tuple-element.38.ready.single, ...), custom_call_target="tpu_custom_call" | custom-call | tf_op jit(solution)/shard_map/lower/pallas_call | solution.py:21
  46.0 0.0 copy-start.1
  46.0 0.0 copy-start.3
  46.0 0.0 collective-permute-done.11.far
  46.1 1.7 %collective-permute-done.10.near = f32[320,128]{1,0:T(8,128)S(1)} collective-permute-done((f32[320,128]{1,0:T(8,128)S(1)}, f32[320,128]{1,0:T(8,128)S(1)}, u32[]{:S(2)}, u32[]{:S(2)}) %collective-permute-start.10) | collective-permute-done | bytes 163872 | tf_op jit(solution)/shard_map/ppermute | solution.py:356
  47.8 1.4 %last.1 = (f32[256,128]{1,0:T(8,128)S(1)}, f32[256,128]{1,0:T(8,128)S(1)}, f32[256,128]{1,0:T(8,128)S(1)}, f32[256,128]{1,0:T(8,128)S(1)}) custom-call(f32[4,256,128]{2,1,0:T(8,128)S(1)} %lower.3.main, f32[320,128]{1,0:T(8,128)S(1)} %collective-permute-done.10.near, f32[320,128]{1,0:T(8,128)S(1)} %collective-permute-done.11.far, ...), custom_call_target="tpu_custom_call" | custom-call | tf_op jit(solution)/shard_map/last/pallas_call | solution.py:21
  49.2 1.0 %collective-permute-start.14 = (f32[256,128]{1,0:T(8,128)S(1)}, f32[256,128]{1,0:T(8,128)S(1)}, u32[]{:S(2)}, u32[]{:S(2)}) collective-permute-start(f32[256,128]{1,0:T(8,128)S(1)} %get-tuple-element.60), channel_id=1, source_target_pairs={{0,2},{1,3},{2,0},{3,1},{4,6},{5,7},{6,4},{7,5},{8,10},{9,11},{10,... | collective-permute-start | bytes 393224 | tf_op jit(solution)/shard_map/ppermute | solution.py:356
  50.2 1.7 %collective-permute-start.12 = (f32[256,128]{1,0:T(8,128)S(1)}, f32[256,128]{1,0:T(8,128)S(1)}, u32[]{:S(2)}, u32[]{:S(2)}) collective-permute-start(f32[256,128]{1,0:T(8,128)S(1)} %get-tuple-element.57), channel_id=1, source_target_pairs={{0,13},{1,12},{2,15},{3,14},{4,9},{5,8},{6,11},{7,10},{8,5},{9,4},... | collective-permute-start | bytes 393224 | tf_op jit(solution)/shard_map/ppermute | solution.py:356
  51.9 0.3 collective-permute-start.13
  52.2 0.9 %collective-permute-done.14.refs_1_ = f32[256,128]{1,0:T(8,128)S(1)} collective-permute-done((f32[256,128]{1,0:T(8,128)S(1)}, f32[256,128]{1,0:T(8,128)S(1)}, u32[]{:S(2)}, u32[]{:S(2)}) %collective-permute-start.14) | collective-permute-done | bytes 131104 | tf_op jit(solution)/shard_map/ppermute | solution.py:356
  53.1 0.0 copy-done.1
  53.1 0.0 copy-done.3
  53.1 1.2 %unpack_own.1.refs_2_ = f32[32,16,8,32]{3,2,1,0:T(8,128)} custom-call(f32[32,16,8,32]{3,2,1,0:T(8,128)S(1)} %bitcast.11, s32[16,8,32]{2,1,0:T(8,128)S(1)} %copy-done.3, f32[256,128]{1,0:T(8,128)S(1)} %get-tuple-element.59.refs_0_, f32[256,128]{1,0:T(8,128)S(1)} %collective-permute-done.14.refs_1_), custom_call_target="tpu_custom_call" | custom-call | tf_op jit(solution)/shard_map/unpack_own/pallas_call | solution.py:21
  54.3 7.3 %collective-permute-done.12.refs_0_ = f32[256,128]{1,0:T(8,128)S(1)} collective-permute-done((f32[256,128]{1,0:T(8,128)S(1)}, f32[256,128]{1,0:T(8,128)S(1)}, u32[]{:S(2)}, u32[]{:S(2)}) %collective-permute-start.12) | collective-permute-done | bytes 131104 | tf_op jit(solution)/shard_map/ppermute | solution.py:356
  61.6 2.7 %collective-permute-done.13.refs_1_ = f32[256,128]{1,0:T(8,128)S(1)} collective-permute-done((f32[256,128]{1,0:T(8,128)S(1)}, f32[256,128]{1,0:T(8,128)S(1)}, u32[]{:S(2)}, u32[]{:S(2)}) %collective-permute-start.13) | collective-permute-done | bytes 131104 | tf_op jit(solution)/shard_map/ppermute | solution.py:356
  64.3 1.2 %unpack_mirrored.1 = f32[32,16,8,32]{3,2,1,0:T(8,128)} custom-call(f32[32,16,8,32]{3,2,1,0:T(8,128)S(1)} %bitcast.12, s32[16,8,32]{2,1,0:T(8,128)S(1)} %copy-done.3, f32[256,128]{1,0:T(8,128)S(1)} %collective-permute-done.12.refs_0_, f32[256,128]{1,0:T(8,128)S(1)} %collective-permute-done.13.refs_1_, ...), custom_call_target="tpu_custom_call", output_to_operand_aliasing={{}: (4, {})} | custom-call | tf_op jit(solution)/shard_map/unpack_mirrored/pallas_call | solution.py:21
  (9 shorter events, 0.1 us)
Async XLA Ops:
  0.0 1.0 %copy-start.4 = (f32[27,2,16,64]{3,2,1,0:T(8,128)S(1)}, f32[27,2,16,64]{3,2,1,0:T(8,128)}, u32[]{:S(2)}) copy-start(f32[27,2,16,64]{3,2,1,0:T(8,128)} %kernel.1) | copy-start | bytes 663556
  1.1 1.6 %copy-start = (f32[2,16,16,8,32]{4,3,2,1,0:T(8,128)S(1)}, f32[2,16,16,8,32]{4,3,2,1,0:T(8,128)}, u32[]{:S(2)}) copy-start(f32[2,16,16,8,32]{4,3,2,1,0:T(8,128)} %param.3) | copy-start | bytes 1572868
  2.7 0.8 %copy-start.2 = (s32[16,8,32]{2,1,0:T(8,128)S(1)}, s32[16,8,32]{2,1,0:T(8,128)}, u32[]{:S(2)}) copy-start(s32[16,8,32]{2,1,0:T(8,128)} %mask.5) | copy-start | bytes 49156
  4.6 6.4 %collective-permute-start = (f32[27,2,8,128]{3,2,1,0:T(8,128)S(1)}, f32[27,2,8,128]{3,2,1,0:T(8,128)S(1)}, u32[]{:S(2)}, u32[]{:S(2)}) collective-permute-start(f32[27,2,8,128]{3,2,1,0:T(8,128)S(1)} %fold.1.refs_0_), channel_id=1, source_target_pairs={{0,2},{1,3},{2,0},{3,1},{4,6},{5,7},{6,4},{7,5},{8,10},{9,11},{10,... | collective-permute-start | bytes 663560 | tf_op jit(solution)/shard_map/ppermute | solution.py:356
  5.8 14.8 %collective-permute-start.1 = (f32[264,128]{1,0:T(8,128)S(1)}, f32[264,128]{1,0:T(8,128)S(1)}, u32[]{:S(2)}, u32[]{:S(2)}) collective-permute-start(f32[264,128]{1,0:T(8,128)S(1)} %get-tuple-element.40), channel_id=1, source_target_pairs={{0,13},{1,12},{2,15},{3,14},{4,9},{5,8},{6,11},{7,10},{8,5},{9,4},... | collective-permute-start | bytes 405512 | tf_op jit(solution)/shard_map/ppermute | solution.py:356
  8.0 5.8 %collective-permute-start.2 = (f32[256,128]{1,0:T(8,128)S(1)}, f32[256,128]{1,0:T(8,128)S(1)}, u32[]{:S(2)}, u32[]{:S(2)}) collective-permute-start(f32[256,128]{1,0:T(8,128)S(1)} %get-tuple-element.41), channel_id=1, source_target_pairs={{0,2},{1,3},{2,0},{3,1},{4,6},{5,7},{6,4},{7,5},{8,10},{9,11},{10,... | collective-permute-start | bytes 393224 | tf_op jit(solution)/shard_map/ppermute | solution.py:356
  8.2 12.4 %collective-permute-start.3 = (f32[256,128]{1,0:T(8,128)S(1)}, f32[256,128]{1,0:T(8,128)S(1)}, u32[]{:S(2)}, u32[]{:S(2)}) collective-permute-start(f32[256,128]{1,0:T(8,128)S(1)} %get-tuple-element.42), channel_id=1, source_target_pairs={{0,15},{1,14},{2,13},{3,12},{4,11},{5,10},{6,9},{7,8},{8,7},{9,6},... | collective-permute-start | bytes 393224 | tf_op jit(solution)/shard_map/ppermute | solution.py:356
  21.4 3.5 %collective-permute-start.4 = (f32[128,128]{1,0:T(8,128)S(1)}, f32[128,128]{1,0:T(8,128)S(1)}, u32[]{:S(2)}, u32[]{:S(2)}) collective-permute-start(f32[128,128]{1,0:T(8,128)S(1)} %get-tuple-element.45), channel_id=1, source_target_pairs={{0,4},{1,5},{2,6},{3,7},{4,0},{5,1},{6,2},{7,3},{8,12},{9,13},{10,... | collective-permute-start | bytes 196616 | tf_op jit(solution)/shard_map/ppermute | solution.py:356
  21.4 4.3 %collective-permute-start.5 = (f32[128,128]{1,0:T(8,128)S(1)}, f32[128,128]{1,0:T(8,128)S(1)}, u32[]{:S(2)}, u32[]{:S(2)}) collective-permute-start(f32[128,128]{1,0:T(8,128)S(1)} %get-tuple-element.46), channel_id=1, source_target_pairs={{0,1},{1,0},{2,3},{3,2},{4,7},{5,6},{6,5},{7,4},{8,11},{9,10},{10,... | collective-permute-start | bytes 196616 | tf_op jit(solution)/shard_map/ppermute | solution.py:356
  25.8 5.9 %collective-permute-start.7 = (f32[320,128]{1,0:T(8,128)S(1)}, f32[320,128]{1,0:T(8,128)S(1)}, u32[]{:S(2)}, u32[]{:S(2)}) collective-permute-start(f32[320,128]{1,0:T(8,128)S(1)} %get-tuple-element.67), channel_id=1, source_target_pairs={{0,13},{1,2},{2,1},{3,14},{4,9},{5,6},{6,5},{7,10},{8,11},{9,4},{1... | collective-permute-start | bytes 491528 | tf_op jit(solution)/shard_map/ppermute | solution.py:356
  27.3 6.2 %collective-permute-start.6 = (f32[320,128]{1,0:T(8,128)S(1)}, f32[320,128]{1,0:T(8,128)S(1)}, u32[]{:S(2)}, u32[]{:S(2)}) collective-permute-start(f32[320,128]{1,0:T(8,128)S(1)} %get-tuple-element.68), channel_id=1, source_target_pairs={{0,2},{1,3},{2,0},{3,1},{4,6},{5,7},{6,4},{7,5},{8,10},{9,11},{10,... | collective-permute-start | bytes 491528 | tf_op jit(solution)/shard_map/ppermute | solution.py:356
  34.9 3.2 %collective-permute-start.8 = (f32[128,128]{1,0:T(8,128)S(1)}, f32[128,128]{1,0:T(8,128)S(1)}, u32[]{:S(2)}, u32[]{:S(2)}) collective-permute-start(f32[128,128]{1,0:T(8,128)S(1)} %get-tuple-element.52), channel_id=1, source_target_pairs={{0,4},{1,5},{2,6},{3,7},{4,0},{5,1},{6,2},{7,3},{8,12},{9,13},{10,... | collective-permute-start | bytes 196616 | tf_op jit(solution)/shard_map/ppermute | solution.py:356
  35.4 4.5 %collective-permute-start.9 = (f32[128,128]{1,0:T(8,128)S(1)}, f32[128,128]{1,0:T(8,128)S(1)}, u32[]{:S(2)}, u32[]{:S(2)}) collective-permute-start(f32[128,128]{1,0:T(8,128)S(1)} %get-tuple-element.53), channel_id=1, source_target_pairs={{0,1},{1,0},{2,3},{3,2},{4,7},{5,6},{6,5},{7,4},{8,11},{9,10},{10,... | collective-permute-start | bytes 196616 | tf_op jit(solution)/shard_map/ppermute | solution.py:356
  39.9 6.1 %collective-permute-start.11 = (f32[320,128]{1,0:T(8,128)S(1)}, f32[320,128]{1,0:T(8,128)S(1)}, u32[]{:S(2)}, u32[]{:S(2)}) collective-permute-start(f32[320,128]{1,0:T(8,128)S(1)} %get-tuple-element.65), channel_id=1, source_target_pairs={{0,13},{1,2},{2,1},{3,14},{4,9},{5,6},{6,5},{7,10},{8,11},{9,4},{1... | collective-permute-start | bytes 491528 | tf_op jit(solution)/shard_map/ppermute | solution.py:356
  41.0 6.8 %collective-permute-start.10 = (f32[320,128]{1,0:T(8,128)S(1)}, f32[320,128]{1,0:T(8,128)S(1)}, u32[]{:S(2)}, u32[]{:S(2)}) collective-permute-start(f32[320,128]{1,0:T(8,128)S(1)} %get-tuple-element.66), channel_id=1, source_target_pairs={{0,2},{1,3},{2,0},{3,1},{4,6},{5,7},{6,4},{7,5},{8,10},{9,11},{10,... | collective-permute-start | bytes 491528 | tf_op jit(solution)/shard_map/ppermute | solution.py:356
  46.0 7.1 %copy-start.1 = (f32[2,16,16,8,32]{4,3,2,1,0:T(8,128)S(1)}, f32[2,16,16,8,32]{4,3,2,1,0:T(8,128)}, u32[]{:S(2)}) copy-start(f32[2,16,16,8,32]{4,3,2,1,0:T(8,128)} %param.3) | copy-start | bytes 1572868
  46.0 7.1 %copy-start.3 = (s32[16,8,32]{2,1,0:T(8,128)S(1)}, s32[16,8,32]{2,1,0:T(8,128)}, u32[]{:S(2)}) copy-start(s32[16,8,32]{2,1,0:T(8,128)} %mask.5) | copy-start | bytes 49156
  49.2 3.9 %collective-permute-start.14 = (f32[256,128]{1,0:T(8,128)S(1)}, f32[256,128]{1,0:T(8,128)S(1)}, u32[]{:S(2)}, u32[]{:S(2)}) collective-permute-start(f32[256,128]{1,0:T(8,128)S(1)} %get-tuple-element.60), channel_id=1, source_target_pairs={{0,2},{1,3},{2,0},{3,1},{4,6},{5,7},{6,4},{7,5},{8,10},{9,11},{10,... | collective-permute-start | bytes 393224 | tf_op jit(solution)/shard_map/ppermute | solution.py:356
  50.2 11.4 %collective-permute-start.12 = (f32[256,128]{1,0:T(8,128)S(1)}, f32[256,128]{1,0:T(8,128)S(1)}, u32[]{:S(2)}, u32[]{:S(2)}) collective-permute-start(f32[256,128]{1,0:T(8,128)S(1)} %get-tuple-element.57), channel_id=1, source_target_pairs={{0,13},{1,12},{2,15},{3,14},{4,9},{5,8},{6,11},{7,10},{8,5},{9,4},... | collective-permute-start | bytes 393224 | tf_op jit(solution)/shard_map/ppermute | solution.py:356
  51.9 12.4 %collective-permute-start.13 = (f32[256,128]{1,0:T(8,128)S(1)}, f32[256,128]{1,0:T(8,128)S(1)}, u32[]{:S(2)}, u32[]{:S(2)}) collective-permute-start(f32[256,128]{1,0:T(8,128)S(1)} %get-tuple-element.58), channel_id=1, source_target_pairs={{0,15},{1,14},{2,13},{3,12},{4,11},{5,10},{6,9},{7,8},{8,7},{9,6},... | collective-permute-start | bytes 393224 | tf_op jit(solution)/shard_map/ppermute | solution.py:356

commit v3 on v0

v3 whole, which is shorter than its diff:
```python
import functools

import jax
import jax.numpy as jnp
from jax import lax
from jax.experimental import pallas as pl
from jax.experimental.pallas import tpu as pltpu
from jax.sharding import PartitionSpec as P

ITERS = 2
AXES = ("kz", "coil", "kx")
F32 = jnp.float32
BF16 = jnp.bfloat16
PARAMS = pltpu.CompilerParams(vmem_limit_bytes=48 << 20)
ANY = pl.BlockSpec(memory_space=pl.ANY)
HBM = pl.BlockSpec(memory_space=pltpu.HBM)
VMEM = pl.BlockSpec(memory_space=pltpu.VMEM)


def call(body, name, args, shapes, scratch=(), far=(), space=ANY, out=VMEM, **options):
    return pl.pallas_call(
        body,
        out_shape=shapes,
        in_specs=[space if i in far else VMEM for i in range(len(args))],
        out_specs=[out] * len(shapes),
        scratch_shapes=list(scratch),
        compiler_params=PARAMS,
        name=name,
        **options,
    )(*args)


def split(x):
    hi = x.astype(BF16)
    return hi, (x - hi.astype(F32)).astype(BF16)


def reversal(n):
    row = lax.broadcasted_iota(jnp.int32, (n, n), 0)
    column = lax.broadcasted_iota(jnp.int32, (n, n), 1)
    return jnp.where(row + column == n - 1, 1.0, 0.0).astype(BF16)


def dot(a, b):
    return jnp.dot(a, b, preferred_element_type=F32)


class Cut:
    def __init__(self, rows, D, W, C, channels):
        self.rows, self.D, self.W, self.C = rows, D, W, C
        self.channels = channels
        self.half = channels // 2
        self.ch = self.half // C
        self.G = rows // C
        self.S = min(rows, self.G + (2 if C == 2 else 4))
        self.H = W // 2
        self.V = self.H + 2
        self.base = 128 // self.H
        self.spare = (self.S - self.base) * self.H
        self.part = self.ch // 2 * D
        self.slots = self.S + 2
        self.pitch = -(-(self.V + 1) // 8) * 8

    def piece(self, d=0):
        c, x = lax.bitwise_xor(lax.axis_index("coil"), d), lax.axis_index("kx")
        return jnp.where(x == 0, c, self.C - 1 - c)

    def start(self, d=0):
        return jnp.clip(self.G * self.piece(d) - 2, 0, self.rows - self.S)

    def range_of(self, last):
        own = self.G * self.piece() - self.start()
        if last:
            return own, self.G
        count = min(self.S, self.G + (1 if self.C == 2 else 2))
        return jnp.clip(own - 1, 0, self.S - count), count


def place():
    return tuple(lax.axis_index(axis) for axis in AXES)


def arrangement(cut):
    S, H, W = cut.S, cut.H, cut.W
    shift = H.bit_length() - 1
    j = lax.broadcasted_iota(jnp.int32, (1, 384), 1)
    own = j - jnp.where(j >= 320, 320, jnp.where(j >= 256, 256, jnp.where(j >= 128, 128, 0)))
    spare = j >= 256
    row = lax.shift_right_logical(own, shift)
    main = row * W + lax.bitwise_and(own, H - 1)
    rest = own - cut.spare
    edge = lax.shift_right_logical(rest, 1) * W + H + lax.bitwise_and(rest, 1)
    source = jnp.where(spare, jnp.where(own < cut.spare, main + cut.base * W, edge), main)
    mirrored = jnp.logical_or(jnp.logical_and(j >= 128, j < 256), j >= 320)
    source = jnp.where(mirrored, S * W - 1 - source, source)
    source = jnp.where(jnp.logical_and(spare, rest >= 2 * S), -1, source)
    lane = lax.broadcasted_iota(jnp.int32, (S * W, 384), 0)
    return jnp.where(lane == source, 1.0, 0.0).astype(BF16)


def pack_kernel(cut, measured, mask, *refs):
    C, S, ch, D, W = cut.C, cut.S, cut.ch, cut.D, cut.W
    outs, (rows, marks, sems) = refs[: 2 * C], refs[2 * C :]
    copies = [pltpu.make_async_copy(mask, marks, sems.at[C])]
    for d in range(C):
        copies.append(pltpu.make_async_copy(measured.at[:, pl.ds(cut.start(d), S)], rows.at[d], sems.at[d]))
    for copy in copies:
        copy.start()
    order = arrangement(cut)
    copies[0].wait()
    for d in range(C):
        copies[d + 1].wait()
        sampled = [marks[cut.start(d) + j] == 1 for j in range(S)]
        kept = [jnp.where(sampled[j][None], rows[d, :, j], 0.0) for j in range(S)]
        kept = jnp.concatenate(kept, -1).reshape(ch * D, S * W)
        if d == 0:
            kept = jnp.concatenate([kept, jnp.concatenate([jnp.where(s, 1.0, 0.0) for s in sampled], -1)], 0)
        hi, lo = split(kept)
        y = dot(hi, order) + dot(lo, order)
        part = cut.part
        for side in range(2):
            out = outs[2 * d + side]
            spare = y[:, 256 + 64 * side : 320 + 64 * side]
            out[: 2 * part] = y[: 2 * part, 128 * side : 128 * side + 128]
            out[2 * part : 3 * part] = jnp.concatenate([spare[:part], spare[part : 2 * part]], 1)
            if d == 0:
                out[3 * part : 3 * part + D] = y[2 * part :, 128 * side : 128 * side + 128]
                out[3 * part + D :] = jnp.concatenate([spare[2 * part :], jnp.zeros((D, 64), F32)], 1)


def pack(measured, mask, cut):
    shapes = []
    for d in range(cut.C):
        shapes += [jax.ShapeDtypeStruct((3 * cut.part + (2 * cut.D if d == 0 else 0), 128), F32)] * 2
    scratch = [
        pltpu.VMEM((cut.C, cut.ch, cut.S, cut.D, cut.W), F32),
        pltpu.VMEM(mask.shape, jnp.int32),
        pltpu.SemaphoreType.DMA((cut.C + 1,)),
    ]
    return call(functools.partial(pack_kernel, cut), "pack", (measured, mask), shapes, scratch, far=(0, 1), space=HBM)


def fold_kernel(kernel, out):
    half = kernel.shape[2] // 2
    out[...] = jnp.concatenate([kernel[:, :, :half], kernel[:, :, half:]], -1)


def weights_kernel(C, *refs):
    folded, (single, double, kernel) = refs[:C], refs[C:]
    taps, _, coils, inputs = kernel.shape
    half = folded[0].shape[2]
    for d in range(C):
        start = pl.multiple_of(lax.bitwise_xor(lax.axis_index("coil"), d) * 2 * half, 2 * half)
        kernel[:, :, pl.ds(start, half)] = folded[d][..., :inputs]
        kernel[:, :, pl.ds(start + half, half)] = folded[d][..., inputs:]

    def parts(tap):
        re, im = kernel[tap, 0], kernel[tap, 1]
        return re[:, :coils], im[:, :coils], re[:, coils:], im[:, coils:]

    N = 4 * coils
    for t in range(taps):
        pr, pi, vr, vi = parts(t)
        qr, qi, ur, ui = parts(taps - 1 - t)
        block = jnp.concatenate(
            [
                jnp.concatenate([pr, -pi, vr, vi], 1),
                jnp.concatenate([pi, pr, vi, -vr], 1),
                jnp.concatenate([ur, ui, qr, -qi], 1),
                jnp.concatenate([ui, -ur, qi, qr], 1),
            ],
            0,
        ).T
        hi, lo = split(block)
        e, tap = t % 3, t // 3
        single[tap, :, e * N : (e + 1) * N] = hi
        double[tap, :, 2 * e * N : (2 * e + 1) * N] = hi
        double[tap, :, (2 * e + 1) * N : (2 * e + 2) * N] = lo


def build_weights(C, folded, coils):
    taps, parts, _, inputs = folded[0].shape
    N = 4 * coils
    shapes = [jax.ShapeDtypeStruct((9, N, 3 * N), BF16), jax.ShapeDtypeStruct((9, N, 6 * N), BF16)]
    scratch = [pltpu.VMEM((taps, parts, coils, inputs // 2), F32)]
    return call(functools.partial(weights_kernel, C), "weights", folded, shapes, scratch)


def middle_row(cut, x):
    return jnp.where(lax.axis_index("kx") == 0, x[cut.S - 1], x[0])


def points_kernel(cut, ready, *refs):
    C, D, H, S, half = cut.C, cut.D, cut.H, cut.S, cut.half
    msgs, (x, marks, middle, main, spare) = refs[: 2 * C], refs[2 * C :]
    part = cut.part
    for d in range(C):
        other = lax.bitwise_xor(lax.axis_index("coil"), d)
        for side in range(2):
            msg = msgs[2 * d + side]
            for ri in range(2):
                start = pl.multiple_of(((side * 2 + ri) * C + other) * part, part)
                main[pl.ds(start, part)] = msg[ri * part : (ri + 1) * part]
            start = pl.multiple_of((side * C + other) * part, part)
            spare[pl.ds(start, part)] = msg[2 * part : 3 * part]

    def spread(target, k, first, rest):
        for r in range(cut.base):
            target[r, pl.ds(k, H, stride=D)] = first[r * H : (r + 1) * H]
        for r in range(cut.base, S):
            target[r, pl.ds(k, H, stride=D)] = rest[(r - cut.base) * H : (r - cut.base + 1) * H]
        for r in range(S):
            place = cut.spare + 2 * r
            target[r, pl.ds(H * D + k, 2, stride=D)] = rest[place : place + 2]

    lane = lax.broadcasted_iota(jnp.int32, (128, cut.channels), 1)
    flags = [msgs[side][3 * part : 3 * part + 2 * D] for side in range(2)]
    flags = jnp.concatenate(flags + [jnp.zeros((128 - 4 * D, 128), F32)], 0).T
    for k in range(D):
        j = D - 1 - k
        mine = main[pl.ds(k, half, stride=D)]
        other = main[pl.ds(half * D + j, half, stride=D)]
        first = jnp.concatenate([mine, other], 0).T
        mine = spare[pl.ds(k, half // 2, stride=D)]
        other = spare[pl.ds(half // 2 * D + j, half // 2, stride=D)]
        rest = jnp.concatenate([mine[:, :64], mine[:, 64:], other[:, :64], other[:, 64:]], 0)
        rest = jnp.concatenate([rest, jnp.zeros_like(rest)], 1).T
        spread(x, k, first, rest)
        first = jnp.where(lane < half, flags[:, k : k + 1], flags[:, 2 * D + j : 2 * D + j + 1])
        rest = jnp.where(lane < half, flags[:, D + k : D + k + 1], flags[:, 3 * D + j : 3 * D + j + 1])
        spread(marks, k, first, rest)
    middle[...] = middle_row(cut, x)


def points(ready, msgs, cut):
    row = (cut.V * cut.D, cut.channels)
    window = jax.ShapeDtypeStruct((cut.S, *row), F32)
    return call(
        functools.partial(points_kernel, cut),
        "points",
        (ready, *msgs),
        [window, window, jax.ShapeDtypeStruct(row, F32)],
        [pltpu.VMEM((cut.channels * cut.D, 128), F32), pltpu.VMEM((cut.half * cut.D, 128), F32)],
        far=(0,),
    )


def beside(cut, middle):
    _, c, x = place()
    inner = c == cut.C - 1
    middle = middle[...]
    before = jnp.where(jnp.logical_and(inner, x == 1), middle, 0.0)
    after = jnp.where(jnp.logical_and(inner, x == 0), middle, 0.0)
    return before, after


def faces_kernel(cut, x, middle, face_a, face_b, edges):
    D, S, V = cut.D, cut.S, cut.V
    edges[0], edges[1] = beside(cut, middle)
    odd = lax.rem(lax.axis_index("kz"), 2) == 1
    for slot in range(cut.slots):
        if slot == 0:
            row = edges.at[0]
        elif slot == S + 1:
            row = edges.at[1]
        else:
            row = x.at[slot - 1]
        first, final = row[pl.ds(0, V, stride=D)], row[pl.ds(D - 1, V, stride=D)]
        face_a[slot * V : (slot + 1) * V] = jnp.where(odd, first, final)
        face_b[slot * V : (slot + 1) * V] = jnp.where(odd, final, first)


def faces(x, middle, cut):
    face = jax.ShapeDtypeStruct((cut.slots * cut.V, cut.channels), F32)
    scratch = [pltpu.VMEM((2, cut.V * cut.D, cut.channels), F32)]
    return call(functools.partial(faces_kernel, cut), "faces", (x, middle), [face, face], scratch)


def multiply(hi, lo, single, double):
    N = single.shape[-1]
    groups = double.shape[-1] // (2 * 128)
    y, z = dot(hi, double), dot(lo, single)
    N = N // groups
    return [
        y[:, 2 * e * N : (2 * e + 1) * N] + y[:, (2 * e + 1) * N : (2 * e + 2) * N] + z[:, e * N : (e + 1) * N]
        for e in range(groups)
    ]


def inside_kernel(cut, last, x, middle, single, double, out, hi, lo):
    D, S = cut.D, cut.S
    count, L, channels = out.shape
    gap = jnp.zeros((D, channels), F32)
    before, after = beside(cut, middle)
    for slot in range(cut.slots):
        row = before if slot == 0 else after if slot == S + 1 else x[slot - 1]
        high = row.astype(BF16).astype(F32)
        for ref, value in ((hi, high), (lo, row - high)):
            ref[0, slot] = jnp.concatenate([gap, value[:-D]], 0).astype(BF16)
            ref[1, slot] = value.astype(BF16)
            ref[2, slot] = jnp.concatenate([value[D:], gap], 0).astype(BF16)
    first, _ = cut.range_of(last)

    def window(ref):
        return jnp.concatenate(
            [
                jnp.concatenate([ref[b, first + i + a, :L] for i in range(count)], 0)
                for a in range(3)
                for b in range(3)
            ],
            1,
        )

    K = 9 * channels
    y = multiply(window(hi), window(lo), single[...].reshape(K, -1), double[...].reshape(K, -1))
    rows = lax.broadcasted_iota(jnp.int32, (count * L, channels), 0) % D
    later = jnp.where(rows == 0, 0.0, pltpu.roll(y[0], 1, 0))
    sooner = jnp.where(rows == D - 1, 0.0, pltpu.roll(y[2], count * L - 1, 0))
    out[...] = (y[1] + later + sooner).reshape(count, L, channels)


def inside(x, middle, weights, cut, last):
    count = cut.range_of(last)[1]
    L = (cut.H if last else cut.V) * cut.D
    out = jax.ShapeDtypeStruct((count, L, cut.channels), F32)
    scratch = [pltpu.VMEM((3, cut.slots, cut.V * cut.D, cut.channels), BF16)] * 2
    return call(functools.partial(inside_kernel, cut, last), "inside", (x, middle, *weights), [out], scratch)[0]


def add_planes(cut, last, target, offset, count, got_a, got_b, single, double, planes):
    D, V, pitch = cut.D, cut.V, cut.pitch
    z, Z = lax.axis_index("kz"), lax.axis_size("kz")
    odd = lax.rem(z, 2) == 1
    ends = jnp.logical_or(z == 0, z == Z - 1)
    first, _ = cut.range_of(last)
    height = -(-count * pitch // 16) * 16
    width = cut.H if last else V
    N, K = cut.channels, 9 * cut.channels
    got_a, got_b = got_a[...], jnp.where(ends, 0.0, got_b[...])
    for e, k, plane in ((0, 0, jnp.where(odd, got_a, got_b)), (2, D - 1, jnp.where(odd, got_b, got_a))):
        planes[...] = jnp.zeros_like(planes)
        for slot in range(cut.slots):
            column = plane[slot * V : (slot + 1) * V]
            for b in range(3):
                place = 8 + slot * pitch + 1 - b
                planes[b, place : place + V] = column
        parts = [
            split(planes[b, pl.ds(pl.multiple_of(8 + (first + a) * pitch, 8), height)])
            for a in range(3)
            for b in range(3)
        ]
        hi, lo = (jnp.concatenate([part[i] for part in parts], 1) for i in range(2))
        one = single[:, :, e * N : (e + 1) * N].reshape(K, N)
        two = double[:, :, 2 * e * N : (2 * e + 2) * N].reshape(K, 2 * N)
        (y,) = multiply(hi, lo, one, two)
        for i in range(count):
            target[offset + i, pl.ds(k, width, stride=D)] += y[i * pitch : i * pitch + width]


def planes_scratch(cut):
    return pltpu.VMEM((3, 8 + cut.slots * cut.pitch + 16, cut.channels), F32)


def middle_kernel(cut, x, marks, main, got_a, got_b, single, double, out, middle, planes):
    first, count = cut.range_of(False)
    out[...] = jnp.zeros_like(out)
    for i in range(count):
        out[first + i] = main[i]
    add_planes(cut, False, out, first, count, got_a, got_b, single, double, planes)
    out[...] = jnp.where(marks[...] > 0.5, x[...], out[...])
    middle[...] = middle_row(cut, out)


def last_kernel(cut, main, got_a, got_b, single, double, *rest):
    C, D, H, G, half = cut.C, cut.D, cut.H, cut.G, cut.half
    outs, (y, stage, planes) = rest[: 2 * C], rest[2 * C :]
    y[...] = main[...]
    add_planes(cut, True, y, 0, G, got_a, got_b, single, double, planes)
    flip = reversal(G * H)
    for k in range(D):
        rows = y[:, pl.ds(k, H, stride=D)].reshape(G * H, 2 * half).T
        stage[pl.ds(k, half, stride=D)] = rows[:half]
        hi, lo = split(rows[half:])
        stage[pl.ds(half * D + D - 1 - k, half, stride=D)] = dot(hi, flip) + dot(lo, flip)
    for d in range(C):
        for side in range(2):
            for ri in range(2):
                start = ((side * 2 + ri) * C + lax.bitwise_xor(lax.axis_index("coil"), d)) * cut.part
                start = pl.multiple_of(start, cut.part)
                outs[2 * d + side][ri * cut.part : (ri + 1) * cut.part] = stage[pl.ds(start, cut.part)]


def unpack_kernel(cut, d, measured, mask, own, mirrored, *refs):
    out, rows, sem = refs[-3:]
    ch, D, G, H = cut.ch, cut.D, cut.G, cut.H
    start = cut.piece(d) * G
    own, mirrored = (msg[...].reshape(ch, D, G * H) for msg in (own, mirrored))
    for j in range(G):
        sampled = (mask[start + j] == 1)[None]
        value = jnp.concatenate([msg[:, :, j * H : (j + 1) * H] for msg in (own, mirrored)], -1)
        rows[:, j] = jnp.where(sampled, measured[:, start + j], value)
    copy = pltpu.make_async_copy(rows, out.at[:, pl.ds(start, G)], sem)
    copy.start()
    copy.wait()


def unpack(d, measured, mask, msgs, cut, into=None):
    args = (measured, mask, *msgs) + (() if into is None else (into,))
    (out,) = call(
        functools.partial(unpack_kernel, cut, d),
        "unpack",
        args,
        [jax.ShapeDtypeStruct(measured.shape, F32)],
        [pltpu.VMEM((cut.ch, cut.G, cut.D, cut.W), F32), pltpu.SemaphoreType.DMA],
        far=() if into is None else (len(args) - 1,),
        out=ANY,
        input_output_aliases={} if into is None else {len(args) - 1: 0},
    )
    return out


def on_device(measured, mask, kernel):
    Z, C, X = (lax.axis_size(axis) for axis in AXES)
    every = [(z, c, x) for z in range(Z) for c in range(C) for x in range(X)]

    def index(z, c, x):
        return (z * C + c) * X + x

    def send(array, target):
        return lax.ppermute(array, AXES, [(index(*p), index(*target(*p))) for p in every])

    def exchange(msgs):
        got = list(msgs)
        for d in range(C):
            got[2 * d + 1] = send(msgs[2 * d + 1], lambda z, c, x: (Z - 1 - z, c ^ d, X - 1 - x))
        for d in range(1, C):
            got[2 * d] = send(msgs[2 * d], lambda z, c, x: (z, c ^ d, x))
        return got

    def plane_a(z, c, x):
        return (z ^ 1, c, x)

    def plane_b(z, c, x):
        other = z + 1 if z % 2 else z - 1
        return (other, c, x) if 0 <= other < Z else (z, c, X - 1 - x)

    def core(z, c, x):
        return (z, c, X - 1 - x)

    parts, coils, rows, D, W = measured.shape
    cut = Cut(rows, D, W, C, 2 * parts * coils * C)
    flat = measured.reshape(parts * coils, rows, D, W)
    taps, _, _, inputs = kernel.shape
    msgs = pack(flat, mask, cut)
    kernel, *msgs = lax.optimization_barrier((kernel, *msgs))
    msgs = exchange(msgs)
    (folded,) = call(
        fold_kernel, "fold", (kernel,), [jax.ShapeDtypeStruct((taps, parts, coils // 2, 2 * inputs), F32)]
    )
    folded = [folded] + [send(folded, lambda z, c, x: (z, c ^ d, x)) for d in range(1, C)]
    weights = build_weights(C, folded, coils * C)
    state, marks, row = points(weights[0], msgs, cut)
    for step in range(ITERS):
        last = step == ITERS - 1
        row = send(row, core)
        face_a, face_b = faces(state, row, cut)
        got_a, got_b = send(face_a, plane_a), send(face_b, plane_b)
        main = inside(state, row, weights, cut, last)
        if not last:
            state, row = call(
                functools.partial(middle_kernel, cut),
                "middle",
                (state, marks, main, got_a, got_b, *weights),
                [jax.ShapeDtypeStruct(state.shape, F32), jax.ShapeDtypeStruct(row.shape, F32)],
                [planes_scratch(cut)],
            )
    message = jax.ShapeDtypeStruct((cut.ch * D, cut.G * cut.H), F32)
    msgs = call(
        functools.partial(last_kernel, cut),
        "last",
        (main, got_a, got_b, *weights),
        [message] * (2 * C),
        [pltpu.VMEM(main.shape, F32), pltpu.VMEM((cut.channels * D, cut.G * cut.H), F32), planes_scratch(cut)],
    )
    msgs = exchange(msgs)
    out = None
    for d in range(C):
        out = unpack(d, flat, mask, msgs[2 * d : 2 * d + 2], cut, out)
    return out.reshape(measured.shape)


def solution(mesh):
    placed = (
        P(None, ("grp", "coil"), "kx", "kz", None),
        P(("grp", "kx"), "kz", None),
        P(None, None, "coil", None),
    )
    return jax.shard_map(
        on_device,
        mesh=mesh,
        in_specs=placed,
        out_specs=P(None, ("grp", "coil"), "kx", "kz", None),
        check_vma=False,
    )
```

time: 734 us -> 61.2 us (0.08)
  waiting for transfers between devices: 398 us -> 27.4 us
  local copies, waits for them, and re-layouts: 196 us -> 2.45 us
  other arithmetic: 55.1 us -> 0 us
  matrix products: 37.5 us -> 0 us
  Pallas kernels: 0 us -> 18.5 us
  starting transfers between devices: 27 us -> 12.4 us
  between operations: 13.7 us -> 0.16 us
    ppermute x14 -> x13, waiting for transfers between devices: 291 us -> 27.4 us  [send(): lax.ppermute(array, AXES, [(index(*p), index(*target(*p))) for p in every])]
    all_gather x4 -> x0, waiting for transfers between devices: 107 us -> none  [the longest x2 107 us: on_device(): lax.all_gather(own_virtual, 'coil', axis=1, tiled=True)]
    squeeze x21 -> x0, local copies, waits for them, and re-layouts: 74.1 us -> none  [the longest x20 74.1 us: convolve(): result = result + products[3 * second + third, :, offset:offset + length]]
    dot_general x6 -> x0, matrix products: 37.5 us -> none  [convolve(): products = jnp.dot(group, window, precision=lax.Precision.HIGHEST)]
    slice x8 -> x0, local copies, waits for them, and re-layouts: 30.7 us -> none  [the longest x4 17.7 us: padded_2(): last = lax.slice_in_dim(array, length - width, length, axis=dim)]
    concatenate x4 -> x0, local copies, waits for them, and re-layouts: 25.1 us -> none  [on_device(): stacked = jnp.concatenate([physical, virtual], 1)]
    unnamed x26 -> x10, local copies, waits for them, and re-layouts: 26.3 us -> 2.45 us
    add x2 -> x0, other arithmetic: 23.2 us -> none  [convolve(): result = result + products[3 * second + third, :, offset:offset + length]]
  transfers between devices with their start and end apart: 18 -> 13, of which waited for: 13 -> 7; matrix products, arithmetic and copies ran while one was open for 5% -> 0% of each run, Pallas kernels for 0% -> 20%
where the time goes in v3:
time: 61.2 us; the launch traced here: 61 us
  waiting for transfers between devices  27.4 us (45%)
  Pallas kernels  18.5 us (30%)
  starting transfers between devices  12.4 us (20%)
  local copies, waits for them, and re-layouts  2.45 us (4%)
    ppermute x13, waiting for transfers between devices, send(): lax.ppermute(array, AXES, [(index(*p), index(*target(*p))) for p in every])  27.4 us
    pallas_call x12, Pallas kernels, call(): pl.pallas_call(body, out_shape=shapes, in_specs=[space if i in far else V...  18.5 us
    ppermute x13, starting transfers between devices, send(): lax.ppermute(array, AXES, [(index(*p), index(*target(*p))) for p in every])  12.4 us
    unnamed x10, local copies, waits for them, and re-layouts  2.45 us
  transfers between devices with their start and end apart: 13, of which 7 were waited for; matrix products, arithmetic and copies ran while one was open for 0% of the time, Pallas kernels for 20%

profile of v3, /device:TPU:9, one launch (start us, length us, event | category | flops | bytes accessed | tf_op | source)
XLA Modules:
  0.0 61.0 jit_solution(14933283965694993222)
XLA Ops:
  0.0 0.0 copy-start
  0.0 1.6 %copy-done = f32[2,16,16,8,32]{4,3,2,1,0:T(8,128)S(1)} copy-done((f32[2,16,16,8,32]{4,3,2,1,0:T(8,128)S(1)}, f32[2,16,16,8,32]{4,3,2,1,0:T(8,128)}, u32[]{:S(2)}) %copy-start) | copy-done | bytes 524312
  1.6 0.0 copy-start.2
  1.6 0.8 %copy-done.2 = s32[16,8,32]{2,1,0:T(8,128)S(1)} copy-done((s32[16,8,32]{2,1,0:T(8,128)S(1)}, s32[16,8,32]{2,1,0:T(8,128)}, u32[]{:S(2)}) %copy-start.2) | copy-done | bytes 16408
  2.4 0.0 copy-start.4
  2.4 1.7 %pack.1 = (f32[400,128]{1,0:T(8,128)S(1)}, f32[400,128]{1,0:T(8,128)S(1)}, f32[384,128]{1,0:T(8,128)S(1)}, f32[384,128]{1,0:T(8,128)S(1)}) custom-call(f32[32,16,8,32]{3,2,1,0:T(8,128)S(1)} %bitcast.2, s32[16,8,32]{2,1,0:T(8,128)S(1)} %copy-done.2), custom_call_target="tpu_custom_call" | custom-call | tf_op jit(solution)/shard_map/pack/pallas_call | solution.py:21
  4.1 0.0 copy-done.4
  4.1 0.1 fold.1.refs_0_
  4.3 1.3 %collective-permute-start = (f32[27,2,8,128]{3,2,1,0:T(8,128)S(1)}, f32[27,2,8,128]{3,2,1,0:T(8,128)S(1)}, u32[]{:S(2)}, u32[]{:S(2)}) collective-permute-start(f32[27,2,8,128]{3,2,1,0:T(8,128)S(1)} %fold.1.refs_0_), channel_id=1, source_target_pairs={{0,2},{1,3},{2,0},{3,1},{4,6},{5,7},{6,4},{7,5},{8,10},{9,11},{10,... | collective-permute-start | bytes 663560 | tf_op jit(solution)/shard_map/ppermute | solution.py:430
  5.6 2.1 %collective-permute-start.1 = (f32[400,128]{1,0:T(8,128)S(1)}, f32[400,128]{1,0:T(8,128)S(1)}, u32[]{:S(2)}, u32[]{:S(2)}) collective-permute-start(f32[400,128]{1,0:T(8,128)S(1)} %get-tuple-element.36), channel_id=1, source_target_pairs={{0,13},{1,12},{2,15},{3,14},{4,9},{5,8},{6,11},{7,10},{8,5},{9,4},... | collective-permute-start | bytes 614408 | tf_op jit(solution)/shard_map/ppermute | solution.py:430
  7.7 0.3 collective-permute-start.2
  7.9 1.2 %collective-permute-start.3 = (f32[384,128]{1,0:T(8,128)S(1)}, f32[384,128]{1,0:T(8,128)S(1)}, u32[]{:S(2)}, u32[]{:S(2)}) collective-permute-start(f32[384,128]{1,0:T(8,128)S(1)} %get-tuple-element.38), channel_id=1, source_target_pairs={{0,15},{1,14},{2,13},{3,12},{4,11},{5,10},{6,9},{7,8},{8,7},{9,6},... | collective-permute-start | bytes 589832 | tf_op jit(solution)/shard_map/ppermute | solution.py:430
  9.2 1.5 %collective-permute-done.refs_1_ = f32[27,2,8,128]{3,2,1,0:T(8,128)S(1)} collective-permute-done((f32[27,2,8,128]{3,2,1,0:T(8,128)S(1)}, f32[27,2,8,128]{3,2,1,0:T(8,128)S(1)}, u32[]{:S(2)}, u32[]{:S(2)}) %collective-permute-start) | collective-permute-done | bytes 221216 | tf_op jit(solution)/shard_map/ppermute | solution.py:430
  10.6 2.0 %weights.1 = (bf16[9,128,384]{2,1,0:T(8,128)(2,1)S(1)}, bf16[9,128,768]{2,1,0:T(8,128)(2,1)S(1)}) custom-call(f32[27,2,8,128]{3,2,1,0:T(8,128)S(1)} %fold.1.refs_0_, f32[27,2,8,128]{3,2,1,0:T(8,128)S(1)} %collective-permute-done.refs_1_), custom_call_target="tpu_custom_call" | custom-call | tf_op jit(solution)/shard_map/weights/pallas_call | solution.py:21
  12.6 2.2 %collective-permute-done.2.refs_2_ = f32[384,128]{1,0:T(8,128)S(1)} collective-permute-done((f32[384,128]{1,0:T(8,128)S(1)}, f32[384,128]{1,0:T(8,128)S(1)}, u32[]{:S(2)}, u32[]{:S(2)}) %collective-permute-start.2) | collective-permute-done | bytes 196640 | tf_op jit(solution)/shard_map/ppermute | solution.py:430
  14.9 11.3 %collective-permute-done.3.refs_3_ = f32[384,128]{1,0:T(8,128)S(1)} collective-permute-done((f32[384,128]{1,0:T(8,128)S(1)}, f32[384,128]{1,0:T(8,128)S(1)}, u32[]{:S(2)}, u32[]{:S(2)}) %collective-permute-start.3) | collective-permute-done | bytes 196640 | tf_op jit(solution)/shard_map/ppermute | solution.py:430
  26.1 0.0 collective-permute-done.1.refs_1_
  26.1 1.0 %points.1 = (f32[10,144,128]{2,1,0:T(8,128)S(1)}, f32[10,144,128]{2,1,0:T(8,128)S(1)}, f32[144,128]{1,0:T(8,128)S(1)}) custom-call(bf16[9,128,384]{2,1,0:T(8,128)(2,1)S(1)} %get-tuple-element.34.ready.single, f32[400,128]{1,0:T(8,128)S(1)} %get-tuple-element.35.refs_0_, f32[400,128]{1,0:T(8,128)S(1)} %collective-permute-done.1.refs_1_, ...), custom_call_target="tpu_custom_call" | custom-call | tf_op jit(solution)/shard_map/points/pallas_call | solution.py:21
  27.1 0.5 collective-permute-start.4
  27.6 0.9 %collective-permute-done.4.middle = f32[144,128]{1,0:T(8,128)S(1)} collective-permute-done((f32[144,128]{1,0:T(8,128)S(1)}, f32[144,128]{1,0:T(8,128)S(1)}, u32[]{:S(2)}, u32[]{:S(2)}) %collective-permute-start.4) | collective-permute-done | bytes 73760 | tf_op jit(solution)/shard_map/ppermute | solution.py:430
  28.5 0.1 faces.2
  28.6 0.1 collective-permute-start.5
  28.7 1.2 %collective-permute-start.6 = (f32[216,128]{1,0:T(8,128)S(1)}, f32[216,128]{1,0:T(8,128)S(1)}, u32[]{:S(2)}, u32[]{:S(2)}) collective-permute-start(f32[216,128]{1,0:T(8,128)S(1)} %get-tuple-element.44), channel_id=1, source_target_pairs={{0,1},{1,0},{2,3},{3,2},{4,8},{5,9},{6,10},{7,11},{8,4},{9,5},{10,... | collective-permute-start | bytes 331784 | tf_op jit(solution)/shard_map/ppermute | solution.py:430
  29.9 4.8 %inside.2.main = f32[9,144,128]{2,1,0:T(8,128)S(1)} custom-call(f32[10,144,128]{2,1,0:T(8,128)S(1)} %get-tuple-element.39.x, f32[144,128]{1,0:T(8,128)S(1)} %collective-permute-done.4.middle, bf16[9,128,384]{2,1,0:T(8,128)(2,1)S(1)} %get-tuple-element.34.ready.single, bf16[9,128,768]{2,1,0:T(8,128)(2,1)S(1)} %get-tuple-element.42.double), custom_call_target="tpu_custom_call" | custom-call | tf_op jit(solution)/shard_map/inside/pallas_call | solution.py:21
  34.7 0.0 collective-permute-done.5.got_a
  34.7 0.0 collective-permute-done.6.got_b
  34.7 1.0 %middle.1 = (f32[10,144,128]{2,1,0:T(8,128)S(1)}, f32[144,128]{1,0:T(8,128)S(1)}) custom-call(f32[10,144,128]{2,1,0:T(8,128)S(1)} %get-tuple-element.39.x, f32[10,144,128]{2,1,0:T(8,128)S(1)} %get-tuple-element.40.marks, f32[9,144,128]{2,1,0:T(8,128)S(1)} %inside.2.main, f32[216,128]{1,0:T(8,128)S(1)} %collective-permute-done.5.got_a, ...), custom_call_target="tpu_custom_call" | custom-call | tf_op jit(solution)/shard_map/middle/pallas_call | solution.py:21
  35.8 0.6 %collective-permute-start.7 = (f32[144,128]{1,0:T(8,128)S(1)}, f32[144,128]{1,0:T(8,128)S(1)}, u32[]{:S(2)}, u32[]{:S(2)}) collective-permute-start(f32[144,128]{1,0:T(8,128)S(1)} %get-tuple-element.46), channel_id=1, source_target_pairs={{0,1},{1,0},{2,3},{3,2},{4,5},{5,4},{6,7},{7,6},{8,9},{9,8},{10,11... | collective-permute-start | bytes 221192 | tf_op jit(solution)/shard_map/ppermute | solution.py:430
  36.4 0.9 %collective-permute-done.7.middle = f32[144,128]{1,0:T(8,128)S(1)} collective-permute-done((f32[144,128]{1,0:T(8,128)S(1)}, f32[144,128]{1,0:T(8,128)S(1)}, u32[]{:S(2)}, u32[]{:S(2)}) %collective-permute-start.7) | collective-permute-done | bytes 73760 | tf_op jit(solution)/shard_map/ppermute | solution.py:430
  37.3 0.1 faces.3
  37.4 0.7 %collective-permute-start.8 = (f32[216,128]{1,0:T(8,128)S(1)}, f32[216,128]{1,0:T(8,128)S(1)}, u32[]{:S(2)}, u32[]{:S(2)}) collective-permute-start(f32[216,128]{1,0:T(8,128)S(1)} %get-tuple-element.47), channel_id=1, source_target_pairs={{0,4},{1,5},{2,6},{3,7},{4,0},{5,1},{6,2},{7,3},{8,12},{9,13},{10,... | collective-permute-start | bytes 331784 | tf_op jit(solution)/shard_map/ppermute | solution.py:430
  38.1 1.2 %collective-permute-start.9 = (f32[216,128]{1,0:T(8,128)S(1)}, f32[216,128]{1,0:T(8,128)S(1)}, u32[]{:S(2)}, u32[]{:S(2)}) collective-permute-start(f32[216,128]{1,0:T(8,128)S(1)} %get-tuple-element.48), channel_id=1, source_target_pairs={{0,1},{1,0},{2,3},{3,2},{4,8},{5,9},{6,10},{7,11},{8,4},{9,5},{10,... | collective-permute-start | bytes 331784 | tf_op jit(solution)/shard_map/ppermute | solution.py:430
  39.2 3.7 %inside.3.main = f32[8,128,128]{2,1,0:T(8,128)S(1)} custom-call(f32[10,144,128]{2,1,0:T(8,128)S(1)} %get-tuple-element.45.x, f32[144,128]{1,0:T(8,128)S(1)} %collective-permute-done.7.middle, bf16[9,128,384]{2,1,0:T(8,128)(2,1)S(1)} %get-tuple-element.34.ready.single, bf16[9,128,768]{2,1,0:T(8,128)(2,1)S(1)} %get-tuple-element.42.double), custom_call_target="tpu_custom_call" | custom-call | tf_op jit(solution)/shard_map/inside/pallas_call | solution.py:21
  42.9 0.0 copy-start.1
  43.0 0.0 copy-start.3
  43.0 0.0 collective-permute-done.8.got_a
  43.0 0.0 collective-permute-done.9.got_b
  43.0 1.0 %last.1 = (f32[256,128]{1,0:T(8,128)S(1)}, f32[256,128]{1,0:T(8,128)S(1)}, f32[256,128]{1,0:T(8,128)S(1)}, f32[256,128]{1,0:T(8,128)S(1)}) custom-call(f32[8,128,128]{2,1,0:T(8,128)S(1)} %inside.3.main, f32[216,128]{1,0:T(8,128)S(1)} %collective-permute-done.8.got_a, f32[216,128]{1,0:T(8,128)S(1)} %collective-permute-done.9.got_b, ...), custom_call_target="tpu_custom_call" | custom-call | tf_op jit(solution)/shard_map/last/pallas_call | solution.py:21
  44.0 1.7 %collective-permute-start.12 = (f32[256,128]{1,0:T(8,128)S(1)}, f32[256,128]{1,0:T(8,128)S(1)}, u32[]{:S(2)}, u32[]{:S(2)}) collective-permute-start(f32[256,128]{1,0:T(8,128)S(1)} %get-tuple-element.52), channel_id=1, source_target_pairs={{0,13},{1,12},{2,15},{3,14},{4,9},{5,8},{6,11},{7,10},{8,5},{9,4},... | collective-permute-start | bytes 393224 | tf_op jit(solution)/shard_map/ppermute | solution.py:430
  45.7 1.1 %collective-permute-start.10 = (f32[256,128]{1,0:T(8,128)S(1)}, f32[256,128]{1,0:T(8,128)S(1)}, u32[]{:S(2)}, u32[]{:S(2)}) collective-permute-start(f32[256,128]{1,0:T(8,128)S(1)} %get-tuple-element.49), channel_id=1, source_target_pairs={{0,2},{1,3},{2,0},{3,1},{4,6},{5,7},{6,4},{7,5},{8,10},{9,11},{10,... | collective-permute-start | bytes 393224 | tf_op jit(solution)/shard_map/ppermute | solution.py:430
  46.8 0.5 collective-permute-start.11
  47.3 8.5 %collective-permute-done.12.mirrored = f32[256,128]{1,0:T(8,128)S(1)} collective-permute-done((f32[256,128]{1,0:T(8,128)S(1)}, f32[256,128]{1,0:T(8,128)S(1)}, u32[]{:S(2)}, u32[]{:S(2)}) %collective-permute-start.12) | collective-permute-done | bytes 131104 | tf_op jit(solution)/shard_map/ppermute | solution.py:430
  55.8 0.0 copy-done.1
  55.8 0.0 copy-done.3
  55.8 1.5 %unpack.2.refs_0_ = f32[32,16,8,32]{3,2,1,0:T(8,128)} custom-call(f32[32,16,8,32]{3,2,1,0:T(8,128)S(1)} %bitcast.3, s32[16,8,32]{2,1,0:T(8,128)S(1)} %copy-done.3, f32[256,128]{1,0:T(8,128)S(1)} %get-tuple-element.51.own, f32[256,128]{1,0:T(8,128)S(1)} %collective-permute-done.12.mirrored), custom_call_target="tpu_custom_call" | custom-call | tf_op jit(solution)/shard_map/unpack/pallas_call | solution.py:21
  57.3 0.0 collective-permute-done.10.own
  57.3 2.1 %collective-permute-done.11.mirrored = f32[256,128]{1,0:T(8,128)S(1)} collective-permute-done((f32[256,128]{1,0:T(8,128)S(1)}, f32[256,128]{1,0:T(8,128)S(1)}, u32[]{:S(2)}, u32[]{:S(2)}) %collective-permute-start.11) | collective-permute-done | bytes 131104 | tf_op jit(solution)/shard_map/ppermute | solution.py:430
  59.4 1.5 %unpack.3 = f32[32,16,8,32]{3,2,1,0:T(8,128)} custom-call(f32[32,16,8,32]{3,2,1,0:T(8,128)S(1)} %bitcast.4, s32[16,8,32]{2,1,0:T(8,128)S(1)} %copy-done.3, f32[256,128]{1,0:T(8,128)S(1)} %collective-permute-done.10.own, f32[256,128]{1,0:T(8,128)S(1)} %collective-permute-done.11.mirrored, f32[32,16,8,32]{3,2,1,0:T(8,128)} %unpack.2.refs_0_), custom_call_target="tpu_custom_call", output_to_operand_aliasing={{}: (4, {})} | custom-call | tf_op jit(solution)/shard_map/unpack/pallas_call | solution.py:21
Async XLA Ops:
  0.0 1.6 %copy-start = (f32[2,16,16,8,32]{4,3,2,1,0:T(8,128)S(1)}, f32[2,16,16,8,32]{4,3,2,1,0:T(8,128)}, u32[]{:S(2)}) copy-start(f32[2,16,16,8,32]{4,3,2,1,0:T(8,128)} %param.3) | copy-start | bytes 1572868
  1.6 0.8 %copy-start.2 = (s32[16,8,32]{2,1,0:T(8,128)S(1)}, s32[16,8,32]{2,1,0:T(8,128)}, u32[]{:S(2)}) copy-start(s32[16,8,32]{2,1,0:T(8,128)} %mask.5) | copy-start | bytes 49156
  2.4 1.7 %copy-start.4 = (f32[27,2,16,64]{3,2,1,0:T(8,128)S(1)}, f32[27,2,16,64]{3,2,1,0:T(8,128)}, u32[]{:S(2)}) copy-start(f32[27,2,16,64]{3,2,1,0:T(8,128)} %kernel) | copy-start | bytes 663556
  4.3 6.4 %collective-permute-start = (f32[27,2,8,128]{3,2,1,0:T(8,128)S(1)}, f32[27,2,8,128]{3,2,1,0:T(8,128)S(1)}, u32[]{:S(2)}, u32[]{:S(2)}) collective-permute-start(f32[27,2,8,128]{3,2,1,0:T(8,128)S(1)} %fold.1.refs_0_), channel_id=1, source_target_pairs={{0,2},{1,3},{2,0},{3,1},{4,6},{5,7},{6,4},{7,5},{8,10},{9,11},{10,... | collective-permute-start | bytes 663560 | tf_op jit(solution)/shard_map/ppermute | solution.py:430
  5.6 20.6 %collective-permute-start.1 = (f32[400,128]{1,0:T(8,128)S(1)}, f32[400,128]{1,0:T(8,128)S(1)}, u32[]{:S(2)}, u32[]{:S(2)}) collective-permute-start(f32[400,128]{1,0:T(8,128)S(1)} %get-tuple-element.36), channel_id=1, source_target_pairs={{0,13},{1,12},{2,15},{3,14},{4,9},{5,8},{6,11},{7,10},{8,5},{9,4},... | collective-permute-start | bytes 614408 | tf_op jit(solution)/shard_map/ppermute | solution.py:430
  7.7 7.2 %collective-permute-start.2 = (f32[384,128]{1,0:T(8,128)S(1)}, f32[384,128]{1,0:T(8,128)S(1)}, u32[]{:S(2)}, u32[]{:S(2)}) collective-permute-start(f32[384,128]{1,0:T(8,128)S(1)} %get-tuple-element.37), channel_id=1, source_target_pairs={{0,2},{1,3},{2,0},{3,1},{4,6},{5,7},{6,4},{7,5},{8,10},{9,11},{10,... | collective-permute-start | bytes 589832 | tf_op jit(solution)/shard_map/ppermute | solution.py:430
  7.9 18.2 %collective-permute-start.3 = (f32[384,128]{1,0:T(8,128)S(1)}, f32[384,128]{1,0:T(8,128)S(1)}, u32[]{:S(2)}, u32[]{:S(2)}) collective-permute-start(f32[384,128]{1,0:T(8,128)S(1)} %get-tuple-element.38), channel_id=1, source_target_pairs={{0,15},{1,14},{2,13},{3,12},{4,11},{5,10},{6,9},{7,8},{8,7},{9,6},... | collective-permute-start | bytes 589832 | tf_op jit(solution)/shard_map/ppermute | solution.py:430
  27.1 1.4 %collective-permute-start.4 = (f32[144,128]{1,0:T(8,128)S(1)}, f32[144,128]{1,0:T(8,128)S(1)}, u32[]{:S(2)}, u32[]{:S(2)}) collective-permute-start(f32[144,128]{1,0:T(8,128)S(1)} %get-tuple-element.41), channel_id=1, source_target_pairs={{0,1},{1,0},{2,3},{3,2},{4,5},{5,4},{6,7},{7,6},{8,9},{9,8},{10,11... | collective-permute-start | bytes 221192 | tf_op jit(solution)/shard_map/ppermute | solution.py:430
  28.6 6.1 %collective-permute-start.5 = (f32[216,128]{1,0:T(8,128)S(1)}, f32[216,128]{1,0:T(8,128)S(1)}, u32[]{:S(2)}, u32[]{:S(2)}) collective-permute-start(f32[216,128]{1,0:T(8,128)S(1)} %get-tuple-element.43), channel_id=1, source_target_pairs={{0,4},{1,5},{2,6},{3,7},{4,0},{5,1},{6,2},{7,3},{8,12},{9,13},{10,... | collective-permute-start | bytes 331784 | tf_op jit(solution)/shard_map/ppermute | solution.py:430
  28.7 6.0 %collective-permute-start.6 = (f32[216,128]{1,0:T(8,128)S(1)}, f32[216,128]{1,0:T(8,128)S(1)}, u32[]{:S(2)}, u32[]{:S(2)}) collective-permute-start(f32[216,128]{1,0:T(8,128)S(1)} %get-tuple-element.44), channel_id=1, source_target_pairs={{0,1},{1,0},{2,3},{3,2},{4,8},{5,9},{6,10},{7,11},{8,4},{9,5},{10,... | collective-permute-start | bytes 331784 | tf_op jit(solution)/shard_map/ppermute | solution.py:430
  35.8 1.5 %collective-permute-start.7 = (f32[144,128]{1,0:T(8,128)S(1)}, f32[144,128]{1,0:T(8,128)S(1)}, u32[]{:S(2)}, u32[]{:S(2)}) collective-permute-start(f32[144,128]{1,0:T(8,128)S(1)} %get-tuple-element.46), channel_id=1, source_target_pairs={{0,1},{1,0},{2,3},{3,2},{4,5},{5,4},{6,7},{7,6},{8,9},{9,8},{10,11... | collective-permute-start | bytes 221192 | tf_op jit(solution)/shard_map/ppermute | solution.py:430
  37.4 5.6 %collective-permute-start.8 = (f32[216,128]{1,0:T(8,128)S(1)}, f32[216,128]{1,0:T(8,128)S(1)}, u32[]{:S(2)}, u32[]{:S(2)}) collective-permute-start(f32[216,128]{1,0:T(8,128)S(1)} %get-tuple-element.47), channel_id=1, source_target_pairs={{0,4},{1,5},{2,6},{3,7},{4,0},{5,1},{6,2},{7,3},{8,12},{9,13},{10,... | collective-permute-start | bytes 331784 | tf_op jit(solution)/shard_map/ppermute | solution.py:430
  38.1 4.9 %collective-permute-start.9 = (f32[216,128]{1,0:T(8,128)S(1)}, f32[216,128]{1,0:T(8,128)S(1)}, u32[]{:S(2)}, u32[]{:S(2)}) collective-permute-start(f32[216,128]{1,0:T(8,128)S(1)} %get-tuple-element.48), channel_id=1, source_target_pairs={{0,1},{1,0},{2,3},{3,2},{4,8},{5,9},{6,10},{7,11},{8,4},{9,5},{10,... | collective-permute-start | bytes 331784 | tf_op jit(solution)/shard_map/ppermute | solution.py:430
  42.9 12.8 %copy-start.1 = (f32[2,16,16,8,32]{4,3,2,1,0:T(8,128)S(1)}, f32[2,16,16,8,32]{4,3,2,1,0:T(8,128)}, u32[]{:S(2)}) copy-start(f32[2,16,16,8,32]{4,3,2,1,0:T(8,128)} %param.3) | copy-start | bytes 1572868
  43.0 12.8 %copy-start.3 = (s32[16,8,32]{2,1,0:T(8,128)S(1)}, s32[16,8,32]{2,1,0:T(8,128)}, u32[]{:S(2)}) copy-start(s32[16,8,32]{2,1,0:T(8,128)} %mask.5) | copy-start | bytes 49156
  44.0 11.7 %collective-permute-start.12 = (f32[256,128]{1,0:T(8,128)S(1)}, f32[256,128]{1,0:T(8,128)S(1)}, u32[]{:S(2)}, u32[]{:S(2)}) collective-permute-start(f32[256,128]{1,0:T(8,128)S(1)} %get-tuple-element.52), channel_id=1, source_target_pairs={{0,13},{1,12},{2,15},{3,14},{4,9},{5,8},{6,11},{7,10},{8,5},{9,4},... | collective-permute-start | bytes 393224 | tf_op jit(solution)/shard_map/ppermute | solution.py:430
  45.7 11.6 %collective-permute-start.10 = (f32[256,128]{1,0:T(8,128)S(1)}, f32[256,128]{1,0:T(8,128)S(1)}, u32[]{:S(2)}, u32[]{:S(2)}) collective-permute-start(f32[256,128]{1,0:T(8,128)S(1)} %get-tuple-element.49), channel_id=1, source_target_pairs={{0,2},{1,3},{2,0},{3,1},{4,6},{5,7},{6,4},{7,5},{8,10},{9,11},{10,... | collective-permute-start | bytes 393224 | tf_op jit(solution)/shard_map/ppermute | solution.py:430
  46.8 12.6 %collective-permute-start.11 = (f32[256,128]{1,0:T(8,128)S(1)}, f32[256,128]{1,0:T(8,128)S(1)}, u32[]{:S(2)}, u32[]{:S(2)}) collective-permute-start(f32[256,128]{1,0:T(8,128)S(1)} %get-tuple-element.50), channel_id=1, source_target_pairs={{0,15},{1,14},{2,13},{3,12},{4,11},{5,10},{6,9},{7,8},{8,7},{9,6},... | collective-permute-start | bytes 393224 | tf_op jit(solution)/shard_map/ppermute | solution.py:430

commit v4 on v3

--- a/solution.py
+++ b/solution.py
@@ -8,23 +8,23 @@
 from jax.sharding import PartitionSpec as P
 
 ITERS = 2
+PACK = 56 << 20
 AXES = ("kz", "coil", "kx")
 F32 = jnp.float32
 BF16 = jnp.bfloat16
-PARAMS = pltpu.CompilerParams(vmem_limit_bytes=48 << 20)
 ANY = pl.BlockSpec(memory_space=pl.ANY)
 HBM = pl.BlockSpec(memory_space=pltpu.HBM)
 VMEM = pl.BlockSpec(memory_space=pltpu.VMEM)
 
 
-def call(body, name, args, shapes, scratch=(), far=(), space=ANY, out=VMEM, **options):
+def call(body, name, args, shapes, scratch=(), far=(), space=ANY, out=VMEM, limit=48 << 20, **options):
     return pl.pallas_call(
         body,
         out_shape=shapes,
         in_specs=[space if i in far else VMEM for i in range(len(args))],
         out_specs=[out] * len(shapes),
         scratch_shapes=list(scratch),
-        compiler_params=PARAMS,
+        compiler_params=pltpu.CompilerParams(vmem_limit_bytes=limit),
         name=name,
         **options,
     )(*args)
@@ -58,6 +58,10 @@
         self.base = 128 // self.H
         self.spare = (self.S - self.base) * self.H
         self.part = self.ch // 2 * D
+        self.used = self.spare + 2 * self.S
+        self.group = self.ch * D // 16
+        self.folds = -(-16 * self.used // 128)
+        self.length = 2 * self.part + self.folds * self.group
         self.slots = self.S + 2
         self.pitch = -(-(self.V + 1) // 8) * 8
 
@@ -98,67 +102,84 @@
     return jnp.where(lane == source, 1.0, 0.0).astype(BF16)
 
 
-def pack_kernel(cut, measured, mask, *refs):
-    C, S, ch, D, W = cut.C, cut.S, cut.ch, cut.D, cut.W
-    outs, (rows, marks, sems) = refs[: 2 * C], refs[2 * C :]
-    copies = [pltpu.make_async_copy(mask, marks, sems.at[C])]
-    for d in range(C):
-        copies.append(pltpu.make_async_copy(measured.at[:, pl.ds(cut.start(d), S)], rows.at[d], sems.at[d]))
+def pack_kernel(cut, d, measured, mask, *refs):
+    S, ch, D, W, part = cut.S, cut.ch, cut.D, cut.W, cut.part
+    outs, (rows, marks, sems) = refs[:2], refs[2:]
+    start = cut.start(d)
+    copies = [pltpu.make_async_copy(mask.at[pl.ds(start, S)], marks, sems.at[0])]
+    copies.append(pltpu.make_async_copy(measured.at[:, pl.ds(start, S)], rows, sems.at[1]))
     for copy in copies:
         copy.start()
     order = arrangement(cut)
-    copies[0].wait()
-    for d in range(C):
-        copies[d + 1].wait()
-        sampled = [marks[cut.start(d) + j] == 1 for j in range(S)]
-        kept = [jnp.where(sampled[j][None], rows[d, :, j], 0.0) for j in range(S)]
-        kept = jnp.concatenate(kept, -1).reshape(ch * D, S * W)
+    for copy in copies:
+        copy.wait()
+    sampled = [marks[j] == 1 for j in range(S)]
+    kept = [jnp.where(sampled[j][None], rows[:, j], 0.0) for j in range(S)]
+    kept = jnp.concatenate(kept, -1).reshape(ch * D, S * W)
+    if d == 0:
+        kept = jnp.concatenate([kept, jnp.concatenate([jnp.where(s, 1.0, 0.0) for s in sampled], -1)], 0)
+    hi, lo = split(kept)
+    y = dot(hi, order) + dot(lo, order)
+    for side in (1, 0):
+        out = outs[side]
+        out[: 2 * part] = y[: 2 * part, 128 * side : 128 * side + 128]
+        spare = y[:, 256 + 64 * side : 320 + 64 * side]
+        group = cut.group
+        folded = [spare[i * group : (i + 1) * group, : cut.used] for i in range(16)]
+        if cut.folds * 128 > 16 * cut.used:
+            folded.append(jnp.zeros((group, cut.folds * 128 - 16 * cut.used), F32))
+        folded = jnp.concatenate(folded, 1)
+        for i in range(cut.folds):
+            place = 2 * part + i * group
+            out[place : place + group] = folded[:, i * 128 : (i + 1) * 128]
         if d == 0:
-            kept = jnp.concatenate([kept, jnp.concatenate([jnp.where(s, 1.0, 0.0) for s in sampled], -1)], 0)
-        hi, lo = split(kept)
-        y = dot(hi, order) + dot(lo, order)
-        part = cut.part
-        for side in range(2):
-            out = outs[2 * d + side]
-            spare = y[:, 256 + 64 * side : 320 + 64 * side]
-            out[: 2 * part] = y[: 2 * part, 128 * side : 128 * side + 128]
-            out[2 * part : 3 * part] = jnp.concatenate([spare[:part], spare[part : 2 * part]], 1)
-            if d == 0:
-                out[3 * part : 3 * part + D] = y[2 * part :, 128 * side : 128 * side + 128]
-                out[3 * part + D :] = jnp.concatenate([spare[2 * part :], jnp.zeros((D, 64), F32)], 1)
-
-
-def pack(measured, mask, cut):
-    shapes = []
-    for d in range(cut.C):
-        shapes += [jax.ShapeDtypeStruct((3 * cut.part + (2 * cut.D if d == 0 else 0), 128), F32)] * 2
+            out[cut.length : cut.length + D] = y[2 * part :, 128 * side : 128 * side + 128]
+            out[cut.length + D :] = jnp.concatenate([spare[2 * part :], jnp.zeros((D, 64), F32)], 1)
+
+
+def pack(d, measured, mask, cut):
+    shapes = [jax.ShapeDtypeStruct((cut.length + (0 if d else 2 * cut.D), 128), F32)] * 2
     scratch = [
-        pltpu.VMEM((cut.C, cut.ch, cut.S, cut.D, cut.W), F32),
-        pltpu.VMEM(mask.shape, jnp.int32),
-        pltpu.SemaphoreType.DMA((cut.C + 1,)),
+        pltpu.VMEM((cut.ch, cut.S, cut.D, cut.W), F32),
+        pltpu.VMEM((cut.S, cut.D, cut.W), jnp.int32),
+        pltpu.SemaphoreType.DMA((2,)),
     ]
-    return call(functools.partial(pack_kernel, cut), "pack", (measured, mask), shapes, scratch, far=(0, 1), space=HBM)
+    body = functools.partial(pack_kernel, cut, d)
+    return call(body, "pack", (measured, mask), shapes, scratch, far=(0, 1), space=HBM, limit=PACK)
 
 
 def fold_kernel(kernel, out):
-    half = kernel.shape[2] // 2
-    out[...] = jnp.concatenate([kernel[:, :, :half], kernel[:, :, half:]], -1)
-
-
-def weights_kernel(C, *refs):
-    folded, (single, double, kernel) = refs[:C], refs[C:]
-    taps, _, coils, inputs = kernel.shape
-    half = folded[0].shape[2]
-    for d in range(C):
-        start = pl.multiple_of(lax.bitwise_xor(lax.axis_index("coil"), d) * 2 * half, 2 * half)
-        kernel[:, :, pl.ds(start, half)] = folded[d][..., :inputs]
-        kernel[:, :, pl.ds(start + half, half)] = folded[d][..., inputs:]
+    count = out.shape[0]
+    half = kernel.shape[1] // 2
+    some = kernel[pl.ds(lax.axis_index("kx") * count, count)]
+    out[...] = jnp.concatenate([some[:, :half], some[:, half:]], -1)
+
+
+def fold(kernel):
+    count, coils, inputs = kernel.shape
+    shape = jax.ShapeDtypeStruct((count // 2, coils // 2, 2 * inputs), F32)
+    return call(fold_kernel, "fold", (kernel,), [shape])[0]
+
+
+def weights_kernel(cut, own, *refs):
+    folded, (single, double, kernel) = refs[:-3], refs[-3:]
+    count, coils, inputs = kernel.shape
+    local = coils // cut.C
+    c, x = lax.axis_index("coil"), lax.axis_index("kx")
+    kernel[:, pl.ds(pl.multiple_of(c * local, local), local)] = own[...]
+    for i, half in enumerate(folded):
+        d, other = i // 2 + 1, i % 2
+        place = pl.multiple_of(lax.bitwise_xor(c, d) * local, local)
+        taps = pl.ds(lax.bitwise_xor(x, other) * (count // 2), count // 2)
+        kernel[taps, pl.ds(place, local // 2)] = half[..., :inputs]
+        kernel[taps, pl.ds(place + local // 2, local // 2)] = half[..., inputs:]
 
     def parts(tap):
-        re, im = kernel[tap, 0], kernel[tap, 1]
+        re, im = kernel[2 * tap], kernel[2 * tap + 1]
         return re[:, :coils], im[:, :coils], re[:, coils:], im[:, coils:]
 
     N = 4 * coils
+    taps = count // 2
     for t in range(taps):
         pr, pi, vr, vi = parts(t)
         qr, qi, ur, ui = parts(taps - 1 - t)
@@ -178,12 +199,12 @@
         double[tap, :, (2 * e + 1) * N : (2 * e + 2) * N] = lo
 
 
-def build_weights(C, folded, coils):
-    taps, parts, _, inputs = folded[0].shape
-    N = 4 * coils
+def build_weights(kernel, folded, cut):
+    count, coils, inputs = kernel.shape
+    N = cut.channels
     shapes = [jax.ShapeDtypeStruct((9, N, 3 * N), BF16), jax.ShapeDtypeStruct((9, N, 6 * N), BF16)]
-    scratch = [pltpu.VMEM((taps, parts, coils, inputs // 2), F32)]
-    return call(functools.partial(weights_kernel, C), "weights", folded, shapes, scratch)
+    scratch = [pltpu.VMEM((count, coils * cut.C, inputs), F32)]
+    return call(functools.partial(weights_kernel, cut), "weights", (kernel, *folded), shapes, scratch)
 
 
 def middle_row(cut, x):
@@ -201,8 +222,12 @@
             for ri in range(2):
                 start = pl.multiple_of(((side * 2 + ri) * C + other) * part, part)
                 main[pl.ds(start, part)] = msg[ri * part : (ri + 1) * part]
-            start = pl.multiple_of((side * C + other) * part, part)
-            spare[pl.ds(start, part)] = msg[2 * part : 3 * part]
+            folded = msg[2 * part : cut.length].reshape(cut.folds, cut.group, 128)
+            folded = jnp.concatenate([folded[i] for i in range(cut.folds)], 1)
+            for i in range(16):
+                ri, rest = i // 8, i % 8 * cut.group
+                start = pl.multiple_of(((side * 2 + ri) * C + other) * part + rest, cut.group)
+                spare[pl.ds(start, cut.group), : cut.used] = folded[:, i * cut.used : (i + 1) * cut.used]
 
     def spread(target, k, first, rest):
         for r in range(cut.base):
@@ -214,17 +239,16 @@
             target[r, pl.ds(H * D + k, 2, stride=D)] = rest[place : place + 2]
 
     lane = lax.broadcasted_iota(jnp.int32, (128, cut.channels), 1)
-    flags = [msgs[side][3 * part : 3 * part + 2 * D] for side in range(2)]
+    flags = [msgs[side][cut.length : cut.length + 2 * D] for side in range(2)]
     flags = jnp.concatenate(flags + [jnp.zeros((128 - 4 * D, 128), F32)], 0).T
     for k in range(D):
         j = D - 1 - k
         mine = main[pl.ds(k, half, stride=D)]
         other = main[pl.ds(half * D + j, half, stride=D)]
         first = jnp.concatenate([mine, other], 0).T
-        mine = spare[pl.ds(k, half // 2, stride=D)]
-        other = spare[pl.ds(half // 2 * D + j, half // 2, stride=D)]
-        rest = jnp.concatenate([mine[:, :64], mine[:, 64:], other[:, :64], other[:, 64:]], 0)
-        rest = jnp.concatenate([rest, jnp.zeros_like(rest)], 1).T
+        mine = spare[pl.ds(k, half, stride=D)]
+        other = spare[pl.ds(half * D + j, half, stride=D)]
+        rest = jnp.concatenate([mine, other], 0).T
         spread(x, k, first, rest)
         first = jnp.where(lane < half, flags[:, k : k + 1], flags[:, 2 * D + j : 2 * D + j + 1])
         rest = jnp.where(lane < half, flags[:, D + k : D + k + 1], flags[:, 3 * D + j : 3 * D + j + 1])
@@ -240,7 +264,7 @@
         "points",
         (ready, *msgs),
         [window, window, jax.ShapeDtypeStruct(row, F32)],
-        [pltpu.VMEM((cut.channels * cut.D, 128), F32), pltpu.VMEM((cut.half * cut.D, 128), F32)],
+        [pltpu.VMEM((cut.channels * cut.D, 128), F32)] * 2,
         far=(0,),
     )
 
@@ -391,17 +415,22 @@
 
 
 def unpack_kernel(cut, d, measured, mask, own, mirrored, *refs):
-    out, rows, sem = refs[-3:]
+    out, rows, sems = refs[-3:]
     ch, D, G, H = cut.ch, cut.D, cut.G, cut.H
     start = cut.piece(d) * G
     own, mirrored = (msg[...].reshape(ch, D, G * H) for msg in (own, mirrored))
+    copies = []
     for j in range(G):
         sampled = (mask[start + j] == 1)[None]
         value = jnp.concatenate([msg[:, :, j * H : (j + 1) * H] for msg in (own, mirrored)], -1)
         rows[:, j] = jnp.where(sampled, measured[:, start + j], value)
-    copy = pltpu.make_async_copy(rows, out.at[:, pl.ds(start, G)], sem)
-    copy.start()
-    copy.wait()
+        if j % 2:
+            some = pl.ds(j - 1, 2)
+            copy = pltpu.make_async_copy(rows.at[:, some], out.at[:, pl.ds(start + j - 1, 2)], sems.at[j // 2])
+            copy.start()
+            copies.append(copy)
+    for copy in copies:
+        copy.wait()
 
 
 def unpack(d, measured, mask, msgs, cut, into=None):
@@ -411,7 +440,7 @@
         "unpack",
         args,
         [jax.ShapeDtypeStruct(measured.shape, F32)],
-        [pltpu.VMEM((cut.ch, cut.G, cut.D, cut.W), F32), pltpu.SemaphoreType.DMA],
+        [pltpu.VMEM((cut.ch, cut.G, cut.D, cut.W), F32), pltpu.SemaphoreType.DMA((cut.G // 2,))],
         far=() if into is None else (len(args) - 1,),
         out=ANY,
         input_output_aliases={} if into is None else {len(args) - 1: 0},
@@ -450,15 +479,17 @@
     parts, coils, rows, D, W = measured.shape
     cut = Cut(rows, D, W, C, 2 * parts * coils * C)
     flat = measured.reshape(parts * coils, rows, D, W)
-    taps, _, _, inputs = kernel.shape
-    msgs = pack(flat, mask, cut)
-    kernel, *msgs = lax.optimization_barrier((kernel, *msgs))
+    kernel = kernel.reshape(-1, *kernel.shape[2:])
+    msgs = pack(0, flat, mask, cut)
+    for d in range(1, C):
+        kernel, mask, *msgs = lax.optimization_barrier((kernel, mask, *msgs))
+        msgs = [*msgs, *pack(d, flat, mask, cut)]
     msgs = exchange(msgs)
-    (folded,) = call(
-        fold_kernel, "fold", (kernel,), [jax.ShapeDtypeStruct((taps, parts, coils // 2, 2 * inputs), F32)]
-    )
-    folded = [folded] + [send(folded, lambda z, c, x: (z, c ^ d, x)) for d in range(1, C)]
-    weights = build_weights(C, folded, coils * C)
+    folded = []
+    for d in range(1, C):
+        half = send(fold(kernel), lambda z, c, x: (z, c ^ d, x))
+        folded += [half, send(half, core)]
+    weights = build_weights(kernel, folded, cut)
     state, marks, row = points(weights[0], msgs, cut)
     for step in range(ITERS):
         last = step == ITERS - 1

time: 61.2 us -> 59.5 us (0.972)
  Pallas kernels: 18.5 us -> 22.1 us
  waiting for transfers between devices: 27.4 us -> 24.1 us
  local copies, waits for them, and re-layouts: 2.45 us -> 0.02 us
    pallas_call x12 -> x13, Pallas kernels: 18.5 us -> 22.1 us  [call(): pl.pallas_call(body, out_shape=shapes, in_specs=[space if i in far else V...]
    ppermute x13 -> x14, waiting for transfers between devices: 27.4 us -> 24.1 us  [send(): lax.ppermute(array, AXES, [(index(*p), index(*target(*p))) for p in every])]
    unnamed x10 -> x8, local copies, waits for them, and re-layouts: 2.45 us -> 0.02 us
    ppermute x13 -> x14, starting transfers between devices: 12.4 us -> 12.8 us  [send(): lax.ppermute(array, AXES, [(index(*p), index(*target(*p))) for p in every])]
  transfers between devices with their start and end apart: 13 -> 14, of which waited for: 7 -> 7; matrix products, arithmetic and copies ran while one was open for 0% -> 0% of each run, Pallas kernels for 20% -> 25%
where the time goes in v4:
time: 59.5 us; the launch traced here: 59.3 us
  waiting for transfers between devices  24.1 us (41%)
  Pallas kernels  22.1 us (37%)
  starting transfers between devices  12.8 us (22%)
    ppermute x14, waiting for transfers between devices, send(): lax.ppermute(array, AXES, [(index(*p), index(*target(*p))) for p in every])  24.1 us
    pallas_call x13, Pallas kernels, call(): pl.pallas_call(body, out_shape=shapes, in_specs=[space if i in far else V...  22.1 us
    ppermute x14, starting transfers between devices, send(): lax.ppermute(array, AXES, [(index(*p), index(*target(*p))) for p in every])  12.8 us
  transfers between devices with their start and end apart: 14, of which 7 were waited for; matrix products, arithmetic and copies ran while one was open for 0% of the time, Pallas kernels for 25%

profile of v4, /device:TPU:9, one launch (start us, length us, event | category | flops | bytes accessed | tf_op | source)
XLA Modules:
  0.0 59.3 jit_solution(3089115690229927566)
XLA Ops:
  0.0 0.0 copy-start.1
  0.0 2.9 %pack.2 = (f32[384,128]{1,0:T(8,128)}, f32[384,128]{1,0:T(8,128)}) custom-call(f32[32,16,8,32]{3,2,1,0:T(8,128)} %bitcast.3, s32[16,8,32]{2,1,0:T(8,128)} %mask.4), custom_call_target="tpu_custom_call" | custom-call | tf_op jit(solution)/shard_map/pack/pallas_call | solution.py:21
  2.9 0.0 copy-start.3
  2.9 0.0 copy-done.1
  2.9 0.1 fold.1
  3.0 1.3 %collective-permute-start = (f32[27,8,128]{2,1,0:T(8,128)S(1)}, f32[27,8,128]{2,1,0:T(8,128)S(1)}, u32[]{:S(2)}, u32[]{:S(2)}) collective-permute-start(f32[27,8,128]{2,1,0:T(8,128)S(1)} %fold.1), channel_id=1, source_target_pairs={{0,2},{1,3},{2,0},{3,1},{4,6},{5,7},{6,4},{7,5},{8,10},{9,11},{10,... | collective-permute-start | bytes 331784 | tf_op jit(solution)/shard_map/ppermute | solution.py:459
  4.3 2.1 %collective-permute-start.2 = (f32[384,128]{1,0:T(8,128)}, f32[384,128]{1,0:T(8,128)S(1)}, u32[]{:S(2)}, u32[]{:S(2)}) collective-permute-start(f32[384,128]{1,0:T(8,128)} %get-tuple-element.34), channel_id=1, source_target_pairs={{0,13},{1,12},{2,15},{3,14},{4,9},{5,8},{6,11},{7,10},{8,5},{9,4},... | collective-permute-start | bytes 589832 | tf_op jit(solution)/shard_map/ppermute | solution.py:459
  6.4 2.8 %pack.3 = (f32[368,128]{1,0:T(8,128)}, f32[368,128]{1,0:T(8,128)}) custom-call(f32[32,16,8,32]{3,2,1,0:T(8,128)} %bitcast.4, s32[16,8,32]{2,1,0:T(8,128)} %mask.4), custom_call_target="tpu_custom_call" | custom-call | tf_op jit(solution)/shard_map/pack/pallas_call | solution.py:21
  9.2 0.3 collective-permute-start.3
  9.5 1.2 %collective-permute-start.4 = (f32[368,128]{1,0:T(8,128)}, f32[368,128]{1,0:T(8,128)S(1)}, u32[]{:S(2)}, u32[]{:S(2)}) collective-permute-start(f32[368,128]{1,0:T(8,128)} %get-tuple-element.36), channel_id=1, source_target_pairs={{0,15},{1,14},{2,13},{3,12},{4,11},{5,10},{6,9},{7,8},{8,7},{9,6},... | collective-permute-start | bytes 565256 | tf_op jit(solution)/shard_map/ppermute | solution.py:459
  10.8 0.0 collective-permute-done.refs_0_
  10.8 0.3 collective-permute-start.1
  11.0 1.0 %collective-permute-done.1.refs_1_ = f32[27,8,128]{2,1,0:T(8,128)S(1)} collective-permute-done((f32[27,8,128]{2,1,0:T(8,128)S(1)}, f32[27,8,128]{2,1,0:T(8,128)S(1)}, u32[]{:S(2)}, u32[]{:S(2)}) %collective-permute-start.1) | collective-permute-done | bytes 110624 | tf_op jit(solution)/shard_map/ppermute | solution.py:459
  12.1 1.9 %weights.1 = (bf16[9,128,384]{2,1,0:T(8,128)(2,1)S(1)}, bf16[9,128,768]{2,1,0:T(8,128)(2,1)S(1)}) custom-call(f32[54,16,64]{2,1,0:T(8,128)S(1)} %bitcast.8, f32[27,8,128]{2,1,0:T(8,128)S(1)} %collective-permute-done.refs_0_, f32[27,8,128]{2,1,0:T(8,128)S(1)} %collective-permute-done.1.refs_1_), custom_call_target="tpu_custom_call" | custom-call | tf_op jit(solution)/shard_map/weights/pallas_call | solution.py:21
  14.0 2.2 %collective-permute-done.3.refs_2_ = f32[368,128]{1,0:T(8,128)S(1)} collective-permute-done((f32[368,128]{1,0:T(8,128)}, f32[368,128]{1,0:T(8,128)S(1)}, u32[]{:S(2)}, u32[]{:S(2)}) %collective-permute-start.3) | collective-permute-done | bytes 188448 | tf_op jit(solution)/shard_map/ppermute | solution.py:459
  16.2 8.2 %collective-permute-done.4.refs_3_ = f32[368,128]{1,0:T(8,128)S(1)} collective-permute-done((f32[368,128]{1,0:T(8,128)}, f32[368,128]{1,0:T(8,128)S(1)}, u32[]{:S(2)}, u32[]{:S(2)}) %collective-permute-start.4) | collective-permute-done | bytes 188448 | tf_op jit(solution)/shard_map/ppermute | solution.py:459
  24.4 0.0 collective-permute-done.2.refs_1_
  24.4 0.0 copy-done.3
  24.4 1.0 %points.1 = (f32[10,144,128]{2,1,0:T(8,128)S(1)}, f32[10,144,128]{2,1,0:T(8,128)S(1)}, f32[144,128]{1,0:T(8,128)S(1)}) custom-call(bf16[9,128,384]{2,1,0:T(8,128)(2,1)S(1)} %get-tuple-element.32.ready.single, f32[384,128]{1,0:T(8,128)S(1)} %copy-done.3, f32[384,128]{1,0:T(8,128)S(1)} %collective-permute-done.2.refs_1_, ...), custom_call_target="tpu_custom_call" | custom-call | tf_op jit(solution)/shard_map/points/pallas_call | solution.py:21
  25.4 0.5 collective-permute-start.5
  25.9 0.9 %collective-permute-done.5.middle = f32[144,128]{1,0:T(8,128)S(1)} collective-permute-done((f32[144,128]{1,0:T(8,128)S(1)}, f32[144,128]{1,0:T(8,128)S(1)}, u32[]{:S(2)}, u32[]{:S(2)}) %collective-permute-start.5) | collective-permute-done | bytes 73760 | tf_op jit(solution)/shard_map/ppermute | solution.py:459
  26.8 0.1 faces.2
  26.8 0.1 collective-permute-start.6
  26.9 1.2 %collective-permute-start.7 = (f32[216,128]{1,0:T(8,128)S(1)}, f32[216,128]{1,0:T(8,128)S(1)}, u32[]{:S(2)}, u32[]{:S(2)}) collective-permute-start(f32[216,128]{1,0:T(8,128)S(1)} %get-tuple-element.42), channel_id=1, source_target_pairs={{0,1},{1,0},{2,3},{3,2},{4,8},{5,9},{6,10},{7,11},{8,4},{9,5},{10,... | collective-permute-start | bytes 331784 | tf_op jit(solution)/shard_map/ppermute | solution.py:459
  28.2 4.8 %inside.2.main = f32[9,144,128]{2,1,0:T(8,128)S(1)} custom-call(f32[10,144,128]{2,1,0:T(8,128)S(1)} %get-tuple-element.37.x, f32[144,128]{1,0:T(8,128)S(1)} %collective-permute-done.5.middle, bf16[9,128,384]{2,1,0:T(8,128)(2,1)S(1)} %get-tuple-element.32.ready.single, bf16[9,128,768]{2,1,0:T(8,128)(2,1)S(1)} %get-tuple-element.40.double), custom_call_target="tpu_custom_call" | custom-call | tf_op jit(solution)/shard_map/inside/pallas_call | solution.py:21
  32.9 0.0 collective-permute-done.6.got_a
  33.0 0.0 collective-permute-done.7.got_b
  33.0 1.0 %middle.1 = (f32[10,144,128]{2,1,0:T(8,128)S(1)}, f32[144,128]{1,0:T(8,128)S(1)}) custom-call(f32[10,144,128]{2,1,0:T(8,128)S(1)} %get-tuple-element.37.x, f32[10,144,128]{2,1,0:T(8,128)S(1)} %get-tuple-element.38.marks, f32[9,144,128]{2,1,0:T(8,128)S(1)} %inside.2.main, f32[216,128]{1,0:T(8,128)S(1)} %collective-permute-done.6.got_a, ...), custom_call_target="tpu_custom_call" | custom-call | tf_op jit(solution)/shard_map/middle/pallas_call | solution.py:21
  34.0 0.6 %collective-permute-start.8 = (f32[144,128]{1,0:T(8,128)S(1)}, f32[144,128]{1,0:T(8,128)S(1)}, u32[]{:S(2)}, u32[]{:S(2)}) collective-permute-start(f32[144,128]{1,0:T(8,128)S(1)} %get-tuple-element.44), channel_id=1, source_target_pairs={{0,1},{1,0},{2,3},{3,2},{4,5},{5,4},{6,7},{7,6},{8,9},{9,8},{10,11... | collective-permute-start | bytes 221192 | tf_op jit(solution)/shard_map/ppermute | solution.py:459
  34.6 0.9 %collective-permute-done.8.middle = f32[144,128]{1,0:T(8,128)S(1)} collective-permute-done((f32[144,128]{1,0:T(8,128)S(1)}, f32[144,128]{1,0:T(8,128)S(1)}, u32[]{:S(2)}, u32[]{:S(2)}) %collective-permute-start.8) | collective-permute-done | bytes 73760 | tf_op jit(solution)/shard_map/ppermute | solution.py:459
  35.5 0.1 faces.3
  35.6 0.7 %collective-permute-start.9 = (f32[216,128]{1,0:T(8,128)S(1)}, f32[216,128]{1,0:T(8,128)S(1)}, u32[]{:S(2)}, u32[]{:S(2)}) collective-permute-start(f32[216,128]{1,0:T(8,128)S(1)} %get-tuple-element.45), channel_id=1, source_target_pairs={{0,4},{1,5},{2,6},{3,7},{4,0},{5,1},{6,2},{7,3},{8,12},{9,13},{10,... | collective-permute-start | bytes 331784 | tf_op jit(solution)/shard_map/ppermute | solution.py:459
  36.3 1.2 %collective-permute-start.10 = (f32[216,128]{1,0:T(8,128)S(1)}, f32[216,128]{1,0:T(8,128)S(1)}, u32[]{:S(2)}, u32[]{:S(2)}) collective-permute-start(f32[216,128]{1,0:T(8,128)S(1)} %get-tuple-element.46), channel_id=1, source_target_pairs={{0,1},{1,0},{2,3},{3,2},{4,8},{5,9},{6,10},{7,11},{8,4},{9,5},{10,... | collective-permute-start | bytes 331784 | tf_op jit(solution)/shard_map/ppermute | solution.py:459
  37.5 3.9 %inside.3.main = f32[8,128,128]{2,1,0:T(8,128)S(1)} custom-call(f32[10,144,128]{2,1,0:T(8,128)S(1)} %get-tuple-element.43.x, f32[144,128]{1,0:T(8,128)S(1)} %collective-permute-done.8.middle, bf16[9,128,384]{2,1,0:T(8,128)(2,1)S(1)} %get-tuple-element.32.ready.single, bf16[9,128,768]{2,1,0:T(8,128)(2,1)S(1)} %get-tuple-element.40.double), custom_call_target="tpu_custom_call" | custom-call | tf_op jit(solution)/shard_map/inside/pallas_call | solution.py:21
  41.4 0.0 copy-start
  41.4 0.0 copy-start.2
  41.4 0.0 collective-permute-done.9.got_a
  41.4 0.0 collective-permute-done.10.got_b
  41.4 1.1 %last.1 = (f32[256,128]{1,0:T(8,128)S(1)}, f32[256,128]{1,0:T(8,128)S(1)}, f32[256,128]{1,0:T(8,128)S(1)}, f32[256,128]{1,0:T(8,128)S(1)}) custom-call(f32[8,128,128]{2,1,0:T(8,128)S(1)} %inside.3.main, f32[216,128]{1,0:T(8,128)S(1)} %collective-permute-done.9.got_a, f32[216,128]{1,0:T(8,128)S(1)} %collective-permute-done.10.got_b, ...), custom_call_target="tpu_custom_call" | custom-call | tf_op jit(solution)/shard_map/last/pallas_call | solution.py:21
  42.5 1.5 %collective-permute-start.13 = (f32[256,128]{1,0:T(8,128)S(1)}, f32[256,128]{1,0:T(8,128)S(1)}, u32[]{:S(2)}, u32[]{:S(2)}) collective-permute-start(f32[256,128]{1,0:T(8,128)S(1)} %get-tuple-element.50), channel_id=1, source_target_pairs={{0,13},{1,12},{2,15},{3,14},{4,9},{5,8},{6,11},{7,10},{8,5},{9,4},... | collective-permute-start | bytes 393224 | tf_op jit(solution)/shard_map/ppermute | solution.py:459
  44.0 1.1 %collective-permute-start.11 = (f32[256,128]{1,0:T(8,128)S(1)}, f32[256,128]{1,0:T(8,128)S(1)}, u32[]{:S(2)}, u32[]{:S(2)}) collective-permute-start(f32[256,128]{1,0:T(8,128)S(1)} %get-tuple-element.47), channel_id=1, source_target_pairs={{0,2},{1,3},{2,0},{3,1},{4,6},{5,7},{6,4},{7,5},{8,10},{9,11},{10,... | collective-permute-start | bytes 393224 | tf_op jit(solution)/shard_map/ppermute | solution.py:459
  45.1 0.6 %collective-permute-start.12 = (f32[256,128]{1,0:T(8,128)S(1)}, f32[256,128]{1,0:T(8,128)S(1)}, u32[]{:S(2)}, u32[]{:S(2)}) collective-permute-start(f32[256,128]{1,0:T(8,128)S(1)} %get-tuple-element.48), channel_id=1, source_target_pairs={{0,15},{1,14},{2,13},{3,12},{4,11},{5,10},{6,9},{7,8},{8,7},{9,6},... | collective-permute-start | bytes 393224 | tf_op jit(solution)/shard_map/ppermute | solution.py:459
  45.8 8.5 %collective-permute-done.13.mirrored = f32[256,128]{1,0:T(8,128)S(1)} collective-permute-done((f32[256,128]{1,0:T(8,128)S(1)}, f32[256,128]{1,0:T(8,128)S(1)}, u32[]{:S(2)}, u32[]{:S(2)}) %collective-permute-start.13) | collective-permute-done | bytes 131104 | tf_op jit(solution)/shard_map/ppermute | solution.py:459
  54.2 0.0 copy-done
  54.2 0.0 copy-done.2
  54.2 1.3 %unpack.2.refs_0_ = f32[32,16,8,32]{3,2,1,0:T(8,128)} custom-call(f32[32,16,8,32]{3,2,1,0:T(8,128)S(1)} %bitcast.5, s32[16,8,32]{2,1,0:T(8,128)S(1)} %copy-done.2, f32[256,128]{1,0:T(8,128)S(1)} %get-tuple-element.49.own, f32[256,128]{1,0:T(8,128)S(1)} %collective-permute-done.13.mirrored), custom_call_target="tpu_custom_call" | custom-call | tf_op jit(solution)/shard_map/unpack/pallas_call | solution.py:21
  55.5 0.0 collective-permute-done.11.own
  55.5 2.3 %collective-permute-done.12.mirrored = f32[256,128]{1,0:T(8,128)S(1)} collective-permute-done((f32[256,128]{1,0:T(8,128)S(1)}, f32[256,128]{1,0:T(8,128)S(1)}, u32[]{:S(2)}, u32[]{:S(2)}) %collective-permute-start.12) | collective-permute-done | bytes 131104 | tf_op jit(solution)/shard_map/ppermute | solution.py:459
  57.9 1.3 %unpack.3 = f32[32,16,8,32]{3,2,1,0:T(8,128)} custom-call(f32[32,16,8,32]{3,2,1,0:T(8,128)S(1)} %bitcast.6, s32[16,8,32]{2,1,0:T(8,128)S(1)} %copy-done.2, f32[256,128]{1,0:T(8,128)S(1)} %collective-permute-done.11.own, f32[256,128]{1,0:T(8,128)S(1)} %collective-permute-done.12.mirrored, f32[32,16,8,32]{3,2,1,0:T(8,128)} %unpack.2.refs_0_), custom_call_target="tpu_custom_call", output_to_operand_aliasing={{}: (4, {})} | custom-call | tf_op jit(solution)/shard_map/unpack/pallas_call | solution.py:21
Async XLA Ops:
  0.0 2.9 %copy-start.1 = (f32[27,2,16,64]{3,2,1,0:T(8,128)S(1)}, f32[27,2,16,64]{3,2,1,0:T(8,128)}, u32[]{:S(2)}) copy-start(f32[27,2,16,64]{3,2,1,0:T(8,128)} %param.5) | copy-start | bytes 663556
  2.9 21.5 %copy-start.3 = (f32[384,128]{1,0:T(8,128)S(1)}, f32[384,128]{1,0:T(8,128)}, u32[]{:S(2)}) copy-start(f32[384,128]{1,0:T(8,128)} %get-tuple-element.33.refs_0_) | copy-start | bytes 589828
  3.0 7.8 %collective-permute-start = (f32[27,8,128]{2,1,0:T(8,128)S(1)}, f32[27,8,128]{2,1,0:T(8,128)S(1)}, u32[]{:S(2)}, u32[]{:S(2)}) collective-permute-start(f32[27,8,128]{2,1,0:T(8,128)S(1)} %fold.1), channel_id=1, source_target_pairs={{0,2},{1,3},{2,0},{3,1},{4,6},{5,7},{6,4},{7,5},{8,10},{9,11},{10,... | collective-permute-start | bytes 331784 | tf_op jit(solution)/shard_map/ppermute | solution.py:459
  4.3 20.1 %collective-permute-start.2 = (f32[384,128]{1,0:T(8,128)}, f32[384,128]{1,0:T(8,128)S(1)}, u32[]{:S(2)}, u32[]{:S(2)}) collective-permute-start(f32[384,128]{1,0:T(8,128)} %get-tuple-element.34), channel_id=1, source_target_pairs={{0,13},{1,12},{2,15},{3,14},{4,9},{5,8},{6,11},{7,10},{8,5},{9,4},... | collective-permute-start | bytes 589832 | tf_op jit(solution)/shard_map/ppermute | solution.py:459
  9.2 7.0 %collective-permute-start.3 = (f32[368,128]{1,0:T(8,128)}, f32[368,128]{1,0:T(8,128)S(1)}, u32[]{:S(2)}, u32[]{:S(2)}) collective-permute-start(f32[368,128]{1,0:T(8,128)} %get-tuple-element.35), channel_id=1, source_target_pairs={{0,2},{1,3},{2,0},{3,1},{4,6},{5,7},{6,4},{7,5},{8,10},{9,11},{10,... | collective-permute-start | bytes 565256 | tf_op jit(solution)/shard_map/ppermute | solution.py:459
  9.5 14.8 %collective-permute-start.4 = (f32[368,128]{1,0:T(8,128)}, f32[368,128]{1,0:T(8,128)S(1)}, u32[]{:S(2)}, u32[]{:S(2)}) collective-permute-start(f32[368,128]{1,0:T(8,128)} %get-tuple-element.36), channel_id=1, source_target_pairs={{0,15},{1,14},{2,13},{3,12},{4,11},{5,10},{6,9},{7,8},{8,7},{9,6},... | collective-permute-start | bytes 565256 | tf_op jit(solution)/shard_map/ppermute | solution.py:459
  10.8 1.3 %collective-permute-start.1 = (f32[27,8,128]{2,1,0:T(8,128)S(1)}, f32[27,8,128]{2,1,0:T(8,128)S(1)}, u32[]{:S(2)}, u32[]{:S(2)}) collective-permute-start(f32[27,8,128]{2,1,0:T(8,128)S(1)} %collective-permute-done.refs_0_), channel_id=1, source_target_pairs={{0,1},{1,0},{2,3},{3,2},{4,5},{5,4},{6,7},{7,6},{8,9},{9,8},{10,11... | collective-permute-start | bytes 331784 | tf_op jit(solution)/shard_map/ppermute | solution.py:459
  25.4 1.4 %collective-permute-start.5 = (f32[144,128]{1,0:T(8,128)S(1)}, f32[144,128]{1,0:T(8,128)S(1)}, u32[]{:S(2)}, u32[]{:S(2)}) collective-permute-start(f32[144,128]{1,0:T(8,128)S(1)} %get-tuple-element.39), channel_id=1, source_target_pairs={{0,1},{1,0},{2,3},{3,2},{4,5},{5,4},{6,7},{7,6},{8,9},{9,8},{10,11... | collective-permute-start | bytes 221192 | tf_op jit(solution)/shard_map/ppermute | solution.py:459
  26.8 6.1 %collective-permute-start.6 = (f32[216,128]{1,0:T(8,128)S(1)}, f32[216,128]{1,0:T(8,128)S(1)}, u32[]{:S(2)}, u32[]{:S(2)}) collective-permute-start(f32[216,128]{1,0:T(8,128)S(1)} %get-tuple-element.41), channel_id=1, source_target_pairs={{0,4},{1,5},{2,6},{3,7},{4,0},{5,1},{6,2},{7,3},{8,12},{9,13},{10,... | collective-permute-start | bytes 331784 | tf_op jit(solution)/shard_map/ppermute | solution.py:459
  26.9 6.0 %collective-permute-start.7 = (f32[216,128]{1,0:T(8,128)S(1)}, f32[216,128]{1,0:T(8,128)S(1)}, u32[]{:S(2)}, u32[]{:S(2)}) collective-permute-start(f32[216,128]{1,0:T(8,128)S(1)} %get-tuple-element.42), channel_id=1, source_target_pairs={{0,1},{1,0},{2,3},{3,2},{4,8},{5,9},{6,10},{7,11},{8,4},{9,5},{10,... | collective-permute-start | bytes 331784 | tf_op jit(solution)/shard_map/ppermute | solution.py:459
  34.0 1.5 %collective-permute-start.8 = (f32[144,128]{1,0:T(8,128)S(1)}, f32[144,128]{1,0:T(8,128)S(1)}, u32[]{:S(2)}, u32[]{:S(2)}) collective-permute-start(f32[144,128]{1,0:T(8,128)S(1)} %get-tuple-element.44), channel_id=1, source_target_pairs={{0,1},{1,0},{2,3},{3,2},{4,5},{5,4},{6,7},{7,6},{8,9},{9,8},{10,11... | collective-permute-start | bytes 221192 | tf_op jit(solution)/shard_map/ppermute | solution.py:459
  35.6 5.8 %collective-permute-start.9 = (f32[216,128]{1,0:T(8,128)S(1)}, f32[216,128]{1,0:T(8,128)S(1)}, u32[]{:S(2)}, u32[]{:S(2)}) collective-permute-start(f32[216,128]{1,0:T(8,128)S(1)} %get-tuple-element.45), channel_id=1, source_target_pairs={{0,4},{1,5},{2,6},{3,7},{4,0},{5,1},{6,2},{7,3},{8,12},{9,13},{10,... | collective-permute-start | bytes 331784 | tf_op jit(solution)/shard_map/ppermute | solution.py:459
  36.3 5.1 %collective-permute-start.10 = (f32[216,128]{1,0:T(8,128)S(1)}, f32[216,128]{1,0:T(8,128)S(1)}, u32[]{:S(2)}, u32[]{:S(2)}) collective-permute-start(f32[216,128]{1,0:T(8,128)S(1)} %get-tuple-element.46), channel_id=1, source_target_pairs={{0,1},{1,0},{2,3},{3,2},{4,8},{5,9},{6,10},{7,11},{8,4},{9,5},{10,... | collective-permute-start | bytes 331784 | tf_op jit(solution)/shard_map/ppermute | solution.py:459
  41.4 12.9 %copy-start = (f32[2,16,16,8,32]{4,3,2,1,0:T(8,128)S(1)}, f32[2,16,16,8,32]{4,3,2,1,0:T(8,128)}, u32[]{:S(2)}) copy-start(f32[2,16,16,8,32]{4,3,2,1,0:T(8,128)} %param.3) | copy-start | bytes 1572868
  41.4 12.8 %copy-start.2 = (s32[16,8,32]{2,1,0:T(8,128)S(1)}, s32[16,8,32]{2,1,0:T(8,128)}, u32[]{:S(2)}) copy-start(s32[16,8,32]{2,1,0:T(8,128)} %mask.4) | copy-start | bytes 49156
  42.5 11.7 %collective-permute-start.13 = (f32[256,128]{1,0:T(8,128)S(1)}, f32[256,128]{1,0:T(8,128)S(1)}, u32[]{:S(2)}, u32[]{:S(2)}) collective-permute-start(f32[256,128]{1,0:T(8,128)S(1)} %get-tuple-element.50), channel_id=1, source_target_pairs={{0,13},{1,12},{2,15},{3,14},{4,9},{5,8},{6,11},{7,10},{8,5},{9,4},... | collective-permute-start | bytes 393224 | tf_op jit(solution)/shard_map/ppermute | solution.py:459
  44.0 11.5 %collective-permute-start.11 = (f32[256,128]{1,0:T(8,128)S(1)}, f32[256,128]{1,0:T(8,128)S(1)}, u32[]{:S(2)}, u32[]{:S(2)}) collective-permute-start(f32[256,128]{1,0:T(8,128)S(1)} %get-tuple-element.47), channel_id=1, source_target_pairs={{0,2},{1,3},{2,0},{3,1},{4,6},{5,7},{6,4},{7,5},{8,10},{9,11},{10,... | collective-permute-start | bytes 393224 | tf_op jit(solution)/shard_map/ppermute | solution.py:459
  45.1 12.8 %collective-permute-start.12 = (f32[256,128]{1,0:T(8,128)S(1)}, f32[256,128]{1,0:T(8,128)S(1)}, u32[]{:S(2)}, u32[]{:S(2)}) collective-permute-start(f32[256,128]{1,0:T(8,128)S(1)} %get-tuple-element.48), channel_id=1, source_target_pairs={{0,15},{1,14},{2,13},{3,12},{4,11},{5,10},{6,9},{7,8},{8,7},{9,6},... | collective-permute-start | bytes 393224 | tf_op jit(solution)/shard_map/ppermute | solution.py:459

commit v5 on v4

--- a/solution.py
+++ b/solution.py
@@ -9,6 +9,7 @@
 
 ITERS = 2
 PACK = 56 << 20
+LITTLE = pl.CostEstimate(flops=1000, bytes_accessed=1000, transcendentals=0)
 AXES = ("kz", "coil", "kx")
 F32 = jnp.float32
 BF16 = jnp.bfloat16
@@ -17,7 +18,7 @@
 VMEM = pl.BlockSpec(memory_space=pltpu.VMEM)
 
 
-def call(body, name, args, shapes, scratch=(), far=(), space=ANY, out=VMEM, limit=48 << 20, **options):
+def call(body, name, args, shapes, scratch=(), far=(), space=ANY, out=VMEM, limit=48 << 20, cost=None, **options):
     return pl.pallas_call(
         body,
         out_shape=shapes,
@@ -25,6 +26,7 @@
         out_specs=[out] * len(shapes),
         scratch_shapes=list(scratch),
         compiler_params=pltpu.CompilerParams(vmem_limit_bytes=limit),
+        cost_estimate=cost,
         name=name,
         **options,
     )(*args)
@@ -116,7 +118,7 @@
     sampled = [marks[j] == 1 for j in range(S)]
     kept = [jnp.where(sampled[j][None], rows[:, j], 0.0) for j in range(S)]
     kept = jnp.concatenate(kept, -1).reshape(ch * D, S * W)
-    if d == 0:
+    if d < 2:
         kept = jnp.concatenate([kept, jnp.concatenate([jnp.where(s, 1.0, 0.0) for s in sampled], -1)], 0)
     hi, lo = split(kept)
     y = dot(hi, order) + dot(lo, order)
@@ -132,13 +134,13 @@
         for i in range(cut.folds):
             place = 2 * part + i * group
             out[place : place + group] = folded[:, i * 128 : (i + 1) * 128]
-        if d == 0:
+        if d == side:
             out[cut.length : cut.length + D] = y[2 * part :, 128 * side : 128 * side + 128]
             out[cut.length + D :] = jnp.concatenate([spare[2 * part :], jnp.zeros((D, 64), F32)], 1)
 
 
 def pack(d, measured, mask, cut):
-    shapes = [jax.ShapeDtypeStruct((cut.length + (0 if d else 2 * cut.D), 128), F32)] * 2
+    shapes = [jax.ShapeDtypeStruct((cut.length + (2 * cut.D if d == side else 0), 128), F32) for side in range(2)]
     scratch = [
         pltpu.VMEM((cut.ch, cut.S, cut.D, cut.W), F32),
         pltpu.VMEM((cut.S, cut.D, cut.W), jnp.int32),
@@ -204,69 +206,86 @@
     N = cut.channels
     shapes = [jax.ShapeDtypeStruct((9, N, 3 * N), BF16), jax.ShapeDtypeStruct((9, N, 6 * N), BF16)]
     scratch = [pltpu.VMEM((count, coils * cut.C, inputs), F32)]
-    return call(functools.partial(weights_kernel, cut), "weights", (kernel, *folded), shapes, scratch)
+    return call(functools.partial(weights_kernel, cut), "weights", (kernel, *folded), shapes, scratch, cost=LITTLE)
 
 
 def middle_row(cut, x):
     return jnp.where(lax.axis_index("kx") == 0, x[cut.S - 1], x[0])
 
 
-def points_kernel(cut, ready, *refs):
-    C, D, H, S, half = cut.C, cut.D, cut.H, cut.S, cut.half
-    msgs, (x, marks, middle, main, spare) = refs[: 2 * C], refs[2 * C :]
-    part = cut.part
-    for d in range(C):
+def spread(cut, target, k, first, rest):
+    D, H, S = cut.D, cut.H, cut.S
+    for r in range(cut.base):
+        target[r, pl.ds(k, H, stride=D)] = first[r * H : (r + 1) * H]
+    for r in range(cut.base, S):
+        target[r, pl.ds(k, H, stride=D)] = rest[(r - cut.base) * H : (r - cut.base + 1) * H]
+    for r in range(S):
+        place = cut.spare + 2 * r
+        target[r, pl.ds(H * D + k, 2, stride=D)] = rest[place : place + 2]
+
+
+def assemble(cut, side, msgs, x, main, spare):
+    D, half, part = cut.D, cut.half, cut.part
+    for d, msg in enumerate(msgs):
         other = lax.bitwise_xor(lax.axis_index("coil"), d)
-        for side in range(2):
-            msg = msgs[2 * d + side]
-            for ri in range(2):
-                start = pl.multiple_of(((side * 2 + ri) * C + other) * part, part)
-                main[pl.ds(start, part)] = msg[ri * part : (ri + 1) * part]
-            folded = msg[2 * part : cut.length].reshape(cut.folds, cut.group, 128)
-            folded = jnp.concatenate([folded[i] for i in range(cut.folds)], 1)
-            for i in range(16):
-                ri, rest = i // 8, i % 8 * cut.group
-                start = pl.multiple_of(((side * 2 + ri) * C + other) * part + rest, cut.group)
-                spare[pl.ds(start, cut.group), : cut.used] = folded[:, i * cut.used : (i + 1) * cut.used]
-
-    def spread(target, k, first, rest):
-        for r in range(cut.base):
-            target[r, pl.ds(k, H, stride=D)] = first[r * H : (r + 1) * H]
-        for r in range(cut.base, S):
-            target[r, pl.ds(k, H, stride=D)] = rest[(r - cut.base) * H : (r - cut.base + 1) * H]
-        for r in range(S):
-            place = cut.spare + 2 * r
-            target[r, pl.ds(H * D + k, 2, stride=D)] = rest[place : place + 2]
-
+        folded = msg[2 * part : cut.length].reshape(cut.folds, cut.group, 128)
+        folded = jnp.concatenate([folded[i] for i in range(cut.folds)], 1)
+        for ri in range(2):
+            start = pl.multiple_of((ri * cut.C + other) * part, part)
+            main[pl.ds(start, part)] = msg[ri * part : (ri + 1) * part]
+        for i in range(16):
+            start = pl.multiple_of((i // 8 * cut.C + other) * part + i % 8 * cut.group, cut.group)
+            spare[pl.ds(start, cut.group), : cut.used] = folded[:, i * cut.used : (i + 1) * cut.used]
+    gap = jnp.zeros((half, 128), F32)
+    for k in range(D):
+        some = pl.ds(D - 1 - k if side else k, half, stride=D)
+        blocks = [jnp.concatenate([gap, v] if side else [v, gap], 0).T for v in (main[some], spare[some])]
+        spread(cut, x, k, *blocks)
+
+
+def physical_kernel(cut, ready, *refs):
+    msgs, (x, main, spare) = refs[: cut.C], refs[cut.C :]
+    assemble(cut, 0, msgs, x, main, spare)
+
+
+def mirrored_kernel(cut, physical, *refs):
+    msgs, (x, middle, main, spare) = refs[: cut.C], refs[-4:]
+    assemble(cut, 1, msgs, x, main, spare)
+    x[...] = x[...] + physical[...]
+    middle[...] = middle_row(cut, x)
+
+
+def marks_kernel(cut, ready, own, other, marks):
+    D, half = cut.D, cut.half
     lane = lax.broadcasted_iota(jnp.int32, (128, cut.channels), 1)
-    flags = [msgs[side][cut.length : cut.length + 2 * D] for side in range(2)]
+    flags = [msg[cut.length : cut.length + 2 * D] for msg in (own, other)]
     flags = jnp.concatenate(flags + [jnp.zeros((128 - 4 * D, 128), F32)], 0).T
     for k in range(D):
         j = D - 1 - k
-        mine = main[pl.ds(k, half, stride=D)]
-        other = main[pl.ds(half * D + j, half, stride=D)]
-        first = jnp.concatenate([mine, other], 0).T
-        mine = spare[pl.ds(k, half, stride=D)]
-        other = spare[pl.ds(half * D + j, half, stride=D)]
-        rest = jnp.concatenate([mine, other], 0).T
-        spread(x, k, first, rest)
         first = jnp.where(lane < half, flags[:, k : k + 1], flags[:, 2 * D + j : 2 * D + j + 1])
         rest = jnp.where(lane < half, flags[:, D + k : D + k + 1], flags[:, 3 * D + j : 3 * D + j + 1])
-        spread(marks, k, first, rest)
-    middle[...] = middle_row(cut, x)
-
-
-def points(ready, msgs, cut):
+        spread(cut, marks, k, first, rest)
+
+
+def points(cut, weights, msgs):
     row = (cut.V * cut.D, cut.channels)
     window = jax.ShapeDtypeStruct((cut.S, *row), F32)
-    return call(
-        functools.partial(points_kernel, cut),
-        "points",
-        (ready, *msgs),
-        [window, window, jax.ShapeDtypeStruct(row, F32)],
-        [pltpu.VMEM((cut.channels * cut.D, 128), F32)] * 2,
-        far=(0,),
+    stages = [pltpu.VMEM((cut.half * cut.D, 128), F32)] * 2
+    args = (weights[0], *msgs[0::2])
+    (x,) = call(functools.partial(physical_kernel, cut), "physical", args, [window], stages, far=(0,), cost=LITTLE)
+    added = inside_half(0, x, weights, cut)
+    flags = (added, msgs[0], msgs[3])
+    (marks,) = call(functools.partial(marks_kernel, cut), "marks", flags, [window], far=(0,), cost=LITTLE)
+    args = (x, *msgs[1::2], added, marks)
+    x, middle = call(
+        functools.partial(mirrored_kernel, cut),
+        "mirrored",
+        args,
+        [window, jax.ShapeDtypeStruct(row, F32)],
+        stages,
+        far=(len(args) - 2, len(args) - 1),
     )
+    return x, marks, middle, added
 
 
 def beside(cut, middle):
@@ -311,6 +330,14 @@
     ]
 
 
+def shifted(y, D):
+    M = y[0].shape[0]
+    rows = lax.broadcasted_iota(jnp.int32, y[0].shape, 0) % D
+    later = jnp.where(rows == 0, 0.0, pltpu.roll(y[0], 1, 0))
+    sooner = jnp.where(rows == D - 1, 0.0, pltpu.roll(y[2], M - 1, 0))
+    return y[1] + later + sooner
+
+
 def inside_kernel(cut, last, x, middle, single, double, out, hi, lo):
     D, S = cut.D, cut.S
     count, L, channels = out.shape
@@ -337,10 +364,7 @@
 
     K = 9 * channels
     y = multiply(window(hi), window(lo), single[...].reshape(K, -1), double[...].reshape(K, -1))
-    rows = lax.broadcasted_iota(jnp.int32, (count * L, channels), 0) % D
-    later = jnp.where(rows == 0, 0.0, pltpu.roll(y[0], 1, 0))
-    sooner = jnp.where(rows == D - 1, 0.0, pltpu.roll(y[2], count * L - 1, 0))
-    out[...] = (y[1] + later + sooner).reshape(count, L, channels)
+    out[...] = shifted(y, D).reshape(count, L, channels)
 
 
 def inside(x, middle, weights, cut, last):
@@ -349,6 +373,76 @@
     out = jax.ShapeDtypeStruct((count, L, cut.channels), F32)
     scratch = [pltpu.VMEM((3, cut.slots, cut.V * cut.D, cut.channels), BF16)] * 2
     return call(functools.partial(inside_kernel, cut, last), "inside", (x, middle, *weights), [out], scratch)[0]
+
+
+def half_weights(weights, side, half):
+    rows = slice(half, 2 * half) if side else slice(0, half)
+    order = [0, 1, 3, 4, 6, 7, 2, 5, 8]
+    picked = [weights[tap, rows] for tap in order]
+    return jnp.concatenate(picked + [jnp.zeros_like(picked[0])], 0)
+
+
+def inside_half_kernel(cut, side, x, *refs):
+    if side:
+        middle, added, single, double, out, hi, lo = refs
+    else:
+        single, double, out, hi, lo = refs
+    D, S, half = cut.D, cut.S, cut.half
+    count, L, channels = out.shape
+    gap = jnp.zeros((D, channels), F32)
+    left = lax.broadcasted_iota(jnp.int32, (L, channels), 1) < half
+
+    def pair(one, two):
+        return jnp.where(left, one[side], two[1 - side])
+
+    none = (jnp.zeros((L, channels), F32),) * 2
+
+    def versions(slot):
+        if not 1 <= slot <= S:
+            return none, none, none
+        row = x[slot - 1]
+        both = (row, pltpu.roll(row, half, 1))
+        sooner = tuple(jnp.concatenate([gap, v[:-D]], 0) for v in both)
+        later = tuple(jnp.concatenate([v[D:], gap], 0) for v in both)
+        return sooner, both, later
+
+    following = versions(0)
+    for slot in range(cut.slots):
+        now, following = following, versions(slot + 1)
+        for i, value in enumerate((pair(now[0], now[1]), pair(now[2], following[2]))):
+            hi[i, slot], lo[i, slot] = split(value)
+    first, _ = cut.range_of(False)
+
+    def window(ref):
+        columns = [(0, 0), (0, 1), (0, 2), (1, 0), (1, 2)]
+        return jnp.concatenate(
+            [jnp.concatenate([ref[i, first + j + a] for j in range(count)], 0) for i, a in columns], 1
+        )
+
+    y = multiply(window(hi), window(lo), *(half_weights(w, side, half) for w in (single, double)))
+    y = shifted(y, D).reshape(count, L, channels)
+    if not side:
+        out[...] = y
+        return
+    out[...] = y + added[...]
+    _, c, core = place()
+    row = middle[...]
+    parts = [split(v) for v in (jnp.concatenate([gap, row[:-D]], 0), row, jnp.concatenate([row[D:], gap], 0))]
+    taps = pl.ds(jnp.where(core == 0, 6, 0), 3)
+    one, two = (w[taps].reshape(3 * channels, -1) for w in (single, double))
+    y = shifted(multiply(*(jnp.concatenate([p[i] for p in parts], 1) for i in range(2)), one, two), D)
+    target = jnp.where(core == 0, count - 1, 0)
+    out[target] += jnp.where(c == cut.C - 1, y, 0.0)
+
+
+def inside_half(side, x, weights, cut, *more):
+    count = cut.range_of(False)[1]
+    L = cut.V * cut.D
+    out = jax.ShapeDtypeStruct((count, L, cut.channels), F32)
+    scratch = [pltpu.VMEM((2, cut.slots, L, cut.channels), BF16)] * 2
+    body = functools.partial(inside_half_kernel, cut, side)
+    cost = None if side else LITTLE
+    return call(body, "inside_mirrored" if side else "inside_physical", (x, *more, *weights), [out], scratch, cost=cost)[0]
 
 
 def add_planes(cut, last, target, offset, count, got_a, got_b, single, double, planes):
@@ -480,23 +574,23 @@
     cut = Cut(rows, D, W, C, 2 * parts * coils * C)
     flat = measured.reshape(parts * coils, rows, D, W)
     kernel = kernel.reshape(-1, *kernel.shape[2:])
-    msgs = pack(0, flat, mask, cut)
-    for d in range(1, C):
-        kernel, mask, *msgs = lax.optimization_barrier((kernel, mask, *msgs))
-        msgs = [*msgs, *pack(d, flat, mask, cut)]
+    msgs = []
+    for d in reversed(range(C)):
+        msgs = [*pack(d, flat, mask, cut), *msgs]
+        kernel, mask, *msgs = lax.optimization_barrier((kernel, mask, *msgs)) if d else (kernel, mask, *msgs)
     msgs = exchange(msgs)
     folded = []
     for d in range(1, C):
         half = send(fold(kernel), lambda z, c, x: (z, c ^ d, x))
         folded += [half, send(half, core)]
     weights = build_weights(kernel, folded, cut)
-    state, marks, row = points(weights[0], msgs, cut)
+    state, marks, row, added = points(cut, weights, msgs)
     for step in range(ITERS):
         last = step == ITERS - 1
         row = send(row, core)
         face_a, face_b = faces(state, row, cut)
         got_a, got_b = send(face_a, plane_a), send(face_b, plane_b)
-        main = inside(state, row, weights, cut, last)
+        main = inside(state, row, weights, cut, last) if step else inside_half(1, state, weights, cut, row, added)
         if not last:
             state, row = call(
                 functools.partial(middle_kernel, cut),

time: 59.5 us -> 57.6 us (0.968)
  waiting for transfers between devices: 24.1 us -> 19.1 us
  Pallas kernels: 22.1 us -> 24.3 us
  local copies, waits for them, and re-layouts: 0.02 us -> 0.94 us
    ppermute x14, waiting for transfers between devices: 24.1 us -> 19.1 us  [send(): lax.ppermute(array, AXES, [(index(*p), index(*target(*p))) for p in every])]
    pallas_call x13 -> x16, Pallas kernels: 22.1 us -> 24.3 us  [call(): pl.pallas_call(body, out_shape=shapes, in_specs=[space if i in far else V...]
    unnamed x8, local copies, waits for them, and re-layouts: 0.02 us -> 0.94 us
  transfers between devices with their start and end apart: 14 -> 14, of which waited for: 7 -> 8; matrix products, arithmetic and copies ran while one was open for 0% -> 0% of each run, Pallas kernels for 25% -> 30%
where the time goes in v5:
time: 57.6 us; the launch traced here: 57.5 us
  Pallas kernels  24.3 us (42%)
  waiting for transfers between devices  19.1 us (33%)
  starting transfers between devices  12.8 us (22%)
  local copies, waits for them, and re-layouts  0.94 us (2%)
    pallas_call x16, Pallas kernels, call(): pl.pallas_call(body, out_shape=shapes, in_specs=[space if i in far else V...  24.3 us
    ppermute x14, waiting for transfers between devices, send(): lax.ppermute(array, AXES, [(index(*p), index(*target(*p))) for p in every])  19.1 us
    ppermute x14, starting transfers between devices, send(): lax.ppermute(array, AXES, [(index(*p), index(*target(*p))) for p in every])  12.8 us
  transfers between devices with their start and end apart: 14, of which 8 were waited for; matrix products, arithmetic and copies ran while one was open for 0% of the time, Pallas kernels for 30%

profile of v5, /device:TPU:9, one launch (start us, length us, event | category | flops | bytes accessed | tf_op | source)
XLA Modules:
  0.0 57.5 jit_solution(6128329366726533132)
XLA Ops:
  0.0 0.0 copy-start.1
  0.0 2.9 %pack.2 = (f32[368,128]{1,0:T(8,128)}, f32[384,128]{1,0:T(8,128)}) custom-call(f32[32,16,8,32]{3,2,1,0:T(8,128)} %bitcast.3, s32[16,8,32]{2,1,0:T(8,128)} %mask.4), custom_call_target="tpu_custom_call" | custom-call | tf_op jit(solution)/shard_map/pack/pallas_call | solution.py:22
  2.9 0.0 copy-done.1
  2.9 0.1 fold.1
  3.0 1.3 %collective-permute-start = (f32[27,8,128]{2,1,0:T(8,128)S(1)}, f32[27,8,128]{2,1,0:T(8,128)S(1)}, u32[]{:S(2)}, u32[]{:S(2)}) collective-permute-start(f32[27,8,128]{2,1,0:T(8,128)S(1)} %fold.1), channel_id=1, source_target_pairs={{0,2},{1,3},{2,0},{3,1},{4,6},{5,7},{6,4},{7,5},{8,10},{9,11},{10,... | collective-permute-start | bytes 331784 | tf_op jit(solution)/shard_map/ppermute | solution.py:553
  4.3 2.1 %collective-permute-start.4 = (f32[384,128]{1,0:T(8,128)}, f32[384,128]{1,0:T(8,128)S(1)}, u32[]{:S(2)}, u32[]{:S(2)}) collective-permute-start(f32[384,128]{1,0:T(8,128)} %get-tuple-element.35), channel_id=1, source_target_pairs={{0,15},{1,14},{2,13},{3,12},{4,11},{5,10},{6,9},{7,8},{8,7},{9,6},... | collective-permute-start | bytes 589832 | tf_op jit(solution)/shard_map/ppermute | solution.py:553
  6.4 1.2 %collective-permute-start.2 = (f32[368,128]{1,0:T(8,128)}, f32[368,128]{1,0:T(8,128)S(1)}, u32[]{:S(2)}, u32[]{:S(2)}) collective-permute-start(f32[368,128]{1,0:T(8,128)} %get-tuple-element.33), channel_id=1, source_target_pairs={{0,2},{1,3},{2,0},{3,1},{4,6},{5,7},{6,4},{7,5},{8,10},{9,11},{10,... | collective-permute-start | bytes 565256 | tf_op jit(solution)/shard_map/ppermute | solution.py:553
  7.6 2.8 %pack.3 = (f32[384,128]{1,0:T(8,128)}, f32[368,128]{1,0:T(8,128)}) custom-call(f32[32,16,8,32]{3,2,1,0:T(8,128)} %bitcast.4, s32[16,8,32]{2,1,0:T(8,128)} %mask.4), custom_call_target="tpu_custom_call" | custom-call | tf_op jit(solution)/shard_map/pack/pallas_call | solution.py:22
  10.4 0.1 collective-permute-start.3
  10.5 0.0 collective-permute-done.refs_0_
  10.5 0.5 collective-permute-start.1
  11.1 1.0 %collective-permute-done.1.refs_1_ = f32[27,8,128]{2,1,0:T(8,128)S(1)} collective-permute-done((f32[27,8,128]{2,1,0:T(8,128)S(1)}, f32[27,8,128]{2,1,0:T(8,128)S(1)}, u32[]{:S(2)}, u32[]{:S(2)}) %collective-permute-start.1) | collective-permute-done | bytes 110624 | tf_op jit(solution)/shard_map/ppermute | solution.py:553
  12.0 1.9 %weights.1 = (bf16[9,128,384]{2,1,0:T(8,128)(2,1)S(1)}, bf16[9,128,768]{2,1,0:T(8,128)(2,1)S(1)}) custom-call(f32[54,16,64]{2,1,0:T(8,128)S(1)} %bitcast.8, f32[27,8,128]{2,1,0:T(8,128)S(1)} %collective-permute-done.refs_0_, f32[27,8,128]{2,1,0:T(8,128)S(1)} %collective-permute-done.1.refs_1_), custom_call_target="tpu_custom_call" | custom-call | flops 1000 | bytes 1000 | tf_op jit(solution)/shard_map/weights/pallas_call | solution.py:22
  13.9 1.7 %collective-permute-done.2.refs_1_ = f32[368,128]{1,0:T(8,128)S(1)} collective-permute-done((f32[368,128]{1,0:T(8,128)}, f32[368,128]{1,0:T(8,128)S(1)}, u32[]{:S(2)}, u32[]{:S(2)}) %collective-permute-start.2) | collective-permute-done | bytes 188448 | tf_op jit(solution)/shard_map/ppermute | solution.py:553
  15.6 0.0 copy-start.3
  15.6 0.9 %copy-done.3 = f32[384,128]{1,0:T(8,128)S(1)} copy-done((f32[384,128]{1,0:T(8,128)S(1)}, f32[384,128]{1,0:T(8,128)}, u32[]{:S(2)}) %copy-start.3) | copy-done | bytes 196632
  16.6 0.4 physical.1.x
  17.0 3.1 %inside_physical.1.ready.refs_2_.refs_1_ = f32[9,144,128]{2,1,0:T(8,128)S(1)} custom-call(f32[10,144,128]{2,1,0:T(8,128)S(1)} %physical.1.x, bf16[9,128,384]{2,1,0:T(8,128)(2,1)S(1)} %get-tuple-element.31.ready.refs_0_.refs_2_.single, bf16[9,128,768]{2,1,0:T(8,128)(2,1)S(1)} %get-tuple-element.36.refs_1_.refs_3_.double), custom_call_target="tpu_custom_call" | custom-call | flops 1000 | bytes 1000 | tf_op jit(solution)/shard_map/inside_physical/pallas_call | solution.py:22
  20.1 0.8 %collective-permute-done.4.other.refs_1_ = f32[384,128]{1,0:T(8,128)S(1)} collective-permute-done((f32[384,128]{1,0:T(8,128)}, f32[384,128]{1,0:T(8,128)S(1)}, u32[]{:S(2)}, u32[]{:S(2)}) %collective-permute-start.4) | collective-permute-done | bytes 196640 | tf_op jit(solution)/shard_map/ppermute | solution.py:553
  20.9 0.6 %marks.1.refs_3_ = f32[10,144,128]{2,1,0:T(8,128)S(1)} custom-call(f32[9,144,128]{2,1,0:T(8,128)S(1)} %inside_physical.1.ready.refs_2_.refs_1_, f32[384,128]{1,0:T(8,128)S(1)} %copy-done.3, f32[384,128]{1,0:T(8,128)S(1)} %collective-permute-done.4.other.refs_1_), custom_call_target="tpu_custom_call" | custom-call | flops 1000 | bytes 1000 | tf_op jit(solution)/shard_map/marks/pallas_call | solution.py:22
  21.5 2.9 %collective-permute-done.3.refs_0_ = f32[368,128]{1,0:T(8,128)S(1)} collective-permute-done((f32[368,128]{1,0:T(8,128)}, f32[368,128]{1,0:T(8,128)S(1)}, u32[]{:S(2)}, u32[]{:S(2)}) %collective-permute-start.3) | collective-permute-done | bytes 188448 | tf_op jit(solution)/shard_map/ppermute | solution.py:553
  24.4 0.5 mirrored.1
  24.9 0.5 collective-permute-start.5
  25.4 0.9 %collective-permute-done.5.refs_0_.middle = f32[144,128]{1,0:T(8,128)S(1)} collective-permute-done((f32[144,128]{1,0:T(8,128)S(1)}, f32[144,128]{1,0:T(8,128)S(1)}, u32[]{:S(2)}, u32[]{:S(2)}) %collective-permute-start.5) | collective-permute-done | bytes 73760 | tf_op jit(solution)/shard_map/ppermute | solution.py:553
  26.3 0.1 faces.2
  26.4 0.1 collective-permute-start.6
  26.4 1.3 %collective-permute-start.7 = (f32[216,128]{1,0:T(8,128)S(1)}, f32[216,128]{1,0:T(8,128)S(1)}, u32[]{:S(2)}, u32[]{:S(2)}) collective-permute-start(f32[216,128]{1,0:T(8,128)S(1)} %get-tuple-element.40), channel_id=1, source_target_pairs={{0,1},{1,0},{2,3},{3,2},{4,8},{5,9},{6,10},{7,11},{8,4},{9,5},{10,... | collective-permute-start | bytes 331784 | tf_op jit(solution)/shard_map/ppermute | solution.py:553
  27.7 3.3 %inside_mirrored.1.main = f32[9,144,128]{2,1,0:T(8,128)S(1)} custom-call(f32[10,144,128]{2,1,0:T(8,128)S(1)} %get-tuple-element.37.x, f32[144,128]{1,0:T(8,128)S(1)} %collective-permute-done.5.refs_0_.middle, f32[9,144,128]{2,1,0:T(8,128)S(1)} %inside_physical.1.ready.refs_2_.refs_1_, ...), custom_call_target="tpu_custom_call" | custom-call | tf_op jit(solution)/shard_map/inside_mirrored/pallas_call | solution.py:22
  31.0 0.0 collective-permute-done.6.got_a
  31.0 0.0 collective-permute-done.7.got_b
  31.0 1.1 %middle.1 = (f32[10,144,128]{2,1,0:T(8,128)S(1)}, f32[144,128]{1,0:T(8,128)S(1)}) custom-call(f32[10,144,128]{2,1,0:T(8,128)S(1)} %get-tuple-element.37.x, f32[10,144,128]{2,1,0:T(8,128)S(1)} %marks.1.refs_3_, f32[9,144,128]{2,1,0:T(8,128)S(1)} %inside_mirrored.1.main, f32[216,128]{1,0:T(8,128)S(1)} %collective-permute-done.6.got_a, ...), custom_call_target="tpu_custom_call" | custom-call | tf_op jit(solution)/shard_map/middle/pallas_call | solution.py:22
  32.1 1.0 %collective-permute-start.8 = (f32[144,128]{1,0:T(8,128)S(1)}, f32[144,128]{1,0:T(8,128)S(1)}, u32[]{:S(2)}, u32[]{:S(2)}) collective-permute-start(f32[144,128]{1,0:T(8,128)S(1)} %get-tuple-element.42), channel_id=1, source_target_pairs={{0,1},{1,0},{2,3},{3,2},{4,5},{5,4},{6,7},{7,6},{8,9},{9,8},{10,11... | collective-permute-start | bytes 221192 | tf_op jit(solution)/shard_map/ppermute | solution.py:553
  33.1 0.9 %collective-permute-done.8.middle = f32[144,128]{1,0:T(8,128)S(1)} collective-permute-done((f32[144,128]{1,0:T(8,128)S(1)}, f32[144,128]{1,0:T(8,128)S(1)}, u32[]{:S(2)}, u32[]{:S(2)}) %collective-permute-start.8) | collective-permute-done | bytes 73760 | tf_op jit(solution)/shard_map/ppermute | solution.py:553
  34.0 0.1 faces.3
  34.1 0.3 collective-permute-start.9
  34.4 1.2 %collective-permute-start.10 = (f32[216,128]{1,0:T(8,128)S(1)}, f32[216,128]{1,0:T(8,128)S(1)}, u32[]{:S(2)}, u32[]{:S(2)}) collective-permute-start(f32[216,128]{1,0:T(8,128)S(1)} %get-tuple-element.44), channel_id=1, source_target_pairs={{0,1},{1,0},{2,3},{3,2},{4,8},{5,9},{6,10},{7,11},{8,4},{9,5},{10,... | collective-permute-start | bytes 331784 | tf_op jit(solution)/shard_map/ppermute | solution.py:553
  35.6 3.9 %inside.1.main = f32[8,128,128]{2,1,0:T(8,128)S(1)} custom-call(f32[10,144,128]{2,1,0:T(8,128)S(1)} %get-tuple-element.41.x, f32[144,128]{1,0:T(8,128)S(1)} %collective-permute-done.8.middle, bf16[9,128,384]{2,1,0:T(8,128)(2,1)S(1)} %get-tuple-element.31.ready.refs_0_.refs_2_.single, bf16[9,128,768]{2,1,0:T(8,128)(2,1)S(1)} %get-tuple-element.36.refs_1_.refs_3_.double), custom_call_target="tpu_custom_call" | custom-call | tf_op jit(solution)/shard_map/inside/pallas_call | solution.py:22
  39.5 0.0 copy-start
  39.5 0.0 copy-start.2
  39.5 0.0 collective-permute-done.9.got_a
  39.5 0.0 collective-permute-done.10.got_b
  39.5 1.0 %last.1 = (f32[256,128]{1,0:T(8,128)S(1)}, f32[256,128]{1,0:T(8,128)S(1)}, f32[256,128]{1,0:T(8,128)S(1)}, f32[256,128]{1,0:T(8,128)S(1)}) custom-call(f32[8,128,128]{2,1,0:T(8,128)S(1)} %inside.1.main, f32[216,128]{1,0:T(8,128)S(1)} %collective-permute-done.9.got_a, f32[216,128]{1,0:T(8,128)S(1)} %collective-permute-done.10.got_b, ...), custom_call_target="tpu_custom_call" | custom-call | tf_op jit(solution)/shard_map/last/pallas_call | solution.py:22
  40.6 1.5 %collective-permute-start.13 = (f32[256,128]{1,0:T(8,128)S(1)}, f32[256,128]{1,0:T(8,128)S(1)}, u32[]{:S(2)}, u32[]{:S(2)}) collective-permute-start(f32[256,128]{1,0:T(8,128)S(1)} %get-tuple-element.48), channel_id=1, source_target_pairs={{0,13},{1,12},{2,15},{3,14},{4,9},{5,8},{6,11},{7,10},{8,5},{9,4},... | collective-permute-start | bytes 393224 | tf_op jit(solution)/shard_map/ppermute | solution.py:553
  42.1 1.1 %collective-permute-start.11 = (f32[256,128]{1,0:T(8,128)S(1)}, f32[256,128]{1,0:T(8,128)S(1)}, u32[]{:S(2)}, u32[]{:S(2)}) collective-permute-start(f32[256,128]{1,0:T(8,128)S(1)} %get-tuple-element.45), channel_id=1, source_target_pairs={{0,2},{1,3},{2,0},{3,1},{4,6},{5,7},{6,4},{7,5},{8,10},{9,11},{10,... | collective-permute-start | bytes 393224 | tf_op jit(solution)/shard_map/ppermute | solution.py:553
  43.2 0.6 %collective-permute-start.12 = (f32[256,128]{1,0:T(8,128)S(1)}, f32[256,128]{1,0:T(8,128)S(1)}, u32[]{:S(2)}, u32[]{:S(2)}) collective-permute-start(f32[256,128]{1,0:T(8,128)S(1)} %get-tuple-element.46), channel_id=1, source_target_pairs={{0,15},{1,14},{2,13},{3,12},{4,11},{5,10},{6,9},{7,8},{8,7},{9,6},... | collective-permute-start | bytes 393224 | tf_op jit(solution)/shard_map/ppermute | solution.py:553
  43.9 8.5 %collective-permute-done.13.mirrored = f32[256,128]{1,0:T(8,128)S(1)} collective-permute-done((f32[256,128]{1,0:T(8,128)S(1)}, f32[256,128]{1,0:T(8,128)S(1)}, u32[]{:S(2)}, u32[]{:S(2)}) %collective-permute-start.13) | collective-permute-done | bytes 131104 | tf_op jit(solution)/shard_map/ppermute | solution.py:553
  52.3 0.0 copy-done
  52.3 0.0 copy-done.2
  52.3 1.3 %unpack.2.refs_0_ = f32[32,16,8,32]{3,2,1,0:T(8,128)} custom-call(f32[32,16,8,32]{3,2,1,0:T(8,128)S(1)} %bitcast.5, s32[16,8,32]{2,1,0:T(8,128)S(1)} %copy-done.2, f32[256,128]{1,0:T(8,128)S(1)} %get-tuple-element.47.own, f32[256,128]{1,0:T(8,128)S(1)} %collective-permute-done.13.mirrored), custom_call_target="tpu_custom_call" | custom-call | tf_op jit(solution)/shard_map/unpack/pallas_call | solution.py:22
  53.6 0.0 collective-permute-done.11.own
  53.6 2.4 %collective-permute-done.12.mirrored = f32[256,128]{1,0:T(8,128)S(1)} collective-permute-done((f32[256,128]{1,0:T(8,128)S(1)}, f32[256,128]{1,0:T(8,128)S(1)}, u32[]{:S(2)}, u32[]{:S(2)}) %collective-permute-start.12) | collective-permute-done | bytes 131104 | tf_op jit(solution)/shard_map/ppermute | solution.py:553
  56.0 1.3 %unpack.3 = f32[32,16,8,32]{3,2,1,0:T(8,128)} custom-call(f32[32,16,8,32]{3,2,1,0:T(8,128)S(1)} %bitcast.6, s32[16,8,32]{2,1,0:T(8,128)S(1)} %copy-done.2, f32[256,128]{1,0:T(8,128)S(1)} %collective-permute-done.11.own, f32[256,128]{1,0:T(8,128)S(1)} %collective-permute-done.12.mirrored, f32[32,16,8,32]{3,2,1,0:T(8,128)} %unpack.2.refs_0_), custom_call_target="tpu_custom_call", output_to_operand_aliasing={{}: (4, {})} | custom-call | tf_op jit(solution)/shard_map/unpack/pallas_call | solution.py:22
Async XLA Ops:
  0.0 2.9 %copy-start.1 = (f32[27,2,16,64]{3,2,1,0:T(8,128)S(1)}, f32[27,2,16,64]{3,2,1,0:T(8,128)}, u32[]{:S(2)}) copy-start(f32[27,2,16,64]{3,2,1,0:T(8,128)} %param.5) | copy-start | bytes 663556
  3.0 7.5 %collective-permute-start = (f32[27,8,128]{2,1,0:T(8,128)S(1)}, f32[27,8,128]{2,1,0:T(8,128)S(1)}, u32[]{:S(2)}, u32[]{:S(2)}) collective-permute-start(f32[27,8,128]{2,1,0:T(8,128)S(1)} %fold.1), channel_id=1, source_target_pairs={{0,2},{1,3},{2,0},{3,1},{4,6},{5,7},{6,4},{7,5},{8,10},{9,11},{10,... | collective-permute-start | bytes 331784 | tf_op jit(solution)/shard_map/ppermute | solution.py:553
  4.3 16.6 %collective-permute-start.4 = (f32[384,128]{1,0:T(8,128)}, f32[384,128]{1,0:T(8,128)S(1)}, u32[]{:S(2)}, u32[]{:S(2)}) collective-permute-start(f32[384,128]{1,0:T(8,128)} %get-tuple-element.35), channel_id=1, source_target_pairs={{0,15},{1,14},{2,13},{3,12},{4,11},{5,10},{6,9},{7,8},{8,7},{9,6},... | collective-permute-start | bytes 589832 | tf_op jit(solution)/shard_map/ppermute | solution.py:553
  6.4 9.2 %collective-permute-start.2 = (f32[368,128]{1,0:T(8,128)}, f32[368,128]{1,0:T(8,128)S(1)}, u32[]{:S(2)}, u32[]{:S(2)}) collective-permute-start(f32[368,128]{1,0:T(8,128)} %get-tuple-element.33), channel_id=1, source_target_pairs={{0,2},{1,3},{2,0},{3,1},{4,6},{5,7},{6,4},{7,5},{8,10},{9,11},{10,... | collective-permute-start | bytes 565256 | tf_op jit(solution)/shard_map/ppermute | solution.py:553
  10.4 14.0 %collective-permute-start.3 = (f32[368,128]{1,0:T(8,128)}, f32[368,128]{1,0:T(8,128)S(1)}, u32[]{:S(2)}, u32[]{:S(2)}) collective-permute-start(f32[368,128]{1,0:T(8,128)} %get-tuple-element.34), channel_id=1, source_target_pairs={{0,13},{1,12},{2,15},{3,14},{4,9},{5,8},{6,11},{7,10},{8,5},{9,4},... | collective-permute-start | bytes 565256 | tf_op jit(solution)/shard_map/ppermute | solution.py:553
  10.5 1.5 %collective-permute-start.1 = (f32[27,8,128]{2,1,0:T(8,128)S(1)}, f32[27,8,128]{2,1,0:T(8,128)S(1)}, u32[]{:S(2)}, u32[]{:S(2)}) collective-permute-start(f32[27,8,128]{2,1,0:T(8,128)S(1)} %collective-permute-done.refs_0_), channel_id=1, source_target_pairs={{0,1},{1,0},{2,3},{3,2},{4,5},{5,4},{6,7},{7,6},{8,9},{9,8},{10,11... | collective-permute-start | bytes 331784 | tf_op jit(solution)/shard_map/ppermute | solution.py:553
  15.6 0.9 %copy-start.3 = (f32[384,128]{1,0:T(8,128)S(1)}, f32[384,128]{1,0:T(8,128)}, u32[]{:S(2)}) copy-start(f32[384,128]{1,0:T(8,128)} %get-tuple-element.32.refs_0_.own) | copy-start | bytes 589828
  24.9 1.4 %collective-permute-start.5 = (f32[144,128]{1,0:T(8,128)S(1)}, f32[144,128]{1,0:T(8,128)S(1)}, u32[]{:S(2)}, u32[]{:S(2)}) collective-permute-start(f32[144,128]{1,0:T(8,128)S(1)} %get-tuple-element.38), channel_id=1, source_target_pairs={{0,1},{1,0},{2,3},{3,2},{4,5},{5,4},{6,7},{7,6},{8,9},{9,8},{10,11... | collective-permute-start | bytes 221192 | tf_op jit(solution)/shard_map/ppermute | solution.py:553
  26.4 4.7 %collective-permute-start.6 = (f32[216,128]{1,0:T(8,128)S(1)}, f32[216,128]{1,0:T(8,128)S(1)}, u32[]{:S(2)}, u32[]{:S(2)}) collective-permute-start(f32[216,128]{1,0:T(8,128)S(1)} %get-tuple-element.39), channel_id=1, source_target_pairs={{0,4},{1,5},{2,6},{3,7},{4,0},{5,1},{6,2},{7,3},{8,12},{9,13},{10,... | collective-permute-start | bytes 331784 | tf_op jit(solution)/shard_map/ppermute | solution.py:553
  26.4 4.6 %collective-permute-start.7 = (f32[216,128]{1,0:T(8,128)S(1)}, f32[216,128]{1,0:T(8,128)S(1)}, u32[]{:S(2)}, u32[]{:S(2)}) collective-permute-start(f32[216,128]{1,0:T(8,128)S(1)} %get-tuple-element.40), channel_id=1, source_target_pairs={{0,1},{1,0},{2,3},{3,2},{4,8},{5,9},{6,10},{7,11},{8,4},{9,5},{10,... | collective-permute-start | bytes 331784 | tf_op jit(solution)/shard_map/ppermute | solution.py:553
  32.1 1.9 %collective-permute-start.8 = (f32[144,128]{1,0:T(8,128)S(1)}, f32[144,128]{1,0:T(8,128)S(1)}, u32[]{:S(2)}, u32[]{:S(2)}) collective-permute-start(f32[144,128]{1,0:T(8,128)S(1)} %get-tuple-element.42), channel_id=1, source_target_pairs={{0,1},{1,0},{2,3},{3,2},{4,5},{5,4},{6,7},{7,6},{8,9},{9,8},{10,11... | collective-permute-start | bytes 221192 | tf_op jit(solution)/shard_map/ppermute | solution.py:553
  34.1 5.4 %collective-permute-start.9 = (f32[216,128]{1,0:T(8,128)S(1)}, f32[216,128]{1,0:T(8,128)S(1)}, u32[]{:S(2)}, u32[]{:S(2)}) collective-permute-start(f32[216,128]{1,0:T(8,128)S(1)} %get-tuple-element.43), channel_id=1, source_target_pairs={{0,4},{1,5},{2,6},{3,7},{4,0},{5,1},{6,2},{7,3},{8,12},{9,13},{10,... | collective-permute-start | bytes 331784 | tf_op jit(solution)/shard_map/ppermute | solution.py:553
  34.4 5.1 %collective-permute-start.10 = (f32[216,128]{1,0:T(8,128)S(1)}, f32[216,128]{1,0:T(8,128)S(1)}, u32[]{:S(2)}, u32[]{:S(2)}) collective-permute-start(f32[216,128]{1,0:T(8,128)S(1)} %get-tuple-element.44), channel_id=1, source_target_pairs={{0,1},{1,0},{2,3},{3,2},{4,8},{5,9},{6,10},{7,11},{8,4},{9,5},{10,... | collective-permute-start | bytes 331784 | tf_op jit(solution)/shard_map/ppermute | solution.py:553
  39.5 12.8 %copy-start = (f32[2,16,16,8,32]{4,3,2,1,0:T(8,128)S(1)}, f32[2,16,16,8,32]{4,3,2,1,0:T(8,128)}, u32[]{:S(2)}) copy-start(f32[2,16,16,8,32]{4,3,2,1,0:T(8,128)} %param.3) | copy-start | bytes 1572868
  39.5 12.8 %copy-start.2 = (s32[16,8,32]{2,1,0:T(8,128)S(1)}, s32[16,8,32]{2,1,0:T(8,128)}, u32[]{:S(2)}) copy-start(s32[16,8,32]{2,1,0:T(8,128)} %mask.4) | copy-start | bytes 49156
  40.6 11.7 %collective-permute-start.13 = (f32[256,128]{1,0:T(8,128)S(1)}, f32[256,128]{1,0:T(8,128)S(1)}, u32[]{:S(2)}, u32[]{:S(2)}) collective-permute-start(f32[256,128]{1,0:T(8,128)S(1)} %get-tuple-element.48), channel_id=1, source_target_pairs={{0,13},{1,12},{2,15},{3,14},{4,9},{5,8},{6,11},{7,10},{8,5},{9,4},... | collective-permute-start | bytes 393224 | tf_op jit(solution)/shard_map/ppermute | solution.py:553
  42.1 11.5 %collective-permute-start.11 = (f32[256,128]{1,0:T(8,128)S(1)}, f32[256,128]{1,0:T(8,128)S(1)}, u32[]{:S(2)}, u32[]{:S(2)}) collective-permute-start(f32[256,128]{1,0:T(8,128)S(1)} %get-tuple-element.45), channel_id=1, source_target_pairs={{0,2},{1,3},{2,0},{3,1},{4,6},{5,7},{6,4},{7,5},{8,10},{9,11},{10,... | collective-permute-start | bytes 393224 | tf_op jit(solution)/shard_map/ppermute | solution.py:553
  43.2 12.8 %collective-permute-start.12 = (f32[256,128]{1,0:T(8,128)S(1)}, f32[256,128]{1,0:T(8,128)S(1)}, u32[]{:S(2)}, u32[]{:S(2)}) collective-permute-start(f32[256,128]{1,0:T(8,128)S(1)} %get-tuple-element.46), channel_id=1, source_target_pairs={{0,15},{1,14},{2,13},{3,12},{4,11},{5,10},{6,9},{7,8},{8,7},{9,6},... | collective-permute-start | bytes 393224 | tf_op jit(solution)/shard_map/ppermute | solution.py:553

commit v6 on v5

--- a/solution.py
+++ b/solution.py
@@ -7,7 +7,6 @@
 from jax.experimental.pallas import tpu as pltpu
 from jax.sharding import PartitionSpec as P
 
-ITERS = 2
 PACK = 56 << 20
 LITTLE = pl.CostEstimate(flops=1000, bytes_accessed=1000, transcendentals=0)
 AXES = ("kz", "coil", "kx")
@@ -18,7 +17,7 @@
 VMEM = pl.BlockSpec(memory_space=pltpu.VMEM)
 
 
-def call(body, name, args, shapes, scratch=(), far=(), space=ANY, out=VMEM, limit=48 << 20, cost=None, **options):
+def call(body, name, args, shapes, scratch=(), far=(), space=ANY, out=VMEM, limit=32 << 20, cost=None, **options):
     return pl.pallas_call(
         body,
         out_shape=shapes,
@@ -64,7 +63,6 @@
         self.group = self.ch * D // 16
         self.folds = -(-16 * self.used // 128)
         self.length = 2 * self.part + self.folds * self.group
-        self.slots = self.S + 2
         self.pitch = -(-(self.V + 1) // 8) * 8
 
     def piece(self, d=0):
@@ -74,12 +72,8 @@
     def start(self, d=0):
         return jnp.clip(self.G * self.piece(d) - 2, 0, self.rows - self.S)
 
-    def range_of(self, last):
-        own = self.G * self.piece() - self.start()
-        if last:
-            return own, self.G
-        count = min(self.S, self.G + (1 if self.C == 2 else 2))
-        return jnp.clip(own - 1, 0, self.S - count), count
+    def own(self):
+        return self.G * self.piece() - self.start()
 
 
 def place():
@@ -209,19 +203,18 @@
     return call(functools.partial(weights_kernel, cut), "weights", (kernel, *folded), shapes, scratch, cost=LITTLE)
 
 
-def middle_row(cut, x):
-    return jnp.where(lax.axis_index("kx") == 0, x[cut.S - 1], x[0])
-
-
 def spread(cut, target, k, first, rest):
     D, H, S = cut.D, cut.H, cut.S
+    if k == 0:
+        for r in (0, 1, S + 2, S + 3):
+            target[r] = jnp.zeros(target.shape[1:], F32)
     for r in range(cut.base):
-        target[r, pl.ds(k, H, stride=D)] = first[r * H : (r + 1) * H]
+        target[r + 2, pl.ds(k, H, stride=D)] = first[r * H : (r + 1) * H]
     for r in range(cut.base, S):
-        target[r, pl.ds(k, H, stride=D)] = rest[(r - cut.base) * H : (r - cut.base + 1) * H]
+        target[r + 2, pl.ds(k, H, stride=D)] = rest[(r - cut.base) * H : (r - cut.base + 1) * H]
     for r in range(S):
         place = cut.spare + 2 * r
-        target[r, pl.ds(H * D + k, 2, stride=D)] = rest[place : place + 2]
+        target[r + 2, pl.ds(H * D + k, 2, stride=D)] = rest[place : place + 2]
 
 
 def assemble(cut, side, msgs, x, main, spare):
@@ -248,11 +241,14 @@
     assemble(cut, 0, msgs, x, main, spare)
 
 
-def mirrored_kernel(cut, physical, *refs):
-    msgs, (x, middle, main, spare) = refs[: cut.C], refs[-4:]
+def mirrored_kernel(cut, physical, marks, *refs):
+    msgs, (x, rows, main, spare) = refs[: cut.C], refs[-4:]
     assemble(cut, 1, msgs, x, main, spare)
     x[...] = x[...] + physical[...]
-    middle[...] = middle_row(cut, x)
+    lower, S = lax.axis_index("kx") == 0, cut.S
+    rows[0] = jnp.where(lower, x[S + 1], x[2])
+    rows[1] = jnp.where(lower, x[S], x[3])
+    rows[2] = jnp.where(lower, marks[S + 1], marks[2])
 
 
 def marks_kernel(cut, ready, own, other, marks):
@@ -269,54 +265,57 @@
 
 def points(cut, weights, msgs):
     row = (cut.V * cut.D, cut.channels)
-    window = jax.ShapeDtypeStruct((cut.S, *row), F32)
+    window = jax.ShapeDtypeStruct((cut.S + 4, *row), F32)
     stages = [pltpu.VMEM((cut.half * cut.D, 128), F32)] * 2
     args = (weights[0], *msgs[0::2])
     (x,) = call(functools.partial(physical_kernel, cut), "physical", args, [window], stages, far=(0,), cost=LITTLE)
     added = inside_half(0, x, weights, cut)
     flags = (added, msgs[0], msgs[3])
     (marks,) = call(functools.partial(marks_kernel, cut), "marks", flags, [window], far=(0,), cost=LITTLE)
-    args = (x, *msgs[1::2], added, marks)
-    x, middle = call(
+    args = (x, marks, *msgs[1::2])
+    x, rows = call(
         functools.partial(mirrored_kernel, cut),
         "mirrored",
         args,
-        [window, jax.ShapeDtypeStruct(row, F32)],
+        [window, jax.ShapeDtypeStruct((3, *row), F32)],
         stages,
-        far=(len(args) - 2, len(args) - 1),
     )
-    return x, marks, middle, added
-
-
-def beside(cut, middle):
+    return x, marks, rows, added
+
+
+def edges(cut):
     _, c, x = place()
     inner = c == cut.C - 1
-    middle = middle[...]
-    before = jnp.where(jnp.logical_and(inner, x == 1), middle, 0.0)
-    after = jnp.where(jnp.logical_and(inner, x == 0), middle, 0.0)
-    return before, after
-
-
-def faces_kernel(cut, x, middle, face_a, face_b, edges):
-    D, S, V = cut.D, cut.S, cut.V
-    edges[0], edges[1] = beside(cut, middle)
+    return jnp.logical_and(inner, x == 1), jnp.logical_and(inner, x == 0)
+
+
+def put_faces(cut, slot, row, face_a, face_b):
+    D, V = cut.D, cut.V
     odd = lax.rem(lax.axis_index("kz"), 2) == 1
-    for slot in range(cut.slots):
-        if slot == 0:
-            row = edges.at[0]
-        elif slot == S + 1:
-            row = edges.at[1]
-        else:
-            row = x.at[slot - 1]
-        first, final = row[pl.ds(0, V, stride=D)], row[pl.ds(D - 1, V, stride=D)]
-        face_a[slot * V : (slot + 1) * V] = jnp.where(odd, first, final)
-        face_b[slot * V : (slot + 1) * V] = jnp.where(odd, final, first)
-
-
-def faces(x, middle, cut):
-    face = jax.ShapeDtypeStruct((cut.slots * cut.V, cut.channels), F32)
-    scratch = [pltpu.VMEM((2, cut.V * cut.D, cut.channels), F32)]
-    return call(functools.partial(faces_kernel, cut), "faces", (x, middle), [face, face], scratch)
+    first, final = row(pl.ds(0, V, stride=D)), row(pl.ds(D - 1, V, stride=D))
+    face_a[slot * V : (slot + 1) * V] = jnp.where(odd, first, final)
+    face_b[slot * V : (slot + 1) * V] = jnp.where(odd, final, first)
+
+
+def faces_kernel(cut, x, rows, face_a, face_b):
+    own, G = cut.own(), cut.G
+    before, after = edges(cut)
+    other = {0: (before, 1), 1: (before, 0), G + 2: (after, 0), G + 3: (after, 1)}
+    for slot in range(G + 4):
+
+        def row(some):
+            value = x[own + slot, some]
+            if slot in other:
+                there, which = other[slot]
+                value = jnp.where(there, rows[which, some], value)
+            return value
+
+        put_faces(cut, slot, row, face_a, face_b)
+
+
+def faces(x, rows, cut):
+    face = jax.ShapeDtypeStruct(((cut.G + 4) * cut.V, cut.channels), F32)
+    return call(functools.partial(faces_kernel, cut), "faces", (x, rows), [face, face])
 
 
 def multiply(hi, lo, single, double):
@@ -338,28 +337,21 @@
     return y[1] + later + sooner
 
 
-def inside_kernel(cut, last, x, middle, single, double, out, hi, lo):
-    D, S = cut.D, cut.S
+def inside_kernel(cut, x, single, double, out, hi, lo):
+    D = cut.D
     count, L, channels = out.shape
     gap = jnp.zeros((D, channels), F32)
-    before, after = beside(cut, middle)
-    for slot in range(cut.slots):
-        row = before if slot == 0 else after if slot == S + 1 else x[slot - 1]
+    for slot in range(count + 2):
+        row = x[slot]
         high = row.astype(BF16).astype(F32)
         for ref, value in ((hi, high), (lo, row - high)):
             ref[0, slot] = jnp.concatenate([gap, value[:-D]], 0).astype(BF16)
             ref[1, slot] = value.astype(BF16)
             ref[2, slot] = jnp.concatenate([value[D:], gap], 0).astype(BF16)
-    first, _ = cut.range_of(last)
 
     def window(ref):
         return jnp.concatenate(
-            [
-                jnp.concatenate([ref[b, first + i + a, :L] for i in range(count)], 0)
-                for a in range(3)
-                for b in range(3)
-            ],
-            1,
+            [jnp.concatenate([ref[b, i + a, :L] for i in range(count)], 0) for a in range(3) for b in range(3)], 1
         )
 
     K = 9 * channels
@@ -367,12 +359,10 @@
     out[...] = shifted(y, D).reshape(count, L, channels)
 
 
-def inside(x, middle, weights, cut, last):
-    count = cut.range_of(last)[1]
-    L = (cut.H if last else cut.V) * cut.D
-    out = jax.ShapeDtypeStruct((count, L, cut.channels), F32)
-    scratch = [pltpu.VMEM((3, cut.slots, cut.V * cut.D, cut.channels), BF16)] * 2
-    return call(functools.partial(inside_kernel, cut, last), "inside", (x, middle, *weights), [out], scratch)[0]
+def inside(x, weights, cut):
+    out = jax.ShapeDtypeStruct((cut.G, cut.H * cut.D, cut.channels), F32)
+    scratch = [pltpu.VMEM((3, cut.G + 2, cut.V * cut.D, cut.channels), BF16)] * 2
+    return call(functools.partial(inside_kernel, cut), "inside", (x, *weights), [out], scratch)[0]
 
 
 def half_weights(weights, side, half):
@@ -384,10 +374,10 @@
 
 def inside_half_kernel(cut, side, x, *refs):
     if side:
-        middle, added, single, double, out, hi, lo = refs
+        rows, added, single, double, out, hi, lo = refs
     else:
         single, double, out, hi, lo = refs
-    D, S, half = cut.D, cut.S, cut.half
+    D, half, own = cut.D, cut.half, cut.own()
     count, L, channels = out.shape
     gap = jnp.zeros((D, channels), F32)
     left = lax.broadcasted_iota(jnp.int32, (L, channels), 1) < half
@@ -398,25 +388,24 @@
     none = (jnp.zeros((L, channels), F32),) * 2
 
     def versions(slot):
-        if not 1 <= slot <= S:
+        if slot == count + 2:
             return none, none, none
-        row = x[slot - 1]
+        row = x[own + slot]
         both = (row, pltpu.roll(row, half, 1))
         sooner = tuple(jnp.concatenate([gap, v[:-D]], 0) for v in both)
         later = tuple(jnp.concatenate([v[D:], gap], 0) for v in both)
         return sooner, both, later
 
     following = versions(0)
-    for slot in range(cut.slots):
+    for slot in range(count + 2):
         now, following = following, versions(slot + 1)
         for i, value in enumerate((pair(now[0], now[1]), pair(now[2], following[2]))):
             hi[i, slot], lo[i, slot] = split(value)
-    first, _ = cut.range_of(False)
 
     def window(ref):
         columns = [(0, 0), (0, 1), (0, 2), (1, 0), (1, 2)]
         return jnp.concatenate(
-            [jnp.concatenate([ref[i, first + j + a] for j in range(count)], 0) for i, a in columns], 1
+            [jnp.concatenate([ref[i, j + a] for j in range(count)], 0) for i, a in columns], 1
         )
 
     y = multiply(window(hi), window(lo), *(half_weights(w, side, half) for w in (single, double)))
@@ -425,45 +414,53 @@
         out[...] = y
         return
     out[...] = y + added[...]
-    _, c, core = place()
-    row = middle[...]
-    parts = [split(v) for v in (jnp.concatenate([gap, row[:-D]], 0), row, jnp.concatenate([row[D:], gap], 0))]
-    taps = pl.ds(jnp.where(core == 0, 6, 0), 3)
-    one, two = (w[taps].reshape(3 * channels, -1) for w in (single, double))
-    y = shifted(multiply(*(jnp.concatenate([p[i] for p in parts], 1) for i in range(2)), one, two), D)
-    target = jnp.where(core == 0, count - 1, 0)
-    out[target] += jnp.where(c == cut.C - 1, y, 0.0)
+    before, after = edges(cut)
+    lower = lax.axis_index("kx") == 0
+    pieces = []
+    for row in (rows[0], rows[1]):
+        parts = [split(v) for v in (jnp.concatenate([gap, row[:-D]], 0), row, jnp.concatenate([row[D:], gap], 0))]
+        pieces.append([jnp.concatenate([p[i] for p in parts], 1) for i in range(2)])
+    near, second = pieces
+    wide = [
+        jnp.concatenate([jnp.concatenate([n, f], 1), jnp.concatenate([jnp.zeros_like(n), n], 1)], 0)
+        for n, f in zip(near, second)
+    ]
+    outer = pl.ds(jnp.where(lower, 6, 0), 3)
+    taps = [jnp.concatenate([w[3:6], w[outer]], 0).reshape(6 * channels, -1) for w in (single, double)]
+    y = shifted(multiply(*wide, *taps), D)
+    there = jnp.logical_or(before, after)
+    for i in range(2):
+        target = jnp.where(lower, count - 1 - i, i)
+        out[target] += jnp.where(there, y[i * L : (i + 1) * L], 0.0)
 
 
 def inside_half(side, x, weights, cut, *more):
-    count = cut.range_of(False)[1]
-    L = cut.V * cut.D
+    count, L = cut.G + 2, cut.V * cut.D
     out = jax.ShapeDtypeStruct((count, L, cut.channels), F32)
-    scratch = [pltpu.VMEM((2, cut.slots, L, cut.channels), BF16)] * 2
+    scratch = [pltpu.VMEM((2, count + 2, L, cut.channels), BF16)] * 2
     body = functools.partial(inside_half_kernel, cut, side)
     cost = None if side else LITTLE
     return call(body, "inside_mirrored" if side else "inside_physical", (x, *more, *weights), [out], scratch, cost=cost)[0]
 
 
-def add_planes(cut, last, target, offset, count, got_a, got_b, single, double, planes):
+def add_planes(cut, width, target, got_a, got_b, single, double, planes):
     D, V, pitch = cut.D, cut.V, cut.pitch
     z, Z = lax.axis_index("kz"), lax.axis_size("kz")
     odd = lax.rem(z, 2) == 1
     ends = jnp.logical_or(z == 0, z == Z - 1)
-    first, _ = cut.range_of(last)
+    count = target.shape[0]
     height = -(-count * pitch // 16) * 16
-    width = cut.H if last else V
     N, K = cut.channels, 9 * cut.channels
     got_a, got_b = got_a[...], jnp.where(ends, 0.0, got_b[...])
     for e, k, plane in ((0, 0, jnp.where(odd, got_a, got_b)), (2, D - 1, jnp.where(odd, got_b, got_a))):
         planes[...] = jnp.zeros_like(planes)
-        for slot in range(cut.slots):
+        for slot in range(count + 2):
             column = plane[slot * V : (slot + 1) * V]
             for b in range(3):
                 place = 8 + slot * pitch + 1 - b
                 planes[b, place : place + V] = column
         parts = [
-            split(planes[b, pl.ds(pl.multiple_of(8 + (first + a) * pitch, 8), height)])
+            split(planes[b, 8 + a * pitch : 8 + a * pitch + height])
             for a in range(3)
             for b in range(3)
         ]
@@ -472,28 +469,38 @@
         two = double[:, :, 2 * e * N : (2 * e + 2) * N].reshape(K, 2 * N)
         (y,) = multiply(hi, lo, one, two)
         for i in range(count):
-            target[offset + i, pl.ds(k, width, stride=D)] += y[i * pitch : i * pitch + width]
-
-
-def planes_scratch(cut):
-    return pltpu.VMEM((3, 8 + cut.slots * cut.pitch + 16, cut.channels), F32)
-
-
-def middle_kernel(cut, x, marks, main, got_a, got_b, single, double, out, middle, planes):
-    first, count = cut.range_of(False)
-    out[...] = jnp.zeros_like(out)
-    for i in range(count):
-        out[first + i] = main[i]
-    add_planes(cut, False, out, first, count, got_a, got_b, single, double, planes)
-    out[...] = jnp.where(marks[...] > 0.5, x[...], out[...])
-    middle[...] = middle_row(cut, out)
+            target[i, pl.ds(k, width, stride=D)] += y[i * pitch : i * pitch + width]
+
+
+def planes_scratch(cut, count):
+    return pltpu.VMEM((3, 8 + (count + 2) * cut.pitch + 16, cut.channels), F32)
+
+
+def middle_kernel(cut, x, marks, rows, main, got_a, got_b, single, double, out, face_a, face_b, planes):
+    G, own = cut.G, cut.own()
+    before, after = edges(cut)
+    core, piece = lax.axis_index("kx"), cut.piece()
+    out[...] = main[...]
+    add_planes(cut, cut.V, out, got_a, got_b, single, double, planes)
+    first = jnp.logical_and(core == 0, piece == 0)
+    final = jnp.logical_and(core == 1, piece == cut.C - 1)
+    for i in range(G + 2):
+        kept, mark = x[own + 1 + i], marks[own + 1 + i]
+        if i in (0, G + 1):
+            there, outside = (before, first) if i == 0 else (after, final)
+            kept, mark = jnp.where(there, rows[0], kept), jnp.where(there, rows[2], mark)
+            value = jnp.where(outside, 0.0, jnp.where(mark > 0.5, kept, out[i]))
+        else:
+            value = jnp.where(mark > 0.5, kept, out[i])
+        out[i] = value
+        put_faces(cut, i, lambda some: out[i, some], face_a, face_b)
 
 
 def last_kernel(cut, main, got_a, got_b, single, double, *rest):
     C, D, H, G, half = cut.C, cut.D, cut.H, cut.G, cut.half
     outs, (y, stage, planes) = rest[: 2 * C], rest[2 * C :]
     y[...] = main[...]
-    add_planes(cut, True, y, 0, G, got_a, got_b, single, double, planes)
+    add_planes(cut, H, y, got_a, got_b, single, double, planes)
     flip = reversal(G * H)
     for k in range(D):
         rows = y[:, pl.ds(k, H, stride=D)].reshape(G * H, 2 * half).T
@@ -584,28 +591,27 @@
         half = send(fold(kernel), lambda z, c, x: (z, c ^ d, x))
         folded += [half, send(half, core)]
     weights = build_weights(kernel, folded, cut)
-    state, marks, row, added = points(cut, weights, msgs)
-    for step in range(ITERS):
-        last = step == ITERS - 1
-        row = send(row, core)
-        face_a, face_b = faces(state, row, cut)
-        got_a, got_b = send(face_a, plane_a), send(face_b, plane_b)
-        main = inside(state, row, weights, cut, last) if step else inside_half(1, state, weights, cut, row, added)
-        if not last:
-            state, row = call(
-                functools.partial(middle_kernel, cut),
-                "middle",
-                (state, marks, main, got_a, got_b, *weights),
-                [jax.ShapeDtypeStruct(state.shape, F32), jax.ShapeDtypeStruct(row.shape, F32)],
-                [planes_scratch(cut)],
-            )
+    state, marks, near, added = points(cut, weights, msgs)
+    near = send(near, core)
+    got = [send(face, to) for face, to in zip(faces(state, near, cut), (plane_a, plane_b))]
+    main = inside_half(1, state, weights, cut, near, added)
+    face = jax.ShapeDtypeStruct(((cut.G + 2) * cut.V, cut.channels), F32)
+    state, *sides = call(
+        functools.partial(middle_kernel, cut),
+        "middle",
+        (state, marks, near, main, *got, *weights),
+        [jax.ShapeDtypeStruct(main.shape, F32), face, face],
+        [planes_scratch(cut, cut.G + 2)],
+    )
+    got = [send(face, to) for face, to in zip(sides, (plane_a, plane_b))]
+    main = inside(state, weights, cut)
     message = jax.ShapeDtypeStruct((cut.ch * D, cut.G * cut.H), F32)
     msgs = call(
         functools.partial(last_kernel, cut),
         "last",
-        (main, got_a, got_b, *weights),
+        (main, *got, *weights),
         [message] * (2 * C),
-        [pltpu.VMEM(main.shape, F32), pltpu.VMEM((cut.channels * D, cut.G * cut.H), F32), planes_scratch(cut)],
+        [pltpu.VMEM(main.shape, F32), pltpu.VMEM((cut.channels * D, cut.G * cut.H), F32), planes_scratch(cut, cut.G)],
     )
     msgs = exchange(msgs)
     out = None

time: 57.6 us -> 56.5 us (0.981)
  waiting for transfers between devices: 19.1 us -> 18.2 us
    ppermute x14 -> x13, waiting for transfers between devices: 19.1 us -> 18.2 us  [send(): lax.ppermute(array, AXES, [(index(*p), index(*target(*p))) for p in every])]
    ppermute x14 -> x13, starting transfers between devices: 12.8 us -> 12.4 us  [send(): lax.ppermute(array, AXES, [(index(*p), index(*target(*p))) for p in every])]
    pallas_call x16 -> x15, Pallas kernels: 24.3 us -> 24.5 us  [call(): pl.pallas_call(body, out_shape=shapes, in_specs=[space if i in far else V...]
  transfers between devices with their start and end apart: 14 -> 13, of which waited for: 8 -> 7; matrix products, arithmetic and copies ran while one was open for 0% -> 0% of each run, Pallas kernels for 30% -> 31%
where the time goes in v6:
time: 56.5 us; the launch traced here: 56.3 us
  Pallas kernels  24.5 us (43%)
  waiting for transfers between devices  18.2 us (32%)
  starting transfers between devices  12.4 us (22%)
  local copies, waits for them, and re-layouts  0.94 us (2%)
    pallas_call x15, Pallas kernels, call(): pl.pallas_call(body, out_shape=shapes, in_specs=[space if i in far else V...  24.5 us
    ppermute x13, waiting for transfers between devices, send(): lax.ppermute(array, AXES, [(index(*p), index(*target(*p))) for p in every])  18.2 us
    ppermute x13, starting transfers between devices, send(): lax.ppermute(array, AXES, [(index(*p), index(*target(*p))) for p in every])  12.4 us
  transfers between devices with their start and end apart: 13, of which 7 were waited for; matrix products, arithmetic and copies ran while one was open for 0% of the time, Pallas kernels for 31%

profile of v6, /device:TPU:9, one launch (start us, length us, event | category | flops | bytes accessed | tf_op | source)
XLA Modules:
  0.0 56.3 jit_solution(12677846078581586455)
XLA Ops:
  0.0 0.0 copy-start.1
  0.0 2.9 %pack.2 = (f32[368,128]{1,0:T(8,128)}, f32[384,128]{1,0:T(8,128)}) custom-call(f32[32,16,8,32]{3,2,1,0:T(8,128)} %bitcast.3, s32[16,8,32]{2,1,0:T(8,128)} %mask.4), custom_call_target="tpu_custom_call" | custom-call | tf_op jit(solution)/shard_map/pack/pallas_call | solution.py:21
  2.9 0.0 copy-done.1
  2.9 0.1 fold.1
  3.0 1.3 %collective-permute-start = (f32[27,8,128]{2,1,0:T(8,128)S(1)}, f32[27,8,128]{2,1,0:T(8,128)S(1)}, u32[]{:S(2)}, u32[]{:S(2)}) collective-permute-start(f32[27,8,128]{2,1,0:T(8,128)S(1)} %fold.1), channel_id=1, source_target_pairs={{0,2},{1,3},{2,0},{3,1},{4,6},{5,7},{6,4},{7,5},{8,10},{9,11},{10,... | collective-permute-start | bytes 331784 | tf_op jit(solution)/shard_map/ppermute | solution.py:560
  4.3 2.1 %collective-permute-start.3 = (f32[384,128]{1,0:T(8,128)}, f32[384,128]{1,0:T(8,128)S(1)}, u32[]{:S(2)}, u32[]{:S(2)}) collective-permute-start(f32[384,128]{1,0:T(8,128)} %get-tuple-element.34), channel_id=1, source_target_pairs={{0,15},{1,14},{2,13},{3,12},{4,11},{5,10},{6,9},{7,8},{8,7},{9,6},... | collective-permute-start | bytes 589832 | tf_op jit(solution)/shard_map/ppermute | solution.py:560
  6.4 1.2 %collective-permute-start.2 = (f32[368,128]{1,0:T(8,128)}, f32[368,128]{1,0:T(8,128)S(1)}, u32[]{:S(2)}, u32[]{:S(2)}) collective-permute-start(f32[368,128]{1,0:T(8,128)} %get-tuple-element.32), channel_id=1, source_target_pairs={{0,2},{1,3},{2,0},{3,1},{4,6},{5,7},{6,4},{7,5},{8,10},{9,11},{10,... | collective-permute-start | bytes 565256 | tf_op jit(solution)/shard_map/ppermute | solution.py:560
  7.6 2.8 %pack.3 = (f32[384,128]{1,0:T(8,128)}, f32[368,128]{1,0:T(8,128)}) custom-call(f32[32,16,8,32]{3,2,1,0:T(8,128)} %bitcast.4, s32[16,8,32]{2,1,0:T(8,128)} %mask.4), custom_call_target="tpu_custom_call" | custom-call | tf_op jit(solution)/shard_map/pack/pallas_call | solution.py:21
  10.4 0.1 collective-permute-start.4
  10.5 0.0 collective-permute-done.refs_0_
  10.5 0.5 collective-permute-start.1
  11.1 1.0 %collective-permute-done.1.refs_1_ = f32[27,8,128]{2,1,0:T(8,128)S(1)} collective-permute-done((f32[27,8,128]{2,1,0:T(8,128)S(1)}, f32[27,8,128]{2,1,0:T(8,128)S(1)}, u32[]{:S(2)}, u32[]{:S(2)}) %collective-permute-start.1) | collective-permute-done | bytes 110624 | tf_op jit(solution)/shard_map/ppermute | solution.py:560
  12.0 1.9 %weights.1 = (bf16[9,128,384]{2,1,0:T(8,128)(2,1)S(1)}, bf16[9,128,768]{2,1,0:T(8,128)(2,1)S(1)}) custom-call(f32[54,16,64]{2,1,0:T(8,128)S(1)} %bitcast.8, f32[27,8,128]{2,1,0:T(8,128)S(1)} %collective-permute-done.refs_0_, f32[27,8,128]{2,1,0:T(8,128)S(1)} %collective-permute-done.1.refs_1_), custom_call_target="tpu_custom_call" | custom-call | flops 1000 | bytes 1000 | tf_op jit(solution)/shard_map/weights/pallas_call | solution.py:21
  13.9 1.7 %collective-permute-done.2.refs_1_ = f32[368,128]{1,0:T(8,128)S(1)} collective-permute-done((f32[368,128]{1,0:T(8,128)}, f32[368,128]{1,0:T(8,128)S(1)}, u32[]{:S(2)}, u32[]{:S(2)}) %collective-permute-start.2) | collective-permute-done | bytes 188448 | tf_op jit(solution)/shard_map/ppermute | solution.py:560
  15.7 0.0 copy-start.3
  15.7 0.9 %copy-done.3 = f32[384,128]{1,0:T(8,128)S(1)} copy-done((f32[384,128]{1,0:T(8,128)S(1)}, f32[384,128]{1,0:T(8,128)}, u32[]{:S(2)}) %copy-start.3) | copy-done | bytes 196632
  16.6 0.4 physical.1.x
  17.0 3.1 %inside_physical.1.ready.refs_1_ = f32[10,144,128]{2,1,0:T(8,128)S(1)} custom-call(f32[14,144,128]{2,1,0:T(8,128)S(1)} %physical.1.x, bf16[9,128,384]{2,1,0:T(8,128)(2,1)S(1)} %get-tuple-element.30.ready.refs_0_.refs_2_.single, bf16[9,128,768]{2,1,0:T(8,128)(2,1)S(1)} %get-tuple-element.33.refs_1_.refs_3_.double), custom_call_target="tpu_custom_call" | custom-call | flops 1000 | bytes 1000 | tf_op jit(solution)/shard_map/inside_physical/pallas_call | solution.py:21
  20.1 0.8 %collective-permute-done.3.other.refs_1_ = f32[384,128]{1,0:T(8,128)S(1)} collective-permute-done((f32[384,128]{1,0:T(8,128)}, f32[384,128]{1,0:T(8,128)S(1)}, u32[]{:S(2)}, u32[]{:S(2)}) %collective-permute-start.3) | collective-permute-done | bytes 196640 | tf_op jit(solution)/shard_map/ppermute | solution.py:560
  20.9 0.6 %marks.1 = f32[14,144,128]{2,1,0:T(8,128)S(1)} custom-call(f32[10,144,128]{2,1,0:T(8,128)S(1)} %inside_physical.1.ready.refs_1_, f32[384,128]{1,0:T(8,128)S(1)} %copy-done.3, f32[384,128]{1,0:T(8,128)S(1)} %collective-permute-done.3.other.refs_1_), custom_call_target="tpu_custom_call" | custom-call | flops 1000 | bytes 1000 | tf_op jit(solution)/shard_map/marks/pallas_call | solution.py:21
  21.5 2.9 %collective-permute-done.4.refs_0_ = f32[368,128]{1,0:T(8,128)S(1)} collective-permute-done((f32[368,128]{1,0:T(8,128)}, f32[368,128]{1,0:T(8,128)S(1)}, u32[]{:S(2)}, u32[]{:S(2)}) %collective-permute-start.4) | collective-permute-done | bytes 188448 | tf_op jit(solution)/shard_map/ppermute | solution.py:560
  24.4 0.5 mirrored.1
  24.9 0.5 collective-permute-start.5
  25.4 1.1 %collective-permute-done.5.refs_0_.rows = f32[3,144,128]{2,1,0:T(8,128)S(1)} collective-permute-done((f32[3,144,128]{2,1,0:T(8,128)S(1)}, f32[3,144,128]{2,1,0:T(8,128)S(1)}, u32[]{:S(2)}, u32[]{:S(2)}) %collective-permute-start.5) | collective-permute-done | bytes 221216 | tf_op jit(solution)/shard_map/ppermute | solution.py:560
  26.5 0.1 faces.1
  26.6 0.1 collective-permute-start.6
  26.6 1.3 %collective-permute-start.7 = (f32[216,128]{1,0:T(8,128)S(1)}, f32[216,128]{1,0:T(8,128)S(1)}, u32[]{:S(2)}, u32[]{:S(2)}) collective-permute-start(f32[216,128]{1,0:T(8,128)S(1)} %get-tuple-element.39), channel_id=1, source_target_pairs={{0,1},{1,0},{2,3},{3,2},{4,8},{5,9},{6,10},{7,11},{8,4},{9,5},{10,... | collective-permute-start | bytes 331784 | tf_op jit(solution)/shard_map/ppermute | solution.py:560
  27.9 3.7 %inside_mirrored.1.main = f32[10,144,128]{2,1,0:T(8,128)S(1)} custom-call(f32[14,144,128]{2,1,0:T(8,128)S(1)} %get-tuple-element.36.x, f32[3,144,128]{2,1,0:T(8,128)S(1)} %collective-permute-done.5.refs_0_.rows, f32[10,144,128]{2,1,0:T(8,128)S(1)} %inside_physical.1.ready.refs_1_, bf16[9,128,384]{2,1,0:T(8,128)(2,1)S(1)} %get-tuple-element.30.ready.refs_0_.refs_2_.single, ...), custom_call_target="tpu_custom_call" | custom-call | tf_op jit(solution)/shard_map/inside_mirrored/pallas_call | solution.py:21
  31.6 0.0 collective-permute-done.6.got_a
  31.6 0.0 collective-permute-done.7.got_b
  31.6 1.1 %middle.1 = (f32[10,144,128]{2,1,0:T(8,128)S(1)}, f32[180,128]{1,0:T(8,128)S(1)}, f32[180,128]{1,0:T(8,128)S(1)}) custom-call(f32[14,144,128]{2,1,0:T(8,128)S(1)} %get-tuple-element.36.x, f32[14,144,128]{2,1,0:T(8,128)S(1)} %marks.1, f32[3,144,128]{2,1,0:T(8,128)S(1)} %collective-permute-done.5.refs_0_.rows, f32[10,144,128]{2,1,0:T(8,128)S(1)} %inside_mirrored.1.main, ...), custom_call_target="tpu_custom_call" | custom-call | tf_op jit(solution)/shard_map/middle/pallas_call | solution.py:21
  32.7 0.9 %collective-permute-start.8 = (f32[180,128]{1,0:T(8,128)S(1)}, f32[180,128]{1,0:T(8,128)S(1)}, u32[]{:S(2)}, u32[]{:S(2)}) collective-permute-start(f32[180,128]{1,0:T(8,128)S(1)} %get-tuple-element.41), channel_id=1, source_target_pairs={{0,4},{1,5},{2,6},{3,7},{4,0},{5,1},{6,2},{7,3},{8,12},{9,13},{10,... | collective-permute-start | bytes 276488 | tf_op jit(solution)/shard_map/ppermute | solution.py:560
  33.6 1.2 %collective-permute-start.9 = (f32[180,128]{1,0:T(8,128)S(1)}, f32[180,128]{1,0:T(8,128)S(1)}, u32[]{:S(2)}, u32[]{:S(2)}) collective-permute-start(f32[180,128]{1,0:T(8,128)S(1)} %get-tuple-element.42), channel_id=1, source_target_pairs={{0,1},{1,0},{2,3},{3,2},{4,8},{5,9},{6,10},{7,11},{8,4},{9,5},{10,... | collective-permute-start | bytes 276488 | tf_op jit(solution)/shard_map/ppermute | solution.py:560
  34.8 3.8 %inside.1.main = f32[8,128,128]{2,1,0:T(8,128)S(1)} custom-call(f32[10,144,128]{2,1,0:T(8,128)S(1)} %get-tuple-element.40.x, bf16[9,128,384]{2,1,0:T(8,128)(2,1)S(1)} %get-tuple-element.30.ready.refs_0_.refs_2_.single, bf16[9,128,768]{2,1,0:T(8,128)(2,1)S(1)} %get-tuple-element.33.refs_1_.refs_3_.double), custom_call_target="tpu_custom_call" | custom-call | tf_op jit(solution)/shard_map/inside/pallas_call | solution.py:21
  38.5 0.0 copy-start
  38.5 0.0 copy-start.2
  38.6 0.0 collective-permute-done.8.got_a
  38.6 0.0 collective-permute-done.9.got_b
  38.6 1.0 %last.1 = (f32[256,128]{1,0:T(8,128)S(1)}, f32[256,128]{1,0:T(8,128)S(1)}, f32[256,128]{1,0:T(8,128)S(1)}, f32[256,128]{1,0:T(8,128)S(1)}) custom-call(f32[8,128,128]{2,1,0:T(8,128)S(1)} %inside.1.main, f32[180,128]{1,0:T(8,128)S(1)} %collective-permute-done.8.got_a, f32[180,128]{1,0:T(8,128)S(1)} %collective-permute-done.9.got_b, ...), custom_call_target="tpu_custom_call" | custom-call | tf_op jit(solution)/shard_map/last/pallas_call | solution.py:21
  39.6 1.3 %collective-permute-start.12 = (f32[256,128]{1,0:T(8,128)S(1)}, f32[256,128]{1,0:T(8,128)S(1)}, u32[]{:S(2)}, u32[]{:S(2)}) collective-permute-start(f32[256,128]{1,0:T(8,128)S(1)} %get-tuple-element.46), channel_id=1, source_target_pairs={{0,13},{1,12},{2,15},{3,14},{4,9},{5,8},{6,11},{7,10},{8,5},{9,4},... | collective-permute-start | bytes 393224 | tf_op jit(solution)/shard_map/ppermute | solution.py:560
  40.9 1.2 %collective-permute-start.10 = (f32[256,128]{1,0:T(8,128)S(1)}, f32[256,128]{1,0:T(8,128)S(1)}, u32[]{:S(2)}, u32[]{:S(2)}) collective-permute-start(f32[256,128]{1,0:T(8,128)S(1)} %get-tuple-element.43), channel_id=1, source_target_pairs={{0,2},{1,3},{2,0},{3,1},{4,6},{5,7},{6,4},{7,5},{8,10},{9,11},{10,... | collective-permute-start | bytes 393224 | tf_op jit(solution)/shard_map/ppermute | solution.py:560
  42.1 0.8 %collective-permute-start.11 = (f32[256,128]{1,0:T(8,128)S(1)}, f32[256,128]{1,0:T(8,128)S(1)}, u32[]{:S(2)}, u32[]{:S(2)}) collective-permute-start(f32[256,128]{1,0:T(8,128)S(1)} %get-tuple-element.44), channel_id=1, source_target_pairs={{0,15},{1,14},{2,13},{3,12},{4,11},{5,10},{6,9},{7,8},{8,7},{9,6},... | collective-permute-start | bytes 393224 | tf_op jit(solution)/shard_map/ppermute | solution.py:560
  42.9 8.2 %collective-permute-done.12.mirrored = f32[256,128]{1,0:T(8,128)S(1)} collective-permute-done((f32[256,128]{1,0:T(8,128)S(1)}, f32[256,128]{1,0:T(8,128)S(1)}, u32[]{:S(2)}, u32[]{:S(2)}) %collective-permute-start.12) | collective-permute-done | bytes 131104 | tf_op jit(solution)/shard_map/ppermute | solution.py:560
  51.1 0.0 copy-done
  51.1 0.0 copy-done.2
  51.1 1.3 %unpack.2.refs_0_ = f32[32,16,8,32]{3,2,1,0:T(8,128)} custom-call(f32[32,16,8,32]{3,2,1,0:T(8,128)S(1)} %bitcast.5, s32[16,8,32]{2,1,0:T(8,128)S(1)} %copy-done.2, f32[256,128]{1,0:T(8,128)S(1)} %get-tuple-element.45.own, f32[256,128]{1,0:T(8,128)S(1)} %collective-permute-done.12.mirrored), custom_call_target="tpu_custom_call" | custom-call | tf_op jit(solution)/shard_map/unpack/pallas_call | solution.py:21
  52.4 0.0 collective-permute-done.10.own
  52.4 2.4 %collective-permute-done.11.mirrored = f32[256,128]{1,0:T(8,128)S(1)} collective-permute-done((f32[256,128]{1,0:T(8,128)S(1)}, f32[256,128]{1,0:T(8,128)S(1)}, u32[]{:S(2)}, u32[]{:S(2)}) %collective-permute-start.11) | collective-permute-done | bytes 131104 | tf_op jit(solution)/shard_map/ppermute | solution.py:560
  54.9 1.3 %unpack.3 = f32[32,16,8,32]{3,2,1,0:T(8,128)} custom-call(f32[32,16,8,32]{3,2,1,0:T(8,128)S(1)} %bitcast.6, s32[16,8,32]{2,1,0:T(8,128)S(1)} %copy-done.2, f32[256,128]{1,0:T(8,128)S(1)} %collective-permute-done.10.own, f32[256,128]{1,0:T(8,128)S(1)} %collective-permute-done.11.mirrored, f32[32,16,8,32]{3,2,1,0:T(8,128)} %unpack.2.refs_0_), custom_call_target="tpu_custom_call", output_to_operand_aliasing={{}: (4, {})} | custom-call | tf_op jit(solution)/shard_map/unpack/pallas_call | solution.py:21
Async XLA Ops:
  0.0 2.9 %copy-start.1 = (f32[27,2,16,64]{3,2,1,0:T(8,128)S(1)}, f32[27,2,16,64]{3,2,1,0:T(8,128)}, u32[]{:S(2)}) copy-start(f32[27,2,16,64]{3,2,1,0:T(8,128)} %param.5) | copy-start | bytes 663556
  3.0 7.5 %collective-permute-start = (f32[27,8,128]{2,1,0:T(8,128)S(1)}, f32[27,8,128]{2,1,0:T(8,128)S(1)}, u32[]{:S(2)}, u32[]{:S(2)}) collective-permute-start(f32[27,8,128]{2,1,0:T(8,128)S(1)} %fold.1), channel_id=1, source_target_pairs={{0,2},{1,3},{2,0},{3,1},{4,6},{5,7},{6,4},{7,5},{8,10},{9,11},{10,... | collective-permute-start | bytes 331784 | tf_op jit(solution)/shard_map/ppermute | solution.py:560
  4.3 16.6 %collective-permute-start.3 = (f32[384,128]{1,0:T(8,128)}, f32[384,128]{1,0:T(8,128)S(1)}, u32[]{:S(2)}, u32[]{:S(2)}) collective-permute-start(f32[384,128]{1,0:T(8,128)} %get-tuple-element.34), channel_id=1, source_target_pairs={{0,15},{1,14},{2,13},{3,12},{4,11},{5,10},{6,9},{7,8},{8,7},{9,6},... | collective-permute-start | bytes 589832 | tf_op jit(solution)/shard_map/ppermute | solution.py:560
  6.4 9.2 %collective-permute-start.2 = (f32[368,128]{1,0:T(8,128)}, f32[368,128]{1,0:T(8,128)S(1)}, u32[]{:S(2)}, u32[]{:S(2)}) collective-permute-start(f32[368,128]{1,0:T(8,128)} %get-tuple-element.32), channel_id=1, source_target_pairs={{0,2},{1,3},{2,0},{3,1},{4,6},{5,7},{6,4},{7,5},{8,10},{9,11},{10,... | collective-permute-start | bytes 565256 | tf_op jit(solution)/shard_map/ppermute | solution.py:560
  10.4 14.0 %collective-permute-start.4 = (f32[368,128]{1,0:T(8,128)}, f32[368,128]{1,0:T(8,128)S(1)}, u32[]{:S(2)}, u32[]{:S(2)}) collective-permute-start(f32[368,128]{1,0:T(8,128)} %get-tuple-element.35), channel_id=1, source_target_pairs={{0,13},{1,12},{2,15},{3,14},{4,9},{5,8},{6,11},{7,10},{8,5},{9,4},... | collective-permute-start | bytes 565256 | tf_op jit(solution)/shard_map/ppermute | solution.py:560
  10.5 1.5 %collective-permute-start.1 = (f32[27,8,128]{2,1,0:T(8,128)S(1)}, f32[27,8,128]{2,1,0:T(8,128)S(1)}, u32[]{:S(2)}, u32[]{:S(2)}) collective-permute-start(f32[27,8,128]{2,1,0:T(8,128)S(1)} %collective-permute-done.refs_0_), channel_id=1, source_target_pairs={{0,1},{1,0},{2,3},{3,2},{4,5},{5,4},{6,7},{7,6},{8,9},{9,8},{10,11... | collective-permute-start | bytes 331784 | tf_op jit(solution)/shard_map/ppermute | solution.py:560
  15.7 0.9 %copy-start.3 = (f32[384,128]{1,0:T(8,128)S(1)}, f32[384,128]{1,0:T(8,128)}, u32[]{:S(2)}) copy-start(f32[384,128]{1,0:T(8,128)} %get-tuple-element.31.refs_0_.own) | copy-start | bytes 589828
  24.9 1.6 %collective-permute-start.5 = (f32[3,144,128]{2,1,0:T(8,128)S(1)}, f32[3,144,128]{2,1,0:T(8,128)S(1)}, u32[]{:S(2)}, u32[]{:S(2)}) collective-permute-start(f32[3,144,128]{2,1,0:T(8,128)S(1)} %get-tuple-element.37), channel_id=1, source_target_pairs={{0,1},{1,0},{2,3},{3,2},{4,5},{5,4},{6,7},{7,6},{8,9},{9,8},{10,11... | collective-permute-start | bytes 663560 | tf_op jit(solution)/shard_map/ppermute | solution.py:560
  26.6 5.0 %collective-permute-start.6 = (f32[216,128]{1,0:T(8,128)S(1)}, f32[216,128]{1,0:T(8,128)S(1)}, u32[]{:S(2)}, u32[]{:S(2)}) collective-permute-start(f32[216,128]{1,0:T(8,128)S(1)} %get-tuple-element.38), channel_id=1, source_target_pairs={{0,4},{1,5},{2,6},{3,7},{4,0},{5,1},{6,2},{7,3},{8,12},{9,13},{10,... | collective-permute-start | bytes 331784 | tf_op jit(solution)/shard_map/ppermute | solution.py:560
  26.6 4.9 %collective-permute-start.7 = (f32[216,128]{1,0:T(8,128)S(1)}, f32[216,128]{1,0:T(8,128)S(1)}, u32[]{:S(2)}, u32[]{:S(2)}) collective-permute-start(f32[216,128]{1,0:T(8,128)S(1)} %get-tuple-element.39), channel_id=1, source_target_pairs={{0,1},{1,0},{2,3},{3,2},{4,8},{5,9},{6,10},{7,11},{8,4},{9,5},{10,... | collective-permute-start | bytes 331784 | tf_op jit(solution)/shard_map/ppermute | solution.py:560
  32.7 5.9 %collective-permute-start.8 = (f32[180,128]{1,0:T(8,128)S(1)}, f32[180,128]{1,0:T(8,128)S(1)}, u32[]{:S(2)}, u32[]{:S(2)}) collective-permute-start(f32[180,128]{1,0:T(8,128)S(1)} %get-tuple-element.41), channel_id=1, source_target_pairs={{0,4},{1,5},{2,6},{3,7},{4,0},{5,1},{6,2},{7,3},{8,12},{9,13},{10,... | collective-permute-start | bytes 276488 | tf_op jit(solution)/shard_map/ppermute | solution.py:560
  33.6 5.0 %collective-permute-start.9 = (f32[180,128]{1,0:T(8,128)S(1)}, f32[180,128]{1,0:T(8,128)S(1)}, u32[]{:S(2)}, u32[]{:S(2)}) collective-permute-start(f32[180,128]{1,0:T(8,128)S(1)} %get-tuple-element.42), channel_id=1, source_target_pairs={{0,1},{1,0},{2,3},{3,2},{4,8},{5,9},{6,10},{7,11},{8,4},{9,5},{10,... | collective-permute-start | bytes 276488 | tf_op jit(solution)/shard_map/ppermute | solution.py:560
  38.5 12.6 %copy-start = (f32[2,16,16,8,32]{4,3,2,1,0:T(8,128)S(1)}, f32[2,16,16,8,32]{4,3,2,1,0:T(8,128)}, u32[]{:S(2)}) copy-start(f32[2,16,16,8,32]{4,3,2,1,0:T(8,128)} %param.3) | copy-start | bytes 1572868
  38.5 12.6 %copy-start.2 = (s32[16,8,32]{2,1,0:T(8,128)S(1)}, s32[16,8,32]{2,1,0:T(8,128)}, u32[]{:S(2)}) copy-start(s32[16,8,32]{2,1,0:T(8,128)} %mask.4) | copy-start | bytes 49156
  39.6 11.5 %collective-permute-start.12 = (f32[256,128]{1,0:T(8,128)S(1)}, f32[256,128]{1,0:T(8,128)S(1)}, u32[]{:S(2)}, u32[]{:S(2)}) collective-permute-start(f32[256,128]{1,0:T(8,128)S(1)} %get-tuple-element.46), channel_id=1, source_target_pairs={{0,13},{1,12},{2,15},{3,14},{4,9},{5,8},{6,11},{7,10},{8,5},{9,4},... | collective-permute-start | bytes 393224 | tf_op jit(solution)/shard_map/ppermute | solution.py:560
  40.9 11.6 %collective-permute-start.10 = (f32[256,128]{1,0:T(8,128)S(1)}, f32[256,128]{1,0:T(8,128)S(1)}, u32[]{:S(2)}, u32[]{:S(2)}) collective-permute-start(f32[256,128]{1,0:T(8,128)S(1)} %get-tuple-element.43), channel_id=1, source_target_pairs={{0,2},{1,3},{2,0},{3,1},{4,6},{5,7},{6,4},{7,5},{8,10},{9,11},{10,... | collective-permute-start | bytes 393224 | tf_op jit(solution)/shard_map/ppermute | solution.py:560
  42.1 12.8 %collective-permute-start.11 = (f32[256,128]{1,0:T(8,128)S(1)}, f32[256,128]{1,0:T(8,128)S(1)}, u32[]{:S(2)}, u32[]{:S(2)}) collective-permute-start(f32[256,128]{1,0:T(8,128)S(1)} %get-tuple-element.44), channel_id=1, source_target_pairs={{0,15},{1,14},{2,13},{3,12},{4,11},{5,10},{6,9},{7,8},{8,7},{9,6},... | collective-permute-start | bytes 393224 | tf_op jit(solution)/shard_map/ppermute | solution.py:560

commit v7 on v6

--- a/solution.py
+++ b/solution.py
@@ -496,7 +496,7 @@
         put_faces(cut, i, lambda some: out[i, some], face_a, face_b)
 
 
-def last_kernel(cut, main, got_a, got_b, single, double, *rest):
+def last_kernel(cut, main, got_b, got_a, single, double, *rest):
     C, D, H, G, half = cut.C, cut.D, cut.H, cut.G, cut.half
     outs, (y, stage, planes) = rest[: 2 * C], rest[2 * C :]
     y[...] = main[...]
@@ -515,7 +515,7 @@
                 outs[2 * d + side][ri * cut.part : (ri + 1) * cut.part] = stage[pl.ds(start, cut.part)]
 
 
-def unpack_kernel(cut, d, measured, mask, own, mirrored, *refs):
+def unpack_kernel(cut, d, measured, mask, mirrored, own, *refs):
     out, rows, sems = refs[-3:]
     ch, D, G, H = cut.ch, cut.D, cut.G, cut.H
     start = cut.piece(d) * G
@@ -603,7 +603,7 @@
         [jax.ShapeDtypeStruct(main.shape, F32), face, face],
         [planes_scratch(cut, cut.G + 2)],
     )
-    got = [send(face, to) for face, to in zip(sides, (plane_a, plane_b))]
+    got = [send(face, to) for face, to in zip(sides[::-1], (plane_b, plane_a))]
     main = inside(state, weights, cut)
     message = jax.ShapeDtypeStruct((cut.ch * D, cut.G * cut.H), F32)
     msgs = call(
@@ -615,8 +615,8 @@
     )
     msgs = exchange(msgs)
     out = None
-    for d in range(C):
-        out = unpack(d, flat, mask, msgs[2 * d : 2 * d + 2], cut, out)
+    for d in reversed(range(C)):
+        out = unpack(d, flat, mask, (msgs[2 * d + 1], msgs[2 * d]), cut, out)
     return out.reshape(measured.shape)
 
 

time: 56.5 us -> 55.3 us (0.979); the launches traced: 56.3 us -> 54.5 us
  waiting for transfers between devices: 18.2 us -> 17 us
  starting transfers between devices: 12.4 us -> 11.7 us
    ppermute x13, waiting for transfers between devices: 18.2 us -> 17 us  [send(): lax.ppermute(array, AXES, [(index(*p), index(*target(*p))) for p in every])]
    ppermute x13, starting transfers between devices: 12.4 us -> 11.7 us  [send(): lax.ppermute(array, AXES, [(index(*p), index(*target(*p))) for p in every])]
  transfers between devices with their start and end apart: 13 -> 13, of which waited for: 7 -> 7; matrix products, arithmetic and copies ran while one was open for 0% -> 0% of each run, Pallas kernels for 31% -> 32%
where the time goes in v7:
time: 55.3 us; the launch traced here: 54.5 us
  Pallas kernels  24.5 us (44%)
  waiting for transfers between devices  17 us (31%)
  starting transfers between devices  11.7 us (21%)
  local copies, waits for them, and re-layouts  0.94 us (2%)
    pallas_call x15, Pallas kernels, call(): pl.pallas_call(body, out_shape=shapes, in_specs=[space if i in far else V...  24.5 us
    ppermute x13, waiting for transfers between devices, send(): lax.ppermute(array, AXES, [(index(*p), index(*target(*p))) for p in every])  17 us
    ppermute x13, starting transfers between devices, send(): lax.ppermute(array, AXES, [(index(*p), index(*target(*p))) for p in every])  11.7 us
  transfers between devices with their start and end apart: 13, of which 7 were waited for; matrix products, arithmetic and copies ran while one was open for 0% of the time, Pallas kernels for 32%

profile of v7, /device:TPU:9, one launch (start us, length us, event | category | flops | bytes accessed | tf_op | source)
XLA Modules:
  0.0 54.5 jit_solution(12605970779971058145)
XLA Ops:
  0.0 0.0 copy-start.1
  0.0 2.9 %pack.2 = (f32[368,128]{1,0:T(8,128)}, f32[384,128]{1,0:T(8,128)}) custom-call(f32[32,16,8,32]{3,2,1,0:T(8,128)} %bitcast.3, s32[16,8,32]{2,1,0:T(8,128)} %mask.4), custom_call_target="tpu_custom_call" | custom-call | tf_op jit(solution)/shard_map/pack/pallas_call | solution.py:21
  2.9 0.0 copy-done.1
  2.9 0.1 fold.1
  3.0 1.3 %collective-permute-start = (f32[27,8,128]{2,1,0:T(8,128)S(1)}, f32[27,8,128]{2,1,0:T(8,128)S(1)}, u32[]{:S(2)}, u32[]{:S(2)}) collective-permute-start(f32[27,8,128]{2,1,0:T(8,128)S(1)} %fold.1), channel_id=1, source_target_pairs={{0,2},{1,3},{2,0},{3,1},{4,6},{5,7},{6,4},{7,5},{8,10},{9,11},{10,... | collective-permute-start | bytes 331784 | tf_op jit(solution)/shard_map/ppermute | solution.py:560
  4.3 2.1 %collective-permute-start.3 = (f32[384,128]{1,0:T(8,128)}, f32[384,128]{1,0:T(8,128)S(1)}, u32[]{:S(2)}, u32[]{:S(2)}) collective-permute-start(f32[384,128]{1,0:T(8,128)} %get-tuple-element.34), channel_id=1, source_target_pairs={{0,15},{1,14},{2,13},{3,12},{4,11},{5,10},{6,9},{7,8},{8,7},{9,6},... | collective-permute-start | bytes 589832 | tf_op jit(solution)/shard_map/ppermute | solution.py:560
  6.4 1.2 %collective-permute-start.2 = (f32[368,128]{1,0:T(8,128)}, f32[368,128]{1,0:T(8,128)S(1)}, u32[]{:S(2)}, u32[]{:S(2)}) collective-permute-start(f32[368,128]{1,0:T(8,128)} %get-tuple-element.32), channel_id=1, source_target_pairs={{0,2},{1,3},{2,0},{3,1},{4,6},{5,7},{6,4},{7,5},{8,10},{9,11},{10,... | collective-permute-start | bytes 565256 | tf_op jit(solution)/shard_map/ppermute | solution.py:560
  7.6 2.8 %pack.3 = (f32[384,128]{1,0:T(8,128)}, f32[368,128]{1,0:T(8,128)}) custom-call(f32[32,16,8,32]{3,2,1,0:T(8,128)} %bitcast.4, s32[16,8,32]{2,1,0:T(8,128)} %mask.4), custom_call_target="tpu_custom_call" | custom-call | tf_op jit(solution)/shard_map/pack/pallas_call | solution.py:21
  10.4 0.1 collective-permute-start.4
  10.5 0.0 collective-permute-done.refs_0_
  10.5 0.5 %collective-permute-start.1 = (f32[27,8,128]{2,1,0:T(8,128)S(1)}, f32[27,8,128]{2,1,0:T(8,128)S(1)}, u32[]{:S(2)}, u32[]{:S(2)}) collective-permute-start(f32[27,8,128]{2,1,0:T(8,128)S(1)} %collective-permute-done.refs_0_), channel_id=1, source_target_pairs={{0,1},{1,0},{2,3},{3,2},{4,5},{5,4},{6,7},{7,6},{8,9},{9,8},{10,11... | collective-permute-start | bytes 331784 | tf_op jit(solution)/shard_map/ppermute | solution.py:560
  11.1 1.0 %collective-permute-done.1.refs_1_ = f32[27,8,128]{2,1,0:T(8,128)S(1)} collective-permute-done((f32[27,8,128]{2,1,0:T(8,128)S(1)}, f32[27,8,128]{2,1,0:T(8,128)S(1)}, u32[]{:S(2)}, u32[]{:S(2)}) %collective-permute-start.1) | collective-permute-done | bytes 110624 | tf_op jit(solution)/shard_map/ppermute | solution.py:560
  12.0 1.9 %weights.1 = (bf16[9,128,384]{2,1,0:T(8,128)(2,1)S(1)}, bf16[9,128,768]{2,1,0:T(8,128)(2,1)S(1)}) custom-call(f32[54,16,64]{2,1,0:T(8,128)S(1)} %bitcast.8, f32[27,8,128]{2,1,0:T(8,128)S(1)} %collective-permute-done.refs_0_, f32[27,8,128]{2,1,0:T(8,128)S(1)} %collective-permute-done.1.refs_1_), custom_call_target="tpu_custom_call" | custom-call | flops 1000 | bytes 1000 | tf_op jit(solution)/shard_map/weights/pallas_call | solution.py:21
  13.9 1.7 %collective-permute-done.2.refs_1_ = f32[368,128]{1,0:T(8,128)S(1)} collective-permute-done((f32[368,128]{1,0:T(8,128)}, f32[368,128]{1,0:T(8,128)S(1)}, u32[]{:S(2)}, u32[]{:S(2)}) %collective-permute-start.2) | collective-permute-done | bytes 188448 | tf_op jit(solution)/shard_map/ppermute | solution.py:560
  15.7 0.0 copy-start.3
  15.7 0.9 %copy-done.3 = f32[384,128]{1,0:T(8,128)S(1)} copy-done((f32[384,128]{1,0:T(8,128)S(1)}, f32[384,128]{1,0:T(8,128)}, u32[]{:S(2)}) %copy-start.3) | copy-done | bytes 196632
  16.6 0.4 physical.1.x
  17.0 3.1 %inside_physical.1.ready.refs_1_ = f32[10,144,128]{2,1,0:T(8,128)S(1)} custom-call(f32[14,144,128]{2,1,0:T(8,128)S(1)} %physical.1.x, bf16[9,128,384]{2,1,0:T(8,128)(2,1)S(1)} %get-tuple-element.30.ready.refs_0_.refs_2_.single, bf16[9,128,768]{2,1,0:T(8,128)(2,1)S(1)} %get-tuple-element.33.refs_1_.refs_3_.double), custom_call_target="tpu_custom_call" | custom-call | flops 1000 | bytes 1000 | tf_op jit(solution)/shard_map/inside_physical/pallas_call | solution.py:21
  20.1 0.8 %collective-permute-done.3.other.refs_1_ = f32[384,128]{1,0:T(8,128)S(1)} collective-permute-done((f32[384,128]{1,0:T(8,128)}, f32[384,128]{1,0:T(8,128)S(1)}, u32[]{:S(2)}, u32[]{:S(2)}) %collective-permute-start.3) | collective-permute-done | bytes 196640 | tf_op jit(solution)/shard_map/ppermute | solution.py:560
  20.9 0.6 %marks.1 = f32[14,144,128]{2,1,0:T(8,128)S(1)} custom-call(f32[10,144,128]{2,1,0:T(8,128)S(1)} %inside_physical.1.ready.refs_1_, f32[384,128]{1,0:T(8,128)S(1)} %copy-done.3, f32[384,128]{1,0:T(8,128)S(1)} %collective-permute-done.3.other.refs_1_), custom_call_target="tpu_custom_call" | custom-call | flops 1000 | bytes 1000 | tf_op jit(solution)/shard_map/marks/pallas_call | solution.py:21
  21.5 2.9 %collective-permute-done.4.refs_0_ = f32[368,128]{1,0:T(8,128)S(1)} collective-permute-done((f32[368,128]{1,0:T(8,128)}, f32[368,128]{1,0:T(8,128)S(1)}, u32[]{:S(2)}, u32[]{:S(2)}) %collective-permute-start.4) | collective-permute-done | bytes 188448 | tf_op jit(solution)/shard_map/ppermute | solution.py:560
  24.4 0.5 mirrored.1
  24.9 0.5 collective-permute-start.5
  25.4 1.1 %collective-permute-done.5.refs_0_.rows = f32[3,144,128]{2,1,0:T(8,128)S(1)} collective-permute-done((f32[3,144,128]{2,1,0:T(8,128)S(1)}, f32[3,144,128]{2,1,0:T(8,128)S(1)}, u32[]{:S(2)}, u32[]{:S(2)}) %collective-permute-start.5) | collective-permute-done | bytes 221216 | tf_op jit(solution)/shard_map/ppermute | solution.py:560
  26.5 0.1 faces.1
  26.6 0.1 collective-permute-start.6
  26.6 1.3 %collective-permute-start.7 = (f32[216,128]{1,0:T(8,128)S(1)}, f32[216,128]{1,0:T(8,128)S(1)}, u32[]{:S(2)}, u32[]{:S(2)}) collective-permute-start(f32[216,128]{1,0:T(8,128)S(1)} %get-tuple-element.39), channel_id=1, source_target_pairs={{0,1},{1,0},{2,3},{3,2},{4,8},{5,9},{6,10},{7,11},{8,4},{9,5},{10,... | collective-permute-start | bytes 331784 | tf_op jit(solution)/shard_map/ppermute | solution.py:560
  27.9 3.7 %inside_mirrored.1.main = f32[10,144,128]{2,1,0:T(8,128)S(1)} custom-call(f32[14,144,128]{2,1,0:T(8,128)S(1)} %get-tuple-element.36.x, f32[3,144,128]{2,1,0:T(8,128)S(1)} %collective-permute-done.5.refs_0_.rows, f32[10,144,128]{2,1,0:T(8,128)S(1)} %inside_physical.1.ready.refs_1_, bf16[9,128,384]{2,1,0:T(8,128)(2,1)S(1)} %get-tuple-element.30.ready.refs_0_.refs_2_.single, ...), custom_call_target="tpu_custom_call" | custom-call | tf_op jit(solution)/shard_map/inside_mirrored/pallas_call | solution.py:21
  31.6 0.0 collective-permute-done.6.got_a
  31.6 0.0 collective-permute-done.7.got_b
  31.6 1.1 %middle.1 = (f32[10,144,128]{2,1,0:T(8,128)S(1)}, f32[180,128]{1,0:T(8,128)S(1)}, f32[180,128]{1,0:T(8,128)S(1)}) custom-call(f32[14,144,128]{2,1,0:T(8,128)S(1)} %get-tuple-element.36.x, f32[14,144,128]{2,1,0:T(8,128)S(1)} %marks.1, f32[3,144,128]{2,1,0:T(8,128)S(1)} %collective-permute-done.5.refs_0_.rows, f32[10,144,128]{2,1,0:T(8,128)S(1)} %inside_mirrored.1.main, ...), custom_call_target="tpu_custom_call" | custom-call | tf_op jit(solution)/shard_map/middle/pallas_call | solution.py:21
  32.7 0.6 %collective-permute-start.8 = (f32[180,128]{1,0:T(8,128)S(1)}, f32[180,128]{1,0:T(8,128)S(1)}, u32[]{:S(2)}, u32[]{:S(2)}) collective-permute-start(f32[180,128]{1,0:T(8,128)S(1)} %get-tuple-element.41), channel_id=1, source_target_pairs={{0,1},{1,0},{2,3},{3,2},{4,8},{5,9},{6,10},{7,11},{8,4},{9,5},{10,... | collective-permute-start | bytes 276488 | tf_op jit(solution)/shard_map/ppermute | solution.py:560
  33.3 0.4 collective-permute-start.9
  33.7 3.8 %inside.1.main = f32[8,128,128]{2,1,0:T(8,128)S(1)} custom-call(f32[10,144,128]{2,1,0:T(8,128)S(1)} %get-tuple-element.40.x, bf16[9,128,384]{2,1,0:T(8,128)(2,1)S(1)} %get-tuple-element.30.ready.refs_0_.refs_2_.single, bf16[9,128,768]{2,1,0:T(8,128)(2,1)S(1)} %get-tuple-element.33.refs_1_.refs_3_.double), custom_call_target="tpu_custom_call" | custom-call | tf_op jit(solution)/shard_map/inside/pallas_call | solution.py:21
  37.4 0.0 copy-start
  37.4 0.0 copy-start.2
  37.4 0.0 collective-permute-done.8.got_b
  37.5 0.0 collective-permute-done.9.got_a
  37.5 1.0 %last.1 = (f32[256,128]{1,0:T(8,128)S(1)}, f32[256,128]{1,0:T(8,128)S(1)}, f32[256,128]{1,0:T(8,128)S(1)}, f32[256,128]{1,0:T(8,128)S(1)}) custom-call(f32[8,128,128]{2,1,0:T(8,128)S(1)} %inside.1.main, f32[180,128]{1,0:T(8,128)S(1)} %collective-permute-done.8.got_b, f32[180,128]{1,0:T(8,128)S(1)} %collective-permute-done.9.got_a, ...), custom_call_target="tpu_custom_call" | custom-call | tf_op jit(solution)/shard_map/last/pallas_call | solution.py:21
  38.5 3.1 %collective-permute-start.11 = (f32[256,128]{1,0:T(8,128)S(1)}, f32[256,128]{1,0:T(8,128)S(1)}, u32[]{:S(2)}, u32[]{:S(2)}) collective-permute-start(f32[256,128]{1,0:T(8,128)S(1)} %get-tuple-element.45), channel_id=1, source_target_pairs={{0,15},{1,14},{2,13},{3,12},{4,11},{5,10},{6,9},{7,8},{8,7},{9,6},... | collective-permute-start | bytes 393224 | tf_op jit(solution)/shard_map/ppermute | solution.py:560
  41.6 0.3 collective-permute-start.12
  41.9 0.4 collective-permute-start.10
  42.2 8.6 %collective-permute-done.11.mirrored = f32[256,128]{1,0:T(8,128)S(1)} collective-permute-done((f32[256,128]{1,0:T(8,128)S(1)}, f32[256,128]{1,0:T(8,128)S(1)}, u32[]{:S(2)}, u32[]{:S(2)}) %collective-permute-start.11) | collective-permute-done | bytes 131104 | tf_op jit(solution)/shard_map/ppermute | solution.py:560
  50.8 0.0 collective-permute-done.12.own
  50.8 0.0 copy-done
  50.8 0.0 copy-done.2
  50.8 1.3 %unpack.2.refs_0_ = f32[32,16,8,32]{3,2,1,0:T(8,128)} custom-call(f32[32,16,8,32]{3,2,1,0:T(8,128)S(1)} %bitcast.5, s32[16,8,32]{2,1,0:T(8,128)S(1)} %copy-done.2, f32[256,128]{1,0:T(8,128)S(1)} %collective-permute-done.11.mirrored, f32[256,128]{1,0:T(8,128)S(1)} %collective-permute-done.12.own), custom_call_target="tpu_custom_call" | custom-call | tf_op jit(solution)/shard_map/unpack/pallas_call | solution.py:21
  52.1 0.9 %collective-permute-done.10.mirrored = f32[256,128]{1,0:T(8,128)S(1)} collective-permute-done((f32[256,128]{1,0:T(8,128)S(1)}, f32[256,128]{1,0:T(8,128)S(1)}, u32[]{:S(2)}, u32[]{:S(2)}) %collective-permute-start.10) | collective-permute-done | bytes 131104 | tf_op jit(solution)/shard_map/ppermute | solution.py:560
  53.0 1.3 %unpack.3 = f32[32,16,8,32]{3,2,1,0:T(8,128)} custom-call(f32[32,16,8,32]{3,2,1,0:T(8,128)S(1)} %bitcast.6, s32[16,8,32]{2,1,0:T(8,128)S(1)} %copy-done.2, f32[256,128]{1,0:T(8,128)S(1)} %collective-permute-done.10.mirrored, f32[256,128]{1,0:T(8,128)S(1)} %get-tuple-element.44.own, f32[32,16,8,32]{3,2,1,0:T(8,128)} %unpack.2.refs_0_), custom_call_target="tpu_custom_call", output_to_operand_aliasing={{}: (4, {})} | custom-call | tf_op jit(solution)/shard_map/unpack/pallas_call | solution.py:21
Async XLA Ops:
  0.0 2.9 %copy-start.1 = (f32[27,2,16,64]{3,2,1,0:T(8,128)S(1)}, f32[27,2,16,64]{3,2,1,0:T(8,128)}, u32[]{:S(2)}) copy-start(f32[27,2,16,64]{3,2,1,0:T(8,128)} %param.5) | copy-start | bytes 663556
  3.0 7.5 %collective-permute-start = (f32[27,8,128]{2,1,0:T(8,128)S(1)}, f32[27,8,128]{2,1,0:T(8,128)S(1)}, u32[]{:S(2)}, u32[]{:S(2)}) collective-permute-start(f32[27,8,128]{2,1,0:T(8,128)S(1)} %fold.1), channel_id=1, source_target_pairs={{0,2},{1,3},{2,0},{3,1},{4,6},{5,7},{6,4},{7,5},{8,10},{9,11},{10,... | collective-permute-start | bytes 331784 | tf_op jit(solution)/shard_map/ppermute | solution.py:560
  4.3 16.6 %collective-permute-start.3 = (f32[384,128]{1,0:T(8,128)}, f32[384,128]{1,0:T(8,128)S(1)}, u32[]{:S(2)}, u32[]{:S(2)}) collective-permute-start(f32[384,128]{1,0:T(8,128)} %get-tuple-element.34), channel_id=1, source_target_pairs={{0,15},{1,14},{2,13},{3,12},{4,11},{5,10},{6,9},{7,8},{8,7},{9,6},... | collective-permute-start | bytes 589832 | tf_op jit(solution)/shard_map/ppermute | solution.py:560
  6.4 9.2 %collective-permute-start.2 = (f32[368,128]{1,0:T(8,128)}, f32[368,128]{1,0:T(8,128)S(1)}, u32[]{:S(2)}, u32[]{:S(2)}) collective-permute-start(f32[368,128]{1,0:T(8,128)} %get-tuple-element.32), channel_id=1, source_target_pairs={{0,2},{1,3},{2,0},{3,1},{4,6},{5,7},{6,4},{7,5},{8,10},{9,11},{10,... | collective-permute-start | bytes 565256 | tf_op jit(solution)/shard_map/ppermute | solution.py:560
  10.4 14.0 %collective-permute-start.4 = (f32[368,128]{1,0:T(8,128)}, f32[368,128]{1,0:T(8,128)S(1)}, u32[]{:S(2)}, u32[]{:S(2)}) collective-permute-start(f32[368,128]{1,0:T(8,128)} %get-tuple-element.35), channel_id=1, source_target_pairs={{0,13},{1,12},{2,15},{3,14},{4,9},{5,8},{6,11},{7,10},{8,5},{9,4},... | collective-permute-start | bytes 565256 | tf_op jit(solution)/shard_map/ppermute | solution.py:560
  10.5 1.5 %collective-permute-start.1 = (f32[27,8,128]{2,1,0:T(8,128)S(1)}, f32[27,8,128]{2,1,0:T(8,128)S(1)}, u32[]{:S(2)}, u32[]{:S(2)}) collective-permute-start(f32[27,8,128]{2,1,0:T(8,128)S(1)} %collective-permute-done.refs_0_), channel_id=1, source_target_pairs={{0,1},{1,0},{2,3},{3,2},{4,5},{5,4},{6,7},{7,6},{8,9},{9,8},{10,11... | collective-permute-start | bytes 331784 | tf_op jit(solution)/shard_map/ppermute | solution.py:560
  15.7 0.9 %copy-start.3 = (f32[384,128]{1,0:T(8,128)S(1)}, f32[384,128]{1,0:T(8,128)}, u32[]{:S(2)}) copy-start(f32[384,128]{1,0:T(8,128)} %get-tuple-element.31.refs_0_.own) | copy-start | bytes 589828
  24.9 1.6 %collective-permute-start.5 = (f32[3,144,128]{2,1,0:T(8,128)S(1)}, f32[3,144,128]{2,1,0:T(8,128)S(1)}, u32[]{:S(2)}, u32[]{:S(2)}) collective-permute-start(f32[3,144,128]{2,1,0:T(8,128)S(1)} %get-tuple-element.37), channel_id=1, source_target_pairs={{0,1},{1,0},{2,3},{3,2},{4,5},{5,4},{6,7},{7,6},{8,9},{9,8},{10,11... | collective-permute-start | bytes 663560 | tf_op jit(solution)/shard_map/ppermute | solution.py:560
  26.6 5.0 %collective-permute-start.6 = (f32[216,128]{1,0:T(8,128)S(1)}, f32[216,128]{1,0:T(8,128)S(1)}, u32[]{:S(2)}, u32[]{:S(2)}) collective-permute-start(f32[216,128]{1,0:T(8,128)S(1)} %get-tuple-element.38), channel_id=1, source_target_pairs={{0,4},{1,5},{2,6},{3,7},{4,0},{5,1},{6,2},{7,3},{8,12},{9,13},{10,... | collective-permute-start | bytes 331784 | tf_op jit(solution)/shard_map/ppermute | solution.py:560
  26.6 4.9 %collective-permute-start.7 = (f32[216,128]{1,0:T(8,128)S(1)}, f32[216,128]{1,0:T(8,128)S(1)}, u32[]{:S(2)}, u32[]{:S(2)}) collective-permute-start(f32[216,128]{1,0:T(8,128)S(1)} %get-tuple-element.39), channel_id=1, source_target_pairs={{0,1},{1,0},{2,3},{3,2},{4,8},{5,9},{6,10},{7,11},{8,4},{9,5},{10,... | collective-permute-start | bytes 331784 | tf_op jit(solution)/shard_map/ppermute | solution.py:560
  32.7 4.8 %collective-permute-start.8 = (f32[180,128]{1,0:T(8,128)S(1)}, f32[180,128]{1,0:T(8,128)S(1)}, u32[]{:S(2)}, u32[]{:S(2)}) collective-permute-start(f32[180,128]{1,0:T(8,128)S(1)} %get-tuple-element.41), channel_id=1, source_target_pairs={{0,1},{1,0},{2,3},{3,2},{4,8},{5,9},{6,10},{7,11},{8,4},{9,5},{10,... | collective-permute-start | bytes 276488 | tf_op jit(solution)/shard_map/ppermute | solution.py:560
  33.3 4.2 %collective-permute-start.9 = (f32[180,128]{1,0:T(8,128)S(1)}, f32[180,128]{1,0:T(8,128)S(1)}, u32[]{:S(2)}, u32[]{:S(2)}) collective-permute-start(f32[180,128]{1,0:T(8,128)S(1)} %get-tuple-element.42), channel_id=1, source_target_pairs={{0,4},{1,5},{2,6},{3,7},{4,0},{5,1},{6,2},{7,3},{8,12},{9,13},{10,... | collective-permute-start | bytes 276488 | tf_op jit(solution)/shard_map/ppermute | solution.py:560
  37.4 13.4 %copy-start = (f32[2,16,16,8,32]{4,3,2,1,0:T(8,128)S(1)}, f32[2,16,16,8,32]{4,3,2,1,0:T(8,128)}, u32[]{:S(2)}) copy-start(f32[2,16,16,8,32]{4,3,2,1,0:T(8,128)} %param.3) | copy-start | bytes 1572868
  37.4 13.4 %copy-start.2 = (s32[16,8,32]{2,1,0:T(8,128)S(1)}, s32[16,8,32]{2,1,0:T(8,128)}, u32[]{:S(2)}) copy-start(s32[16,8,32]{2,1,0:T(8,128)} %mask.4) | copy-start | bytes 49156
  38.5 12.3 %collective-permute-start.11 = (f32[256,128]{1,0:T(8,128)S(1)}, f32[256,128]{1,0:T(8,128)S(1)}, u32[]{:S(2)}, u32[]{:S(2)}) collective-permute-start(f32[256,128]{1,0:T(8,128)S(1)} %get-tuple-element.45), channel_id=1, source_target_pairs={{0,15},{1,14},{2,13},{3,12},{4,11},{5,10},{6,9},{7,8},{8,7},{9,6},... | collective-permute-start | bytes 393224 | tf_op jit(solution)/shard_map/ppermute | solution.py:560
  41.6 9.2 %collective-permute-start.12 = (f32[256,128]{1,0:T(8,128)S(1)}, f32[256,128]{1,0:T(8,128)S(1)}, u32[]{:S(2)}, u32[]{:S(2)}) collective-permute-start(f32[256,128]{1,0:T(8,128)S(1)} %get-tuple-element.46), channel_id=1, source_target_pairs={{0,2},{1,3},{2,0},{3,1},{4,6},{5,7},{6,4},{7,5},{8,10},{9,11},{10,... | collective-permute-start | bytes 393224 | tf_op jit(solution)/shard_map/ppermute | solution.py:560
  41.9 11.2 %collective-permute-start.10 = (f32[256,128]{1,0:T(8,128)S(1)}, f32[256,128]{1,0:T(8,128)S(1)}, u32[]{:S(2)}, u32[]{:S(2)}) collective-permute-start(f32[256,128]{1,0:T(8,128)S(1)} %get-tuple-element.43), channel_id=1, source_target_pairs={{0,13},{1,12},{2,15},{3,14},{4,9},{5,8},{6,11},{7,10},{8,5},{9,4},... | collective-permute-start | bytes 393224 | tf_op jit(solution)/shard_map/ppermute | solution.py:560

commit v8 on v7

--- a/solution.py
+++ b/solution.py
@@ -141,7 +141,7 @@
         pltpu.SemaphoreType.DMA((2,)),
     ]
     body = functools.partial(pack_kernel, cut, d)
-    return call(body, "pack", (measured, mask), shapes, scratch, far=(0, 1), space=HBM, limit=PACK)
+    return call(body, "pack", (measured, mask), shapes, scratch, far=(0, 1), space=HBM, limit=PACK if d else 52 << 20)
 
 
 def fold_kernel(kernel, out):
@@ -241,17 +241,16 @@
     assemble(cut, 0, msgs, x, main, spare)
 
 
-def mirrored_kernel(cut, physical, marks, *refs):
+def mirrored_kernel(cut, physical, ready, *refs):
     msgs, (x, rows, main, spare) = refs[: cut.C], refs[-4:]
     assemble(cut, 1, msgs, x, main, spare)
     x[...] = x[...] + physical[...]
     lower, S = lax.axis_index("kx") == 0, cut.S
     rows[0] = jnp.where(lower, x[S + 1], x[2])
     rows[1] = jnp.where(lower, x[S], x[3])
-    rows[2] = jnp.where(lower, marks[S + 1], marks[2])
-
-
-def marks_kernel(cut, ready, own, other, marks):
+
+
+def marks_kernel(cut, ready, own, other, marks, edge):
     D, half = cut.D, cut.half
     lane = lax.broadcasted_iota(jnp.int32, (128, cut.channels), 1)
     flags = [msg[cut.length : cut.length + 2 * D] for msg in (own, other)]
@@ -261,9 +260,10 @@
         first = jnp.where(lane < half, flags[:, k : k + 1], flags[:, 2 * D + j : 2 * D + j + 1])
         rest = jnp.where(lane < half, flags[:, D + k : D + k + 1], flags[:, 3 * D + j : 3 * D + j + 1])
         spread(cut, marks, k, first, rest)
-
-
-def points(cut, weights, msgs):
+    edge[...] = jnp.where(lax.axis_index("kx") == 0, marks[cut.S + 1], marks[2])
+
+
+def points(cut, weights, msgs, swap):
     row = (cut.V * cut.D, cut.channels)
     window = jax.ShapeDtypeStruct((cut.S + 4, *row), F32)
     stages = [pltpu.VMEM((cut.half * cut.D, 128), F32)] * 2
@@ -271,16 +271,19 @@
     (x,) = call(functools.partial(physical_kernel, cut), "physical", args, [window], stages, far=(0,), cost=LITTLE)
     added = inside_half(0, x, weights, cut)
     flags = (added, msgs[0], msgs[3])
-    (marks,) = call(functools.partial(marks_kernel, cut), "marks", flags, [window], far=(0,), cost=LITTLE)
-    args = (x, marks, *msgs[1::2])
+    edge = jax.ShapeDtypeStruct(row, F32)
+    marks, edge = call(functools.partial(marks_kernel, cut), "marks", flags, [window, edge], far=(0,), cost=LITTLE)
+    edge = swap(edge)
+    args = (x, edge, *msgs[1::2])
     x, rows = call(
         functools.partial(mirrored_kernel, cut),
         "mirrored",
         args,
-        [window, jax.ShapeDtypeStruct((3, *row), F32)],
+        [window, jax.ShapeDtypeStruct((2, *row), F32)],
         stages,
+        far=(1,),
     )
-    return x, marks, rows, added
+    return x, marks, edge, rows, added
 
 
 def edges(cut):
@@ -452,8 +455,8 @@
     height = -(-count * pitch // 16) * 16
     N, K = cut.channels, 9 * cut.channels
     got_a, got_b = got_a[...], jnp.where(ends, 0.0, got_b[...])
+    planes[...] = jnp.zeros_like(planes)
     for e, k, plane in ((0, 0, jnp.where(odd, got_a, got_b)), (2, D - 1, jnp.where(odd, got_b, got_a))):
-        planes[...] = jnp.zeros_like(planes)
         for slot in range(count + 2):
             column = plane[slot * V : (slot + 1) * V]
             for b in range(3):
@@ -476,7 +479,7 @@
     return pltpu.VMEM((3, 8 + (count + 2) * cut.pitch + 16, cut.channels), F32)
 
 
-def middle_kernel(cut, x, marks, rows, main, got_a, got_b, single, double, out, face_a, face_b, planes):
+def middle_kernel(cut, x, marks, edge, rows, main, got_a, got_b, single, double, out, face_a, face_b, planes):
     G, own = cut.G, cut.own()
     before, after = edges(cut)
     core, piece = lax.axis_index("kx"), cut.piece()
@@ -488,7 +491,7 @@
         kept, mark = x[own + 1 + i], marks[own + 1 + i]
         if i in (0, G + 1):
             there, outside = (before, first) if i == 0 else (after, final)
-            kept, mark = jnp.where(there, rows[0], kept), jnp.where(there, rows[2], mark)
+            kept, mark = jnp.where(there, rows[0], kept), jnp.where(there, edge[...], mark)
             value = jnp.where(outside, 0.0, jnp.where(mark > 0.5, kept, out[i]))
         else:
             value = jnp.where(mark > 0.5, kept, out[i])
@@ -591,7 +594,7 @@
         half = send(fold(kernel), lambda z, c, x: (z, c ^ d, x))
         folded += [half, send(half, core)]
     weights = build_weights(kernel, folded, cut)
-    state, marks, near, added = points(cut, weights, msgs)
+    state, marks, edge, near, added = points(cut, weights, msgs, lambda row: send(row, core))
     near = send(near, core)
     got = [send(face, to) for face, to in zip(faces(state, near, cut), (plane_a, plane_b))]
     main = inside_half(1, state, weights, cut, near, added)
@@ -599,7 +602,7 @@
     state, *sides = call(
         functools.partial(middle_kernel, cut),
         "middle",
-        (state, marks, near, main, *got, *weights),
+        (state, marks, edge, near, main, *got, *weights),
         [jax.ShapeDtypeStruct(main.shape, F32), face, face],
         [planes_scratch(cut, cut.G + 2)],
     )

time: 55.3 us -> 55.1 us (level)
  starting transfers between devices: 11.7 us -> 12.7 us
  local copies, waits for them, and re-layouts: 0.94 us -> 0.01 us
  Pallas kernels: 24.5 us -> 23.6 us
  waiting for transfers between devices: 17 us -> 17.6 us
    ppermute x13 -> x14, starting transfers between devices: 11.7 us -> 12.7 us  [send(): lax.ppermute(array, AXES, [(index(*p), index(*target(*p))) for p in every])]
    unnamed x8 -> x6, local copies, waits for them, and re-layouts: 0.94 us -> 0.01 us
    pallas_call x15, Pallas kernels: 24.5 us -> 23.6 us  [call(): pl.pallas_call(body, out_shape=shapes, in_specs=[space if i in far else V...]
    ppermute x13 -> x14, waiting for transfers between devices: 17 us -> 17.6 us  [send(): lax.ppermute(array, AXES, [(index(*p), index(*target(*p))) for p in every])]
  transfers between devices with their start and end apart: 13 -> 14, of which waited for: 7 -> 7; matrix products, arithmetic and copies ran while one was open for 0% -> 0% of each run, Pallas kernels for 32% -> 31%
where the time goes in v8:
time: 55.1 us; the launch traced here: 54.3 us
  Pallas kernels  23.6 us (43%)
  waiting for transfers between devices  17.6 us (32%)
  starting transfers between devices  12.7 us (23%)
    pallas_call x15, Pallas kernels, call(): pl.pallas_call(body, out_shape=shapes, in_specs=[space if i in far else V...  23.6 us
    ppermute x14, waiting for transfers between devices, send(): lax.ppermute(array, AXES, [(index(*p), index(*target(*p))) for p in every])  17.6 us
    ppermute x14, starting transfers between devices, send(): lax.ppermute(array, AXES, [(index(*p), index(*target(*p))) for p in every])  12.7 us
  transfers between devices with their start and end apart: 14, of which 7 were waited for; matrix products, arithmetic and copies ran while one was open for 0% of the time, Pallas kernels for 31%

profile of v8, /device:TPU:9, one launch (start us, length us, event | category | flops | bytes accessed | tf_op | source)
XLA Modules:
  0.0 54.3 jit_solution(16219889074944931320)
XLA Ops:
  0.0 0.0 copy-start.2
  0.0 0.0 copy-start.1
  0.0 2.9 %pack.2 = (f32[368,128]{1,0:T(8,128)}, f32[384,128]{1,0:T(8,128)}) custom-call(f32[32,16,8,32]{3,2,1,0:T(8,128)} %bitcast.3, s32[16,8,32]{2,1,0:T(8,128)} %mask.4), custom_call_target="tpu_custom_call" | custom-call | tf_op jit(solution)/shard_map/pack/pallas_call | solution.py:21
  2.9 0.0 copy-done.1
  2.9 0.1 fold.1
  3.0 1.3 %collective-permute-start = (f32[27,8,128]{2,1,0:T(8,128)S(1)}, f32[27,8,128]{2,1,0:T(8,128)S(1)}, u32[]{:S(2)}, u32[]{:S(2)}) collective-permute-start(f32[27,8,128]{2,1,0:T(8,128)S(1)} %fold.1), channel_id=1, source_target_pairs={{0,2},{1,3},{2,0},{3,1},{4,6},{5,7},{6,4},{7,5},{8,10},{9,11},{10,... | collective-permute-start | bytes 331784 | tf_op jit(solution)/shard_map/ppermute | solution.py:563
  4.3 2.1 %collective-permute-start.3 = (f32[384,128]{1,0:T(8,128)}, f32[384,128]{1,0:T(8,128)S(1)}, u32[]{:S(2)}, u32[]{:S(2)}) collective-permute-start(f32[384,128]{1,0:T(8,128)} %get-tuple-element.36), channel_id=1, source_target_pairs={{0,15},{1,14},{2,13},{3,12},{4,11},{5,10},{6,9},{7,8},{8,7},{9,6},... | collective-permute-start | bytes 589832 | tf_op jit(solution)/shard_map/ppermute | solution.py:563
  6.4 1.2 %collective-permute-start.2 = (f32[368,128]{1,0:T(8,128)}, f32[368,128]{1,0:T(8,128)S(1)}, u32[]{:S(2)}, u32[]{:S(2)}) collective-permute-start(f32[368,128]{1,0:T(8,128)} %get-tuple-element.34), channel_id=1, source_target_pairs={{0,2},{1,3},{2,0},{3,1},{4,6},{5,7},{6,4},{7,5},{8,10},{9,11},{10,... | collective-permute-start | bytes 565256 | tf_op jit(solution)/shard_map/ppermute | solution.py:563
  7.6 0.0 copy-done.2
  7.6 2.1 %pack.3 = (f32[384,128]{1,0:T(8,128)S(1)}, f32[368,128]{1,0:T(8,128)S(1)}) custom-call(f32[32,16,8,32]{3,2,1,0:T(8,128)} %bitcast.4, s32[16,8,32]{2,1,0:T(8,128)S(1)} %copy-done.2), custom_call_target="tpu_custom_call" | custom-call | tf_op jit(solution)/shard_map/pack/pallas_call | solution.py:21
  9.7 0.1 collective-permute-start.5
  9.7 0.0 collective-permute-done.refs_0_
  9.8 0.5 %collective-permute-start.1 = (f32[27,8,128]{2,1,0:T(8,128)S(1)}, f32[27,8,128]{2,1,0:T(8,128)S(1)}, u32[]{:S(2)}, u32[]{:S(2)}) collective-permute-start(f32[27,8,128]{2,1,0:T(8,128)S(1)} %collective-permute-done.refs_0_), channel_id=1, source_target_pairs={{0,1},{1,0},{2,3},{3,2},{4,5},{5,4},{6,7},{7,6},{8,9},{9,8},{10,11... | collective-permute-start | bytes 331784 | tf_op jit(solution)/shard_map/ppermute | solution.py:563
  10.3 1.0 %collective-permute-done.1.refs_1_ = f32[27,8,128]{2,1,0:T(8,128)S(1)} collective-permute-done((f32[27,8,128]{2,1,0:T(8,128)S(1)}, f32[27,8,128]{2,1,0:T(8,128)S(1)}, u32[]{:S(2)}, u32[]{:S(2)}) %collective-permute-start.1) | collective-permute-done | bytes 110624 | tf_op jit(solution)/shard_map/ppermute | solution.py:563
  11.3 1.9 %weights.1 = (bf16[9,128,384]{2,1,0:T(8,128)(2,1)S(1)}, bf16[9,128,768]{2,1,0:T(8,128)(2,1)S(1)}) custom-call(f32[54,16,64]{2,1,0:T(8,128)S(1)} %bitcast.8, f32[27,8,128]{2,1,0:T(8,128)S(1)} %collective-permute-done.refs_0_, f32[27,8,128]{2,1,0:T(8,128)S(1)} %collective-permute-done.1.refs_1_), custom_call_target="tpu_custom_call" | custom-call | flops 1000 | bytes 1000 | tf_op jit(solution)/shard_map/weights/pallas_call | solution.py:21
  13.2 1.5 %collective-permute-done.2.refs_1_ = f32[368,128]{1,0:T(8,128)S(1)} collective-permute-done((f32[368,128]{1,0:T(8,128)}, f32[368,128]{1,0:T(8,128)S(1)}, u32[]{:S(2)}, u32[]{:S(2)}) %collective-permute-start.2) | collective-permute-done | bytes 188448 | tf_op jit(solution)/shard_map/ppermute | solution.py:563
  14.7 0.4 physical.1.x
  15.1 3.1 %inside_physical.1.ready.refs_1_ = f32[10,144,128]{2,1,0:T(8,128)S(1)} custom-call(f32[14,144,128]{2,1,0:T(8,128)S(1)} %physical.1.x, bf16[9,128,384]{2,1,0:T(8,128)(2,1)S(1)} %get-tuple-element.32.ready.refs_0_.refs_2_.single, bf16[9,128,768]{2,1,0:T(8,128)(2,1)S(1)} %get-tuple-element.35.refs_1_.refs_3_.double), custom_call_target="tpu_custom_call" | custom-call | flops 1000 | bytes 1000 | tf_op jit(solution)/shard_map/inside_physical/pallas_call | solution.py:21
  18.2 2.6 %collective-permute-done.3.other.refs_1_ = f32[384,128]{1,0:T(8,128)S(1)} collective-permute-done((f32[384,128]{1,0:T(8,128)}, f32[384,128]{1,0:T(8,128)S(1)}, u32[]{:S(2)}, u32[]{:S(2)}) %collective-permute-start.3) | collective-permute-done | bytes 196640 | tf_op jit(solution)/shard_map/ppermute | solution.py:563
  20.9 0.6 %marks.1 = (f32[14,144,128]{2,1,0:T(8,128)S(1)}, f32[144,128]{1,0:T(8,128)S(1)}) custom-call(f32[10,144,128]{2,1,0:T(8,128)S(1)} %inside_physical.1.ready.refs_1_, f32[384,128]{1,0:T(8,128)S(1)} %get-tuple-element.33.refs_0_.own, f32[384,128]{1,0:T(8,128)S(1)} %collective-permute-done.3.other.refs_1_), custom_call_target="tpu_custom_call" | custom-call | flops 1000 | bytes 1000 | tf_op jit(solution)/shard_map/marks/pallas_call | solution.py:21
  21.5 1.0 %collective-permute-start.4 = (f32[144,128]{1,0:T(8,128)S(1)}, f32[144,128]{1,0:T(8,128)S(1)}, u32[]{:S(2)}, u32[]{:S(2)}) collective-permute-start(f32[144,128]{1,0:T(8,128)S(1)} %get-tuple-element.37), channel_id=1, source_target_pairs={{0,1},{1,0},{2,3},{3,2},{4,5},{5,4},{6,7},{7,6},{8,9},{9,8},{10,11... | collective-permute-start | bytes 221192 | tf_op jit(solution)/shard_map/ppermute | solution.py:563
  22.5 1.9 %collective-permute-done.5.refs_0_ = f32[368,128]{1,0:T(8,128)S(1)} collective-permute-done((f32[368,128]{1,0:T(8,128)S(1)}, f32[368,128]{1,0:T(8,128)S(1)}, u32[]{:S(2)}, u32[]{:S(2)}) %collective-permute-start.5) | collective-permute-done | bytes 188448 | tf_op jit(solution)/shard_map/ppermute | solution.py:563
  24.4 0.0 collective-permute-done.4.ready.edge
  24.4 0.5 mirrored.1
  24.9 0.5 collective-permute-start.6
  25.4 1.0 %collective-permute-done.6.refs_0_.rows = f32[2,144,128]{2,1,0:T(8,128)S(1)} collective-permute-done((f32[2,144,128]{2,1,0:T(8,128)S(1)}, f32[2,144,128]{2,1,0:T(8,128)S(1)}, u32[]{:S(2)}, u32[]{:S(2)}) %collective-permute-start.6) | collective-permute-done | bytes 147488 | tf_op jit(solution)/shard_map/ppermute | solution.py:563
  26.4 0.1 faces.1
  26.4 0.2 collective-permute-start.7
  26.6 1.2 %collective-permute-start.8 = (f32[216,128]{1,0:T(8,128)S(1)}, f32[216,128]{1,0:T(8,128)S(1)}, u32[]{:S(2)}, u32[]{:S(2)}) collective-permute-start(f32[216,128]{1,0:T(8,128)S(1)} %get-tuple-element.43), channel_id=1, source_target_pairs={{0,1},{1,0},{2,3},{3,2},{4,8},{5,9},{6,10},{7,11},{8,4},{9,5},{10,... | collective-permute-start | bytes 331784 | tf_op jit(solution)/shard_map/ppermute | solution.py:563
  27.8 3.7 %inside_mirrored.1.main = f32[10,144,128]{2,1,0:T(8,128)S(1)} custom-call(f32[14,144,128]{2,1,0:T(8,128)S(1)} %get-tuple-element.39.x, f32[2,144,128]{2,1,0:T(8,128)S(1)} %collective-permute-done.6.refs_0_.rows, f32[10,144,128]{2,1,0:T(8,128)S(1)} %inside_physical.1.ready.refs_1_, bf16[9,128,384]{2,1,0:T(8,128)(2,1)S(1)} %get-tuple-element.32.ready.refs_0_.refs_2_.single, ...), custom_call_target="tpu_custom_call" | custom-call | tf_op jit(solution)/shard_map/inside_mirrored/pallas_call | solution.py:21
  31.5 0.0 collective-permute-done.7.got_a
  31.5 0.0 collective-permute-done.8.got_b
  31.5 1.0 %middle.1 = (f32[10,144,128]{2,1,0:T(8,128)S(1)}, f32[180,128]{1,0:T(8,128)S(1)}, f32[180,128]{1,0:T(8,128)S(1)}) custom-call(f32[14,144,128]{2,1,0:T(8,128)S(1)} %get-tuple-element.39.x, f32[14,144,128]{2,1,0:T(8,128)S(1)} %get-tuple-element.40.marks, f32[144,128]{1,0:T(8,128)S(1)} %collective-permute-done.4.ready.edge, ...), custom_call_target="tpu_custom_call" | custom-call | tf_op jit(solution)/shard_map/middle/pallas_call | solution.py:21
  32.5 0.6 %collective-permute-start.9 = (f32[180,128]{1,0:T(8,128)S(1)}, f32[180,128]{1,0:T(8,128)S(1)}, u32[]{:S(2)}, u32[]{:S(2)}) collective-permute-start(f32[180,128]{1,0:T(8,128)S(1)} %get-tuple-element.45), channel_id=1, source_target_pairs={{0,1},{1,0},{2,3},{3,2},{4,8},{5,9},{6,10},{7,11},{8,4},{9,5},{10,... | collective-permute-start | bytes 276488 | tf_op jit(solution)/shard_map/ppermute | solution.py:563
  33.1 0.3 collective-permute-start.10
  33.5 3.8 %inside.1.main = f32[8,128,128]{2,1,0:T(8,128)S(1)} custom-call(f32[10,144,128]{2,1,0:T(8,128)S(1)} %get-tuple-element.44.x, bf16[9,128,384]{2,1,0:T(8,128)(2,1)S(1)} %get-tuple-element.32.ready.refs_0_.refs_2_.single, bf16[9,128,768]{2,1,0:T(8,128)(2,1)S(1)} %get-tuple-element.35.refs_1_.refs_3_.double), custom_call_target="tpu_custom_call" | custom-call | tf_op jit(solution)/shard_map/inside/pallas_call | solution.py:21
  37.3 0.0 copy-start
  37.3 0.0 collective-permute-done.9.got_b
  37.3 0.0 collective-permute-done.10.got_a
  37.3 1.0 %last.1 = (f32[256,128]{1,0:T(8,128)S(1)}, f32[256,128]{1,0:T(8,128)S(1)}, f32[256,128]{1,0:T(8,128)S(1)}, f32[256,128]{1,0:T(8,128)S(1)}) custom-call(f32[8,128,128]{2,1,0:T(8,128)S(1)} %inside.1.main, f32[180,128]{1,0:T(8,128)S(1)} %collective-permute-done.9.got_b, f32[180,128]{1,0:T(8,128)S(1)} %collective-permute-done.10.got_a, ...), custom_call_target="tpu_custom_call" | custom-call | tf_op jit(solution)/shard_map/last/pallas_call | solution.py:21
  38.3 3.1 %collective-permute-start.12 = (f32[256,128]{1,0:T(8,128)S(1)}, f32[256,128]{1,0:T(8,128)S(1)}, u32[]{:S(2)}, u32[]{:S(2)}) collective-permute-start(f32[256,128]{1,0:T(8,128)S(1)} %get-tuple-element.49), channel_id=1, source_target_pairs={{0,15},{1,14},{2,13},{3,12},{4,11},{5,10},{6,9},{7,8},{8,7},{9,6},... | collective-permute-start | bytes 393224 | tf_op jit(solution)/shard_map/ppermute | solution.py:563
  41.4 0.3 collective-permute-start.13
  41.7 0.4 collective-permute-start.11
  42.1 8.5 %collective-permute-done.12.mirrored = f32[256,128]{1,0:T(8,128)S(1)} collective-permute-done((f32[256,128]{1,0:T(8,128)S(1)}, f32[256,128]{1,0:T(8,128)S(1)}, u32[]{:S(2)}, u32[]{:S(2)}) %collective-permute-start.12) | collective-permute-done | bytes 131104 | tf_op jit(solution)/shard_map/ppermute | solution.py:563
  50.6 0.0 collective-permute-done.13.own
  50.6 0.0 copy-done
  50.6 1.3 %unpack.2.refs_0_ = f32[32,16,8,32]{3,2,1,0:T(8,128)} custom-call(f32[32,16,8,32]{3,2,1,0:T(8,128)S(1)} %bitcast.5, s32[16,8,32]{2,1,0:T(8,128)S(1)} %copy-done.2, f32[256,128]{1,0:T(8,128)S(1)} %collective-permute-done.12.mirrored, f32[256,128]{1,0:T(8,128)S(1)} %collective-permute-done.13.own), custom_call_target="tpu_custom_call" | custom-call | tf_op jit(solution)/shard_map/unpack/pallas_call | solution.py:21
  51.9 0.9 %collective-permute-done.11.mirrored = f32[256,128]{1,0:T(8,128)S(1)} collective-permute-done((f32[256,128]{1,0:T(8,128)S(1)}, f32[256,128]{1,0:T(8,128)S(1)}, u32[]{:S(2)}, u32[]{:S(2)}) %collective-permute-start.11) | collective-permute-done | bytes 131104 | tf_op jit(solution)/shard_map/ppermute | solution.py:563
  52.8 1.3 %unpack.3 = f32[32,16,8,32]{3,2,1,0:T(8,128)} custom-call(f32[32,16,8,32]{3,2,1,0:T(8,128)S(1)} %bitcast.6, s32[16,8,32]{2,1,0:T(8,128)S(1)} %copy-done.2, f32[256,128]{1,0:T(8,128)S(1)} %collective-permute-done.11.mirrored, f32[256,128]{1,0:T(8,128)S(1)} %get-tuple-element.48.own, f32[32,16,8,32]{3,2,1,0:T(8,128)} %unpack.2.refs_0_), custom_call_target="tpu_custom_call", output_to_operand_aliasing={{}: (4, {})} | custom-call | tf_op jit(solution)/shard_map/unpack/pallas_call | solution.py:21
Async XLA Ops:
  0.0 7.6 %copy-start.2 = (s32[16,8,32]{2,1,0:T(8,128)S(1)}, s32[16,8,32]{2,1,0:T(8,128)}, u32[]{:S(2)}) copy-start(s32[16,8,32]{2,1,0:T(8,128)} %mask.4) | copy-start | bytes 49156
  0.0 2.9 %copy-start.1 = (f32[27,2,16,64]{3,2,1,0:T(8,128)S(1)}, f32[27,2,16,64]{3,2,1,0:T(8,128)}, u32[]{:S(2)}) copy-start(f32[27,2,16,64]{3,2,1,0:T(8,128)} %param.5) | copy-start | bytes 663556
  3.0 6.8 %collective-permute-start = (f32[27,8,128]{2,1,0:T(8,128)S(1)}, f32[27,8,128]{2,1,0:T(8,128)S(1)}, u32[]{:S(2)}, u32[]{:S(2)}) collective-permute-start(f32[27,8,128]{2,1,0:T(8,128)S(1)} %fold.1), channel_id=1, source_target_pairs={{0,2},{1,3},{2,0},{3,1},{4,6},{5,7},{6,4},{7,5},{8,10},{9,11},{10,... | collective-permute-start | bytes 331784 | tf_op jit(solution)/shard_map/ppermute | solution.py:563
  4.3 16.6 %collective-permute-start.3 = (f32[384,128]{1,0:T(8,128)}, f32[384,128]{1,0:T(8,128)S(1)}, u32[]{:S(2)}, u32[]{:S(2)}) collective-permute-start(f32[384,128]{1,0:T(8,128)} %get-tuple-element.36), channel_id=1, source_target_pairs={{0,15},{1,14},{2,13},{3,12},{4,11},{5,10},{6,9},{7,8},{8,7},{9,6},... | collective-permute-start | bytes 589832 | tf_op jit(solution)/shard_map/ppermute | solution.py:563
  6.4 8.3 %collective-permute-start.2 = (f32[368,128]{1,0:T(8,128)}, f32[368,128]{1,0:T(8,128)S(1)}, u32[]{:S(2)}, u32[]{:S(2)}) collective-permute-start(f32[368,128]{1,0:T(8,128)} %get-tuple-element.34), channel_id=1, source_target_pairs={{0,2},{1,3},{2,0},{3,1},{4,6},{5,7},{6,4},{7,5},{8,10},{9,11},{10,... | collective-permute-start | bytes 565256 | tf_op jit(solution)/shard_map/ppermute | solution.py:563
  9.7 14.7 %collective-permute-start.5 = (f32[368,128]{1,0:T(8,128)S(1)}, f32[368,128]{1,0:T(8,128)S(1)}, u32[]{:S(2)}, u32[]{:S(2)}) collective-permute-start(f32[368,128]{1,0:T(8,128)S(1)} %get-tuple-element.38), channel_id=1, source_target_pairs={{0,13},{1,12},{2,15},{3,14},{4,9},{5,8},{6,11},{7,10},{8,5},{9,4},... | collective-permute-start | bytes 565256 | tf_op jit(solution)/shard_map/ppermute | solution.py:563
  9.8 1.5 %collective-permute-start.1 = (f32[27,8,128]{2,1,0:T(8,128)S(1)}, f32[27,8,128]{2,1,0:T(8,128)S(1)}, u32[]{:S(2)}, u32[]{:S(2)}) collective-permute-start(f32[27,8,128]{2,1,0:T(8,128)S(1)} %collective-permute-done.refs_0_), channel_id=1, source_target_pairs={{0,1},{1,0},{2,3},{3,2},{4,5},{5,4},{6,7},{7,6},{8,9},{9,8},{10,11... | collective-permute-start | bytes 331784 | tf_op jit(solution)/shard_map/ppermute | solution.py:563
  21.5 2.9 %collective-permute-start.4 = (f32[144,128]{1,0:T(8,128)S(1)}, f32[144,128]{1,0:T(8,128)S(1)}, u32[]{:S(2)}, u32[]{:S(2)}) collective-permute-start(f32[144,128]{1,0:T(8,128)S(1)} %get-tuple-element.37), channel_id=1, source_target_pairs={{0,1},{1,0},{2,3},{3,2},{4,5},{5,4},{6,7},{7,6},{8,9},{9,8},{10,11... | collective-permute-start | bytes 221192 | tf_op jit(solution)/shard_map/ppermute | solution.py:563
  24.9 1.5 %collective-permute-start.6 = (f32[2,144,128]{2,1,0:T(8,128)S(1)}, f32[2,144,128]{2,1,0:T(8,128)S(1)}, u32[]{:S(2)}, u32[]{:S(2)}) collective-permute-start(f32[2,144,128]{2,1,0:T(8,128)S(1)} %get-tuple-element.41), channel_id=1, source_target_pairs={{0,1},{1,0},{2,3},{3,2},{4,5},{5,4},{6,7},{7,6},{8,9},{9,8},{10,11... | collective-permute-start | bytes 442376 | tf_op jit(solution)/shard_map/ppermute | solution.py:563
  26.4 5.0 %collective-permute-start.7 = (f32[216,128]{1,0:T(8,128)S(1)}, f32[216,128]{1,0:T(8,128)S(1)}, u32[]{:S(2)}, u32[]{:S(2)}) collective-permute-start(f32[216,128]{1,0:T(8,128)S(1)} %get-tuple-element.42), channel_id=1, source_target_pairs={{0,4},{1,5},{2,6},{3,7},{4,0},{5,1},{6,2},{7,3},{8,12},{9,13},{10,... | collective-permute-start | bytes 331784 | tf_op jit(solution)/shard_map/ppermute | solution.py:563
  26.6 4.9 %collective-permute-start.8 = (f32[216,128]{1,0:T(8,128)S(1)}, f32[216,128]{1,0:T(8,128)S(1)}, u32[]{:S(2)}, u32[]{:S(2)}) collective-permute-start(f32[216,128]{1,0:T(8,128)S(1)} %get-tuple-element.43), channel_id=1, source_target_pairs={{0,1},{1,0},{2,3},{3,2},{4,8},{5,9},{6,10},{7,11},{8,4},{9,5},{10,... | collective-permute-start | bytes 331784 | tf_op jit(solution)/shard_map/ppermute | solution.py:563
  32.5 4.8 %collective-permute-start.9 = (f32[180,128]{1,0:T(8,128)S(1)}, f32[180,128]{1,0:T(8,128)S(1)}, u32[]{:S(2)}, u32[]{:S(2)}) collective-permute-start(f32[180,128]{1,0:T(8,128)S(1)} %get-tuple-element.45), channel_id=1, source_target_pairs={{0,1},{1,0},{2,3},{3,2},{4,8},{5,9},{6,10},{7,11},{8,4},{9,5},{10,... | collective-permute-start | bytes 276488 | tf_op jit(solution)/shard_map/ppermute | solution.py:563
  33.1 4.1 %collective-permute-start.10 = (f32[180,128]{1,0:T(8,128)S(1)}, f32[180,128]{1,0:T(8,128)S(1)}, u32[]{:S(2)}, u32[]{:S(2)}) collective-permute-start(f32[180,128]{1,0:T(8,128)S(1)} %get-tuple-element.46), channel_id=1, source_target_pairs={{0,4},{1,5},{2,6},{3,7},{4,0},{5,1},{6,2},{7,3},{8,12},{9,13},{10,... | collective-permute-start | bytes 276488 | tf_op jit(solution)/shard_map/ppermute | solution.py:563
  37.3 13.4 %copy-start = (f32[2,16,16,8,32]{4,3,2,1,0:T(8,128)S(1)}, f32[2,16,16,8,32]{4,3,2,1,0:T(8,128)}, u32[]{:S(2)}) copy-start(f32[2,16,16,8,32]{4,3,2,1,0:T(8,128)} %param.3) | copy-start | bytes 1572868
  38.3 12.3 %collective-permute-start.12 = (f32[256,128]{1,0:T(8,128)S(1)}, f32[256,128]{1,0:T(8,128)S(1)}, u32[]{:S(2)}, u32[]{:S(2)}) collective-permute-start(f32[256,128]{1,0:T(8,128)S(1)} %get-tuple-element.49), channel_id=1, source_target_pairs={{0,15},{1,14},{2,13},{3,12},{4,11},{5,10},{6,9},{7,8},{8,7},{9,6},... | collective-permute-start | bytes 393224 | tf_op jit(solution)/shard_map/ppermute | solution.py:563
  41.4 9.2 %collective-permute-start.13 = (f32[256,128]{1,0:T(8,128)S(1)}, f32[256,128]{1,0:T(8,128)S(1)}, u32[]{:S(2)}, u32[]{:S(2)}) collective-permute-start(f32[256,128]{1,0:T(8,128)S(1)} %get-tuple-element.50), channel_id=1, source_target_pairs={{0,2},{1,3},{2,0},{3,1},{4,6},{5,7},{6,4},{7,5},{8,10},{9,11},{10,... | collective-permute-start | bytes 393224 | tf_op jit(solution)/shard_map/ppermute | solution.py:563
  41.7 11.2 %collective-permute-start.11 = (f32[256,128]{1,0:T(8,128)S(1)}, f32[256,128]{1,0:T(8,128)S(1)}, u32[]{:S(2)}, u32[]{:S(2)}) collective-permute-start(f32[256,128]{1,0:T(8,128)S(1)} %get-tuple-element.47), channel_id=1, source_target_pairs={{0,13},{1,12},{2,15},{3,14},{4,9},{5,8},{6,11},{7,10},{8,5},{9,4},... | collective-permute-start | bytes 393224 | tf_op jit(solution)/shard_map/ppermute | solution.py:563
